TPU v7x, 32 devices: a whole 2x2x4 slice. The times are simulated.
32 devices in a mesh: ctx: 16 (over z, y, core), head: 2 (over x).
Axes of the slice: x: 2, y: 2, z: 4, core: 2. Of those that a mesh axis runs over, the one named last changes fastest.
Arguments:
- queries: bfloat16 [24, 4096, 128], P('head', 'ctx'), may hold values from -40 to 40
- keys: bfloat16 [24, 4096, 128], P('head', 'ctx'), may hold values from -12 to 12
- values: bfloat16 [24, 4096, 128], P('head', 'ctx'), may hold values from -8 to 8
- block_lists: int32 [64, 16], P('ctx'), may hold values from 0 to 63, all different within a row
- coarse_gate: bfloat16 [24, 4096], P('head', 'ctx'), may hold values from 0.5 to 4
Outputs:
- attended: bfloat16 [24, 4096, 128], P('head', 'ctx')
Inputs may be any that keep to these rules, and one draw needn't show every extreme that they name: `block_lists`: each row names 16 different key cubes, and every cube is named by some row.
All inputs are finite; a program needn't handle non-finite values.
Results may differ from a plain program's by a relative error of at most 0.0045.
The roundings to bfloat16 on the way count: a program that leaves them out, or rounds other values in their place, can miss the bound.
Values may be sent and summed in bfloat16 or wider, within the bound.
No kernel may reach another device: no remote copies, remote signals or barrier semaphores. Data moves between devices by JAX's collectives and lax.ppermute only.
A program may use at most 128 MiB of HBM per device.

v0:
```python
import math

import jax
import jax.numpy as jnp
from jax import lax
from jax.sharding import PartitionSpec as P

CUBE = 64


NEG = -1e30


def pool_cubes(field):
    heads, tokens, width = field.shape
    summed = jnp.sum(field.reshape(heads, tokens // CUBE, CUBE, width), axis=2, dtype=jnp.float32)
    return (summed / CUBE).astype(jnp.bfloat16)


def soft_update(carry, scores, allowed, value_block):
    running_max, running_sum, running_acc = carry
    masked = jnp.where(allowed, scores, NEG)
    new_max = jnp.maximum(running_max, jnp.max(masked, axis=-1))
    rescale = jnp.exp(running_max - new_max)
    weights = jnp.where(allowed, jnp.exp(masked - new_max[..., None]), 0.0).astype(jnp.bfloat16)
    new_sum = running_sum * rescale + jnp.sum(weights.astype(jnp.float32), axis=-1)
    product = jnp.einsum("hqk,hkd->hqd", weights, value_block, preferred_element_type=jnp.float32)
    new_acc = running_acc * rescale[..., None] + product
    return (new_max, new_sum, new_acc)


def empty_state(heads, rows, width):
    return (
        jnp.full((heads, rows), NEG, jnp.float32),
        jnp.zeros((heads, rows), jnp.float32),
        jnp.zeros((heads, rows, width), jnp.float32),
    )


def body(queries, keys, values, block_lists, coarse_gate):
    heads, tok_rows, width = queries.shape
    cubes_here = tok_rows // CUBE
    scale = 1.0 / math.sqrt(width)
    pooled_q = pool_cubes(queries)
    pooled_k = pool_cubes(keys)
    pooled_v = pool_cubes(values)
    coarse_cube = None
    scores = (
        jnp.einsum(
            "hqd,hkd->hqk",
            pooled_q,
            lax.all_gather(pooled_k, "ctx", axis=1, tiled=True),
            preferred_element_type=jnp.float32,
        )
        * scale
    )
    coarse_state = soft_update(
        empty_state(heads, cubes_here, width),
        scores,
        True,
        lax.all_gather(pooled_v, "ctx", axis=1, tiled=True),
    )
    coarse_cube = coarse_state[2] / coarse_state[1][..., None]
    fine_state = empty_state(heads, tok_rows, width)
    coarse_state = empty_state(heads, cubes_here, width)
    tile_k = lax.all_gather(keys, "ctx", axis=1, tiled=True)
    tile_v = lax.all_gather(values, "ctx", axis=1, tiled=True)
    count = tile_k.shape[1]
    key_cube = jnp.arange(count, dtype=jnp.int32) // CUBE
    hit = jnp.any(block_lists[:, :, None] == key_cube[None, None, :], axis=1)
    token_mask = jnp.repeat(hit, CUBE, axis=0)
    block = 512

    def one_block(index, state):
        first = index * block
        key_block = lax.dynamic_slice_in_dim(tile_k, first, block, 1)
        value_block = lax.dynamic_slice_in_dim(tile_v, first, block, 1)
        mask_block = lax.dynamic_slice_in_dim(token_mask, first, block, 1)
        scores = (
            jnp.einsum("hqd,hkd->hqk", queries, key_block, preferred_element_type=jnp.float32)
            * scale
        )
        return soft_update(state, scores, mask_block[None], value_block)

    fine_state = lax.fori_loop(0, count // block, one_block, fine_state)
    fine_state, coarse_state = (fine_state, coarse_state)
    fine_out = fine_state[2] / fine_state[1][..., None]
    coarse_tokens = jnp.repeat(coarse_cube, CUBE, axis=1)
    return (fine_out + coarse_gate.astype(jnp.float32)[..., None] * coarse_tokens).astype(
        jnp.bfloat16
    )


def solution(mesh):
    in_specs = (
        P("head", "ctx", None),
        P("head", "ctx", None),
        P("head", "ctx", None),
        P("ctx", None),
        P("head", "ctx"),
    )
    out_specs = P("head", "ctx", None)
    return jax.shard_map(body, mesh=mesh, in_specs=in_specs, out_specs=out_specs, check_vma=False)
```

profile of v0, /device:TPU:0, one launch (start us, length us, event | category | flops | bytes accessed | tf_op | source)
XLA Modules:
  0.0 348.2 jit_solution(11049110698822374032)
XLA Ops:
  8.0 1.3 convert_reduce_fusion.1
  9.4 1.3 convert_reduce_fusion.2
  11.4 24.8 %all_gather.15 = bf16[12,64,128]{2,0,1:T(8,128)(2,1)S(1)} all-gather(bf16[12,4,128]{2,0,1:T(8,128)(2,1)S(1)} %copy.24), channel_id=1, replica_groups=mesh['ctx'=16,'head'=2] {'ctx'}, dimensions={1}, use_global_device_ids=true | all-gather | bytes 208896 | tf_op jit(solution)/shard_map/all_gather | solution.py:61
  36.3 19.2 %all_gather.14 = bf16[12,64,128]{2,0,1:T(8,128)(2,1)S(1)} all-gather(bf16[12,4,128]{2,0,1:T(8,128)(2,1)S(1)} %copy.22), channel_id=1, replica_groups=mesh['ctx'=16,'head'=2] {'ctx'}, dimensions={1}, use_global_device_ids=true | all-gather | bytes 208896 | tf_op jit(solution)/shard_map/all_gather | solution.py:52
  58.5 56.7 %all-gather.3.cloned.1.call-done = bf16[12,4096,128]{2,1,0:T(8,128)(2,1)} async-done(((bf16[12,256,128]{2,1,0:T(8,128)(2,1)}), bf16[12,4096,128]{2,1,0:T(8,128)(2,1)}) %all-gather.3.cloned.1.call-update) | async-done | bytes 12582928 | tf_op jit(solution)/shard_map/all_gather | solution.py:66
  115.2 101.2 %all-gather.5.cloned.1.call-done = bf16[12,4096,128]{2,1,0:T(8,128)(2,1)} async-done(((bf16[12,256,128]{2,1,0:T(8,128)(2,1)}), bf16[12,4096,128]{2,1,0:T(8,128)(2,1)}) %all-gather.5.cloned.1.call-update) | async-done | bytes 12582928 | tf_op jit(solution)/shard_map/all_gather | solution.py:67
  216.8 121.7 %while.18 = (s32[]{:T(128)}, f32[12,256]{1,0:T(8,128)S(1)}, f32[12,256]{1,0:T(8,128)S(1)}, f32[12,256,128]{2,1,0:T(8,128)}, pred[256,4096]{1,0:T(8,128)(4,1)S(1)...) while((s32[]{:T(128)}, f32[12,256]{1,0:T(8,128)S(1)}, ...), condition=%wide.region_4.5_spmd.clone, body=%wide.region_1.4_spmd.clone.sunk | while | flops 830094336 | bytes 52232412 | solution.py:85
  217.1 5.2 %fusion.31 = (f32[12,256]{1,0:T(8,128)S(1)}, f32[12,512,256]{2,1,0:T(8,128)}) fusion(pred[256,512]{0,1:T(8,128)(4,1)S(1)} %copy.35, bf16[12,256,128]{2,1,0:T(8,128)(2,1)S(1)} %get-tuple-element.317, bf16[12,4096,128]{2,1,0:T(8,128)(2,1)} %get-tuple-element.316, s32[]{:T(128)S(6)} %select_n.67), kind=kOutput, calls=%fused_computation.3.clone.1 | convolution fusion | flops 407368704 | bytes 8794116 | tf_op jit(solution)/shard_map/while/body/eval_jaxpr/hqd,hkd->hqk/dot_general | solution.py:80
  222.3 4.4 %convert_reduce_fusion.6 = f32[12,256]{1,0:T(8,128)S(1)} fusion(f32[12,256]{1,0:T(8,128)S(1)} %select_maximum_fusion.2, f32[12,512,256]{2,1,0:T(8,128)} %get-tuple-element.284, pred[256,512]{0,1:T(8,128)(4,1)S(1)} %copy.35), kind=kLoop, calls=%fused_computation.1.clone.1 | loop fusion | flops 11006976 | bytes 6447104 | tf_op jit(solution)/shard_map/while/body/eval_jaxpr/reduce_sum | solution.py:26
  226.9 4.9 %fusion.33 = f32[12,256,128]{2,1,0:T(8,128)} fusion(f32[12,256,128]{2,1,0:T(8,128)} %get-tuple-element.302, bf16[12,4096,128]{2,1,0:T(8,128)(2,1)} %get-tuple-element.318, s32[]{:T(128)S(6)} %select_n.67, f32[12,256]{1,0:T(8,128)S(1)} %get-tuple-element.286, pred[]{:T(512)S(6)} %compare.7, f32[12,512,256]{2,1,0:T(8,128)S(1)} %copy-done, ...), kind=kOutput, calls=%fused_computation.5.clone.1 | convolution fusion | flops 411697152 | bytes 11165701 | tf_op jit(solution)/shard_map/while/body/eval_jaxpr/hqk,hkd->hqd/dot_general | solution.py:27
  232.1 5.2 %fusion.31 = (f32[12,256]{1,0:T(8,128)S(1)}, f32[12,512,256]{2,1,0:T(8,128)}) fusion(pred[256,512]{0,1:T(8,128)(4,1)S(1)} %copy.35, bf16[12,256,128]{2,1,0:T(8,128)(2,1)S(1)} %get-tuple-element.317, bf16[12,4096,128]{2,1,0:T(8,128)(2,1)} %get-tuple-element.316, s32[]{:T(128)S(6)} %select_n.67), kind=kOutput, calls=%fused_computation.3.clone.1 | convolution fusion | flops 407368704 | bytes 8794116 | tf_op jit(solution)/shard_map/while/body/eval_jaxpr/hqd,hkd->hqk/dot_general | solution.py:80
  237.3 4.4 %convert_reduce_fusion.6 = f32[12,256]{1,0:T(8,128)S(1)} fusion(f32[12,256]{1,0:T(8,128)S(1)} %select_maximum_fusion.2, f32[12,512,256]{2,1,0:T(8,128)} %get-tuple-element.284, pred[256,512]{0,1:T(8,128)(4,1)S(1)} %copy.35), kind=kLoop, calls=%fused_computation.1.clone.1 | loop fusion | flops 11006976 | bytes 6447104 | tf_op jit(solution)/shard_map/while/body/eval_jaxpr/reduce_sum | solution.py:26
  241.9 5.2 %fusion.33 = f32[12,256,128]{2,1,0:T(8,128)} fusion(f32[12,256,128]{2,1,0:T(8,128)} %get-tuple-element.302, bf16[12,4096,128]{2,1,0:T(8,128)(2,1)} %get-tuple-element.318, s32[]{:T(128)S(6)} %select_n.67, f32[12,256]{1,0:T(8,128)S(1)} %get-tuple-element.286, pred[]{:T(512)S(6)} %compare.7, f32[12,512,256]{2,1,0:T(8,128)S(1)} %copy-done, ...), kind=kOutput, calls=%fused_computation.5.clone.1 | convolution fusion | flops 411697152 | bytes 11165701 | tf_op jit(solution)/shard_map/while/body/eval_jaxpr/hqk,hkd->hqd/dot_general | solution.py:27
  247.4 5.2 %fusion.31 = (f32[12,256]{1,0:T(8,128)S(1)}, f32[12,512,256]{2,1,0:T(8,128)}) fusion(pred[256,512]{0,1:T(8,128)(4,1)S(1)} %copy.35, bf16[12,256,128]{2,1,0:T(8,128)(2,1)S(1)} %get-tuple-element.317, bf16[12,4096,128]{2,1,0:T(8,128)(2,1)} %get-tuple-element.316, s32[]{:T(128)S(6)} %select_n.67), kind=kOutput, calls=%fused_computation.3.clone.1 | convolution fusion | flops 407368704 | bytes 8794116 | tf_op jit(solution)/shard_map/while/body/eval_jaxpr/hqd,hkd->hqk/dot_general | solution.py:80
  252.6 4.4 %convert_reduce_fusion.6 = f32[12,256]{1,0:T(8,128)S(1)} fusion(f32[12,256]{1,0:T(8,128)S(1)} %select_maximum_fusion.2, f32[12,512,256]{2,1,0:T(8,128)} %get-tuple-element.284, pred[256,512]{0,1:T(8,128)(4,1)S(1)} %copy.35), kind=kLoop, calls=%fused_computation.1.clone.1 | loop fusion | flops 11006976 | bytes 6447104 | tf_op jit(solution)/shard_map/while/body/eval_jaxpr/reduce_sum | solution.py:26
  257.1 5.2 %fusion.33 = f32[12,256,128]{2,1,0:T(8,128)} fusion(f32[12,256,128]{2,1,0:T(8,128)} %get-tuple-element.302, bf16[12,4096,128]{2,1,0:T(8,128)(2,1)} %get-tuple-element.318, s32[]{:T(128)S(6)} %select_n.67, f32[12,256]{1,0:T(8,128)S(1)} %get-tuple-element.286, pred[]{:T(512)S(6)} %compare.7, f32[12,512,256]{2,1,0:T(8,128)S(1)} %copy-done, ...), kind=kOutput, calls=%fused_computation.5.clone.1 | convolution fusion | flops 411697152 | bytes 11165701 | tf_op jit(solution)/shard_map/while/body/eval_jaxpr/hqk,hkd->hqd/dot_general | solution.py:27
  262.6 5.2 %fusion.31 = (f32[12,256]{1,0:T(8,128)S(1)}, f32[12,512,256]{2,1,0:T(8,128)}) fusion(pred[256,512]{0,1:T(8,128)(4,1)S(1)} %copy.35, bf16[12,256,128]{2,1,0:T(8,128)(2,1)S(1)} %get-tuple-element.317, bf16[12,4096,128]{2,1,0:T(8,128)(2,1)} %get-tuple-element.316, s32[]{:T(128)S(6)} %select_n.67), kind=kOutput, calls=%fused_computation.3.clone.1 | convolution fusion | flops 407368704 | bytes 8794116 | tf_op jit(solution)/shard_map/while/body/eval_jaxpr/hqd,hkd->hqk/dot_general | solution.py:80
  267.8 4.4 %convert_reduce_fusion.6 = f32[12,256]{1,0:T(8,128)S(1)} fusion(f32[12,256]{1,0:T(8,128)S(1)} %select_maximum_fusion.2, f32[12,512,256]{2,1,0:T(8,128)} %get-tuple-element.284, pred[256,512]{0,1:T(8,128)(4,1)S(1)} %copy.35), kind=kLoop, calls=%fused_computation.1.clone.1 | loop fusion | flops 11006976 | bytes 6447104 | tf_op jit(solution)/shard_map/while/body/eval_jaxpr/reduce_sum | solution.py:26
  272.4 5.2 %fusion.33 = f32[12,256,128]{2,1,0:T(8,128)} fusion(f32[12,256,128]{2,1,0:T(8,128)} %get-tuple-element.302, bf16[12,4096,128]{2,1,0:T(8,128)(2,1)} %get-tuple-element.318, s32[]{:T(128)S(6)} %select_n.67, f32[12,256]{1,0:T(8,128)S(1)} %get-tuple-element.286, pred[]{:T(512)S(6)} %compare.7, f32[12,512,256]{2,1,0:T(8,128)S(1)} %copy-done, ...), kind=kOutput, calls=%fused_computation.5.clone.1 | convolution fusion | flops 411697152 | bytes 11165701 | tf_op jit(solution)/shard_map/while/body/eval_jaxpr/hqk,hkd->hqd/dot_general | solution.py:27
  277.8 5.2 %fusion.31 = (f32[12,256]{1,0:T(8,128)S(1)}, f32[12,512,256]{2,1,0:T(8,128)}) fusion(pred[256,512]{0,1:T(8,128)(4,1)S(1)} %copy.35, bf16[12,256,128]{2,1,0:T(8,128)(2,1)S(1)} %get-tuple-element.317, bf16[12,4096,128]{2,1,0:T(8,128)(2,1)} %get-tuple-element.316, s32[]{:T(128)S(6)} %select_n.67), kind=kOutput, calls=%fused_computation.3.clone.1 | convolution fusion | flops 407368704 | bytes 8794116 | tf_op jit(solution)/shard_map/while/body/eval_jaxpr/hqd,hkd->hqk/dot_general | solution.py:80
  283.0 4.4 %convert_reduce_fusion.6 = f32[12,256]{1,0:T(8,128)S(1)} fusion(f32[12,256]{1,0:T(8,128)S(1)} %select_maximum_fusion.2, f32[12,512,256]{2,1,0:T(8,128)} %get-tuple-element.284, pred[256,512]{0,1:T(8,128)(4,1)S(1)} %copy.35), kind=kLoop, calls=%fused_computation.1.clone.1 | loop fusion | flops 11006976 | bytes 6447104 | tf_op jit(solution)/shard_map/while/body/eval_jaxpr/reduce_sum | solution.py:26
  287.6 5.2 %fusion.33 = f32[12,256,128]{2,1,0:T(8,128)} fusion(f32[12,256,128]{2,1,0:T(8,128)} %get-tuple-element.302, bf16[12,4096,128]{2,1,0:T(8,128)(2,1)} %get-tuple-element.318, s32[]{:T(128)S(6)} %select_n.67, f32[12,256]{1,0:T(8,128)S(1)} %get-tuple-element.286, pred[]{:T(512)S(6)} %compare.7, f32[12,512,256]{2,1,0:T(8,128)S(1)} %copy-done, ...), kind=kOutput, calls=%fused_computation.5.clone.1 | convolution fusion | flops 411697152 | bytes 11165701 | tf_op jit(solution)/shard_map/while/body/eval_jaxpr/hqk,hkd->hqd/dot_general | solution.py:27
  293.1 5.2 %fusion.31 = (f32[12,256]{1,0:T(8,128)S(1)}, f32[12,512,256]{2,1,0:T(8,128)}) fusion(pred[256,512]{0,1:T(8,128)(4,1)S(1)} %copy.35, bf16[12,256,128]{2,1,0:T(8,128)(2,1)S(1)} %get-tuple-element.317, bf16[12,4096,128]{2,1,0:T(8,128)(2,1)} %get-tuple-element.316, s32[]{:T(128)S(6)} %select_n.67), kind=kOutput, calls=%fused_computation.3.clone.1 | convolution fusion | flops 407368704 | bytes 8794116 | tf_op jit(solution)/shard_map/while/body/eval_jaxpr/hqd,hkd->hqk/dot_general | solution.py:80
  298.3 4.4 %convert_reduce_fusion.6 = f32[12,256]{1,0:T(8,128)S(1)} fusion(f32[12,256]{1,0:T(8,128)S(1)} %select_maximum_fusion.2, f32[12,512,256]{2,1,0:T(8,128)} %get-tuple-element.284, pred[256,512]{0,1:T(8,128)(4,1)S(1)} %copy.35), kind=kLoop, calls=%fused_computation.1.clone.1 | loop fusion | flops 11006976 | bytes 6447104 | tf_op jit(solution)/shard_map/while/body/eval_jaxpr/reduce_sum | solution.py:26
  302.9 5.2 %fusion.33 = f32[12,256,128]{2,1,0:T(8,128)} fusion(f32[12,256,128]{2,1,0:T(8,128)} %get-tuple-element.302, bf16[12,4096,128]{2,1,0:T(8,128)(2,1)} %get-tuple-element.318, s32[]{:T(128)S(6)} %select_n.67, f32[12,256]{1,0:T(8,128)S(1)} %get-tuple-element.286, pred[]{:T(512)S(6)} %compare.7, f32[12,512,256]{2,1,0:T(8,128)S(1)} %copy-done, ...), kind=kOutput, calls=%fused_computation.5.clone.1 | convolution fusion | flops 411697152 | bytes 11165701 | tf_op jit(solution)/shard_map/while/body/eval_jaxpr/hqk,hkd->hqd/dot_general | solution.py:27
  308.3 5.2 %fusion.31 = (f32[12,256]{1,0:T(8,128)S(1)}, f32[12,512,256]{2,1,0:T(8,128)}) fusion(pred[256,512]{0,1:T(8,128)(4,1)S(1)} %copy.35, bf16[12,256,128]{2,1,0:T(8,128)(2,1)S(1)} %get-tuple-element.317, bf16[12,4096,128]{2,1,0:T(8,128)(2,1)} %get-tuple-element.316, s32[]{:T(128)S(6)} %select_n.67), kind=kOutput, calls=%fused_computation.3.clone.1 | convolution fusion | flops 407368704 | bytes 8794116 | tf_op jit(solution)/shard_map/while/body/eval_jaxpr/hqd,hkd->hqk/dot_general | solution.py:80
  313.5 4.4 %convert_reduce_fusion.6 = f32[12,256]{1,0:T(8,128)S(1)} fusion(f32[12,256]{1,0:T(8,128)S(1)} %select_maximum_fusion.2, f32[12,512,256]{2,1,0:T(8,128)} %get-tuple-element.284, pred[256,512]{0,1:T(8,128)(4,1)S(1)} %copy.35), kind=kLoop, calls=%fused_computation.1.clone.1 | loop fusion | flops 11006976 | bytes 6447104 | tf_op jit(solution)/shard_map/while/body/eval_jaxpr/reduce_sum | solution.py:26
  318.1 5.2 %fusion.33 = f32[12,256,128]{2,1,0:T(8,128)} fusion(f32[12,256,128]{2,1,0:T(8,128)} %get-tuple-element.302, bf16[12,4096,128]{2,1,0:T(8,128)(2,1)} %get-tuple-element.318, s32[]{:T(128)S(6)} %select_n.67, f32[12,256]{1,0:T(8,128)S(1)} %get-tuple-element.286, pred[]{:T(512)S(6)} %compare.7, f32[12,512,256]{2,1,0:T(8,128)S(1)} %copy-done, ...), kind=kOutput, calls=%fused_computation.5.clone.1 | convolution fusion | flops 411697152 | bytes 11165701 | tf_op jit(solution)/shard_map/while/body/eval_jaxpr/hqk,hkd->hqd/dot_general | solution.py:27
  323.5 5.2 %fusion.31 = (f32[12,256]{1,0:T(8,128)S(1)}, f32[12,512,256]{2,1,0:T(8,128)}) fusion(pred[256,512]{0,1:T(8,128)(4,1)S(1)} %copy.35, bf16[12,256,128]{2,1,0:T(8,128)(2,1)S(1)} %get-tuple-element.317, bf16[12,4096,128]{2,1,0:T(8,128)(2,1)} %get-tuple-element.316, s32[]{:T(128)S(6)} %select_n.67), kind=kOutput, calls=%fused_computation.3.clone.1 | convolution fusion | flops 407368704 | bytes 8794116 | tf_op jit(solution)/shard_map/while/body/eval_jaxpr/hqd,hkd->hqk/dot_general | solution.py:80
  328.8 4.4 %convert_reduce_fusion.6 = f32[12,256]{1,0:T(8,128)S(1)} fusion(f32[12,256]{1,0:T(8,128)S(1)} %select_maximum_fusion.2, f32[12,512,256]{2,1,0:T(8,128)} %get-tuple-element.284, pred[256,512]{0,1:T(8,128)(4,1)S(1)} %copy.35), kind=kLoop, calls=%fused_computation.1.clone.1 | loop fusion | flops 11006976 | bytes 6447104 | tf_op jit(solution)/shard_map/while/body/eval_jaxpr/reduce_sum | solution.py:26
  333.3 5.2 %fusion.33 = f32[12,256,128]{2,1,0:T(8,128)} fusion(f32[12,256,128]{2,1,0:T(8,128)} %get-tuple-element.302, bf16[12,4096,128]{2,1,0:T(8,128)(2,1)} %get-tuple-element.318, s32[]{:T(128)S(6)} %select_n.67, f32[12,256]{1,0:T(8,128)S(1)} %get-tuple-element.286, pred[]{:T(512)S(6)} %compare.7, f32[12,512,256]{2,1,0:T(8,128)S(1)} %copy-done, ...), kind=kOutput, calls=%fused_computation.5.clone.1 | convolution fusion | flops 411697152 | bytes 11165701 | tf_op jit(solution)/shard_map/while/body/eval_jaxpr/hqk,hkd->hqd/dot_general | solution.py:27
  338.5 2.9 fusion.12
  (79 shorter events, 9.1 us)
Async XLA Ops:
  6.5 210.3 %copy-start.1 = (bf16[12,256,128]{2,1,0:T(8,128)(2,1)S(1)}, bf16[12,256,128]{2,1,0:T(8,128)(2,1)}, u32[]{:S(2)}) copy-start(bf16[12,256,128]{2,1,0:T(8,128)(2,1)} %param.7) | copy-start | bytes 2359300
  6.5 108.7 %all-gather.3.cloned.1.call-start = ((), (), s32[]{:S(2)}) async-start(), calls=%async_computation | async-start | bytes 13369344 | tf_op jit(solution)/shard_map/all_gather | solution.py:66
  7.3 209.1 %all-gather.5.cloned.1.call-start = ((), (), s32[]{:S(2)}) async-start(), calls=%async_computation.1 | async-start | bytes 13369344 | tf_op jit(solution)/shard_map/all_gather | solution.py:67
  222.3 4.6 %copy-start = (f32[12,512,256]{2,1,0:T(8,128)S(1)}, f32[12,512,256]{2,1,0:T(8,128)}, u32[]{:S(2)}) copy-start(f32[12,512,256]{2,1,0:T(8,128)} %get-tuple-element.284) | copy-start | bytes 18874372 | tf_op jit(solution)/shard_map/while
  237.3 4.6 %copy-start = (f32[12,512,256]{2,1,0:T(8,128)S(1)}, f32[12,512,256]{2,1,0:T(8,128)}, u32[]{:S(2)}) copy-start(f32[12,512,256]{2,1,0:T(8,128)} %get-tuple-element.284) | copy-start | bytes 18874372 | tf_op jit(solution)/shard_map/while
  252.5 4.6 %copy-start = (f32[12,512,256]{2,1,0:T(8,128)S(1)}, f32[12,512,256]{2,1,0:T(8,128)}, u32[]{:S(2)}) copy-start(f32[12,512,256]{2,1,0:T(8,128)} %get-tuple-element.284) | copy-start | bytes 18874372 | tf_op jit(solution)/shard_map/while
  267.8 4.6 %copy-start = (f32[12,512,256]{2,1,0:T(8,128)S(1)}, f32[12,512,256]{2,1,0:T(8,128)}, u32[]{:S(2)}) copy-start(f32[12,512,256]{2,1,0:T(8,128)} %get-tuple-element.284) | copy-start | bytes 18874372 | tf_op jit(solution)/shard_map/while
  283.0 4.6 %copy-start = (f32[12,512,256]{2,1,0:T(8,128)S(1)}, f32[12,512,256]{2,1,0:T(8,128)}, u32[]{:S(2)}) copy-start(f32[12,512,256]{2,1,0:T(8,128)} %get-tuple-element.284) | copy-start | bytes 18874372 | tf_op jit(solution)/shard_map/while
  298.3 4.6 %copy-start = (f32[12,512,256]{2,1,0:T(8,128)S(1)}, f32[12,512,256]{2,1,0:T(8,128)}, u32[]{:S(2)}) copy-start(f32[12,512,256]{2,1,0:T(8,128)} %get-tuple-element.284) | copy-start | bytes 18874372 | tf_op jit(solution)/shard_map/while
  313.5 4.6 %copy-start = (f32[12,512,256]{2,1,0:T(8,128)S(1)}, f32[12,512,256]{2,1,0:T(8,128)}, u32[]{:S(2)}) copy-start(f32[12,512,256]{2,1,0:T(8,128)} %get-tuple-element.284) | copy-start | bytes 18874372 | tf_op jit(solution)/shard_map/while
  328.7 4.6 %copy-start = (f32[12,512,256]{2,1,0:T(8,128)S(1)}, f32[12,512,256]{2,1,0:T(8,128)}, u32[]{:S(2)}) copy-start(f32[12,512,256]{2,1,0:T(8,128)} %get-tuple-element.284) | copy-start | bytes 18874372 | tf_op jit(solution)/shard_map/while
Sparse Core Ops, SparseCore 0:
  9.6 105.6 all-gather.2
  117.4 98.9 all-gather.4
where the time goes:
time: 349 us; the launch traced here: 348 us
  waiting for transfers between devices  159 us (46%)
  matrix products  83.1 us (24%)
  other arithmetic  44.3 us (13%)
  blocking collectives  44.1 us (13%)
  between operations  13.5 us (4%)
  local copies, waits for them, and re-layouts  3.75 us (1%)
    all_gather x1, waiting for transfers between devices, body(): tile_v = lax.all_gather(values, 'ctx', axis=1, tiled=True)  101 us
    all_gather x1, waiting for transfers between devices, body(): tile_k = lax.all_gather(keys, 'ctx', axis=1, tiled=True)  56.7 us
    dot_general x8, matrix products, one_block(): jnp.einsum('hqd,hkd->hqk', queries, key_block, preferred_element_type=jnp...  41.5 us
    dot_general x9, matrix products, soft_update(): jnp.einsum('hqk,hkd->hqd', weights, value_block, preferred_element_type=j...  41.2 us
    reduce_sum x9, other arithmetic, soft_update(): jnp.sum(weights.astype(jnp.float32), axis=-1)  35.6 us
    all_gather x1, blocking collectives, body(): lax.all_gather(pooled_v, 'ctx', axis=1, tiled=True)  24.8 us
    all_gather x1, blocking collectives, body(): lax.all_gather(pooled_k, 'ctx', axis=1, tiled=True)  19.2 us
  transfers between devices with their start and end apart: 2, of which 2 were waited for; matrix products, arithmetic and copies ran while one was open for 2% of the time, Pallas kernels for 0%

commit v1 on v0

v1 whole, which is shorter than its diff:
```python
import functools
import math

import jax
import jax.numpy as jnp
from jax import lax
from jax.experimental import pallas as pl
from jax.experimental.pallas import tpu as pltpu
from jax.sharding import PartitionSpec as P

CUBE = 64
NEG = -1e30
LEVELS = 32766.0


def pool_cubes(field):
    heads, tokens, width = field.shape
    summed = jnp.sum(field.reshape(heads, tokens // CUBE, CUBE, width), axis=2, dtype=jnp.float32)
    return (summed / CUBE).astype(jnp.bfloat16)


def attend_kernel(blocks, factor, bias_ref, own_q_ref, far_q_ref, *refs):
    kv_refs = refs[:blocks]
    own_acc_ref, far_code_ref, own_stat_ref, far_stat_ref = refs[blocks : blocks + 4]
    score_ref = refs[blocks + 4]
    rows, width = own_q_ref.shape[1:]
    span = kv_refs[0].shape[2]
    cubes = rows // CUBE
    values = jnp.concatenate([ref[1, 0] for ref in kv_refs], axis=0)
    values = jnp.concatenate([values, jnp.ones_like(values)], axis=1)
    for half, q_ref in enumerate((own_q_ref, far_q_ref)):
        query = q_ref[0]
        top = jnp.full((rows, span), NEG, jnp.float32)
        for b in range(blocks):
            scores = lax.dot_general(
                query,
                kv_refs[b][0, 0],
                (((1,), (1,)), ((), ())),
                preferred_element_type=jnp.float32,
            )
            bias = bias_ref[half * cubes : (half + 1) * cubes, b * span : (b + 1) * span]
            scores = (scores.reshape(cubes, CUBE, span) + bias[:, None, :]).reshape(rows, span)
            top = jnp.maximum(top, scores)
            score_ref[:, b * span : (b + 1) * span] = scores
        top = jnp.max(top, axis=1, keepdims=True)
        weights = jnp.exp2((score_ref[...] - top) * factor).astype(jnp.bfloat16)
        both = jnp.dot(weights, values, preferred_element_type=jnp.float32)
        acc, total = both[:, :width], both[:, width:]
        lane = lax.broadcasted_iota(jnp.int32, (rows, width), 1)
        stats = jnp.where(lane == 0, top, total)
        if half == 0:
            own_acc_ref[0] = acc
            own_stat_ref[0] = jnp.transpose(stats)[:8]
        else:
            peak = jnp.max(jnp.abs(acc), axis=1, keepdims=True)
            step = jnp.maximum(peak, 1e-30) / LEVELS
            stats = jnp.where(lane == 2, step, stats)
            far_stat_ref[0] = jnp.transpose(stats)[:8]
            code = jnp.floor(acc / step + 0.5).astype(jnp.int32)
            far_code_ref[0] = code.astype(jnp.int16)


def attend(first, bias, queries, far_q, kvs):
    heads, rows, width = far_q.shape
    blocks = len(kvs)
    span = kvs[0].shape[2]
    factor = math.log2(math.e) / math.sqrt(width)
    head_block = pl.BlockSpec((1, rows, width), lambda h: (h, 0, 0))
    stat_block = pl.BlockSpec((1, 8, rows), lambda h: (h, 0, 0))
    work = heads * 2 * rows * blocks * span
    return pl.pallas_call(
        functools.partial(attend_kernel, blocks, factor),
        grid=(heads,),
        in_specs=[
            pl.BlockSpec(bias.shape, lambda h: (0, 0)),
            pl.BlockSpec((1, rows, width), lambda h: (first + h, 0, 0)),
            head_block,
        ]
        + [pl.BlockSpec((2, 1, span, width), lambda h: (0, h, 0, 0))] * blocks,
        out_specs=[head_block, head_block, stat_block, stat_block],
        out_shape=[
            jax.ShapeDtypeStruct((heads, rows, width), jnp.float32),
            jax.ShapeDtypeStruct((heads, rows, width), jnp.int16),
            jax.ShapeDtypeStruct((heads, 8, rows), jnp.float32),
            jax.ShapeDtypeStruct((heads, 8, rows), jnp.float32),
        ],
        scratch_shapes=[pltpu.VMEM((rows, blocks * span), jnp.float32)],
        compiler_params=pltpu.CompilerParams(vmem_limit_bytes=48 * 1024 * 1024),
        cost_estimate=pl.CostEstimate(
            flops=work * width * 4, bytes_accessed=heads * rows * width * 2 * (2 * blocks + 5), transcendentals=work
        ),
    )(bias, queries, far_q, *kvs)


def body(ring, queries, keys, values, block_lists, coarse_gate):
    heads, rows, width = queries.shape
    cubes = rows // CUBE
    scale = 1.0 / math.sqrt(width)
    factor = math.log2(math.e) * scale
    half = ring // 2
    me = lax.axis_index("ctx")
    lower = [1 << bit for bit in reversed(range(half.bit_length() - 1))]

    def swap(array, bit):
        return lax.ppermute(array, "ctx", [(i, i ^ bit) for i in range(ring)])

    pooled_q = pool_cubes(queries)
    pooled = jnp.concatenate([pool_cubes(keys), pool_cubes(values)], axis=2)[:, None]
    for bit in [1 << b for b in range(ring.bit_length() - 1)]:
        pooled = jnp.concatenate([pooled, swap(pooled, bit)], axis=1)
    pooled = pooled.reshape(heads, ring * cubes, 2 * width)
    coarse_scores = (
        jnp.einsum(
            "hqd,hkd->hqk", pooled_q, pooled[..., :width], preferred_element_type=jnp.float32
        )
        * scale
    )
    coarse_top = jnp.max(coarse_scores, axis=-1, keepdims=True)
    coarse_weights = jnp.exp(coarse_scores - coarse_top).astype(jnp.bfloat16)
    coarse_total = jnp.sum(coarse_weights.astype(jnp.float32), axis=-1)
    coarse_cube = (
        jnp.einsum(
            "hqk,hkd->hqd", coarse_weights, pooled[..., width:], preferred_element_type=jnp.float32
        )
        / coarse_total[..., None]
    )

    lists = jnp.concatenate([block_lists, swap(block_lists, half)], axis=0)
    masks = [0]
    for bit in lower:
        masks = masks + [m ^ bit for m in masks]
    lanes = jnp.concatenate(
        [(me ^ m) * cubes + jnp.arange(rows, dtype=jnp.int32) // CUBE for m in masks]
    )
    hit = jnp.any(lists[:, :, None] == lanes[None, None, :], axis=1)
    bias = jnp.where(hit, 0.0, NEG).astype(jnp.float32)

    parts = 4 if heads % 4 == 0 else 1
    each = heads // parts
    results = []
    for part in range(parts):
        first = part * each
        chosen = slice(first, first + each)
        far_q = swap(queries[chosen], half)
        kvs = [jnp.stack([keys[chosen], values[chosen]])]
        for bit in lower:
            kvs = kvs + [swap(kv, bit) for kv in kvs]
        own_acc, far_code, own_stat, far_stat = attend(first, bias, queries, far_q, kvs)
        code = swap(far_code, half)
        stat = swap(far_stat, half)
        best = jnp.maximum(own_stat[:, 0], stat[:, 0])
        own_share = jnp.exp2((own_stat[:, 0] - best) * factor)
        far_share = jnp.exp2((stat[:, 0] - best) * factor)
        total = own_share * own_stat[:, 1] + far_share * stat[:, 1]
        own_share = own_share / total
        far_share = far_share * stat[:, 2] / total
        fine = own_acc * own_share[..., None] + code.astype(jnp.float32) * far_share[..., None]
        coarse = jnp.repeat(coarse_cube[chosen], CUBE, axis=1)
        gate = coarse_gate[chosen].astype(jnp.float32)[..., None]
        results.append((fine + gate * coarse).astype(jnp.bfloat16))
    return jnp.concatenate(results, axis=0)


def solution(mesh):
    in_specs = (
        P("head", "ctx", None),
        P("head", "ctx", None),
        P("head", "ctx", None),
        P("ctx", None),
        P("head", "ctx"),
    )
    out_specs = P("head", "ctx", None)
    return jax.shard_map(
        functools.partial(body, mesh.shape["ctx"]),
        mesh=mesh,
        in_specs=in_specs,
        out_specs=out_specs,
        check_vma=False,
    )
```

time: 349 us -> 191 us (0.55)
  matrix products: 83.1 us -> 2.42 us
  waiting for transfers between devices: 159 us -> 91.5 us
  blocking collectives: 44.1 us -> 0 us
  starting transfers between devices: 0.04 us -> 41.6 us
  other arithmetic: 44.3 us -> 11 us
  Pallas kernels: 0 us -> 29.5 us
  between operations: 13.5 us -> 0.6 us
  local copies, waits for them, and re-layouts: 3.75 us -> 13.7 us
    all_gather x2 -> x0, waiting for transfers between devices: 158 us -> none  [the longest x1 101 us: body(): tile_v = lax.all_gather(values, 'ctx', axis=1, tiled=True)]
    ppermute x0 -> x45, waiting for transfers between devices: none -> 91.5 us  [swap(): return lax.ppermute(array, 'ctx', [(i, i ^ bit) for i in range(ring)])]
    dot_general x18 -> x1, matrix products: 83.1 us -> 1.14 us  [body(): jnp.einsum('hqk,hkd->hqd', coarse_weights, pooled[..., width:], preferred...]
    all_gather x2 -> x0, blocking collectives: 44.1 us -> none  [the longest x1 24.8 us: body(): lax.all_gather(pooled_v, 'ctx', axis=1, tiled=True)]
    ppermute x0 -> x45, starting transfers between devices: none -> 41.6 us  [swap(): return lax.ppermute(array, 'ctx', [(i, i ^ bit) for i in range(ring)])]
    reduce_sum x9 -> x0, other arithmetic: 35.6 us -> none  [soft_update(): jnp.sum(weights.astype(jnp.float32), axis=-1)]
    pallas_call x0 -> x4, Pallas kernels: none -> 29.5 us  [attend(): pl.pallas_call(functools.partial(attend_kernel, blocks, factor), grid=(he...]
    unnamed x2 -> x71, local copies, waits for them, and re-layouts: 0.01 us -> 8.2 us
  transfers between devices with their start and end apart: 2 -> 45, of which waited for: 2 -> 16; matrix products, arithmetic and copies ran while one was open for 2% -> 10% of each run, Pallas kernels for 0% -> 16%
where the time goes in v1:
time: 191 us; the launch traced here: 190 us
  waiting for transfers between devices  91.5 us (48%)
  starting transfers between devices  41.6 us (22%)
  Pallas kernels  29.5 us (15%)
  local copies, waits for them, and re-layouts  13.7 us (7%)
  other arithmetic  11 us (6%)
  matrix products  2.42 us (1%)
    ppermute x45, waiting for transfers between devices, swap(): return lax.ppermute(array, 'ctx', [(i, i ^ bit) for i in range(ring)])  91.5 us
    ppermute x45, starting transfers between devices, swap(): return lax.ppermute(array, 'ctx', [(i, i ^ bit) for i in range(ring)])  41.6 us
    pallas_call x4, Pallas kernels, attend(): pl.pallas_call(functools.partial(attend_kernel, blocks, factor), grid=(he...  29.5 us
    unnamed x71, local copies, waits for them, and re-layouts  8.2 us
  transfers between devices with their start and end apart: 45, of which 16 were waited for; matrix products, arithmetic and copies ran while one was open for 10% of the time, Pallas kernels for 16%

profile of v1, /device:TPU:0, one launch (start us, length us, event | category | flops | bytes accessed | tf_op | source)
XLA Modules:
  0.0 190.4 jit_solution(15731528034284676290)
XLA Ops:
  0.0 4.0 %collective-permute-start = (s32[4,16]{1,0:T(4,128)}, s32[4,16]{1,0:T(4,128)S(1)}, u32[]{:S(2)}, u32[]{:S(2)}) collective-permute-start(s32[4,16]{1,0:T(4,128)} %param.8), channel_id=1, source_target_pairs={{0,16},{2,18},{4,20},{6,22},{8,24},{10,26},{12,28},{14,30},{16,0},... | collective-permute-start | bytes 776 | tf_op jit(solution)/shard_map/ppermute | solution.py:105
  4.0 1.6 slice_bitcast_fusion.6
  5.7 1.6 collective-permute-start.2
  10.2 2.0 %collective-permute-start.15 = (bf16[3,256,128]{2,1,0:T(8,128)(2,1)}, bf16[3,256,128]{2,1,0:T(8,128)(2,1)S(1)}, u32[]{:S(2)}, u32[]{:S(2)}) collective-permute-start(bf16[3,256,128]{2,1,0:T(8,128)(2,1)} %get-tuple-element.47), channel_id=1, source_target_pairs={{0,16},{2,18},{4,20},{6,22},{8,24},{10,26},{12,28},{14,30},{16,0},... | collective-permute-start | bytes 589832 | tf_op jit(solution)/shard_map/ppermute | solution.py:105
  13.8 1.6 collective-permute-start.12
  15.4 2.6 %collective-permute-done.12 = bf16[12,2,4,256]{3,2,0,1:T(4,128)(2,1)S(1)} collective-permute-done((bf16[12,2,4,256]{3,2,0,1:T(4,128)(2,1)S(1)}, bf16[12,2,4,256]{3,2,0,1:T(4,128)(2,1)S(1)}, u32[]{:S(2)}, u32[]{:S(2)}) %collective-permute-start.12) | collective-permute-done | bytes 49184 | tf_op jit(solution)/shard_map/ppermute | solution.py:105
  19.9 1.6 collective-permute-start.3
  21.5 4.5 %collective-permute-done.13 = bf16[12,4,4,256]{3,2,0,1:T(4,128)(2,1)S(1)} collective-permute-done((bf16[12,4,4,256]{3,2,0,1:T(4,128)(2,1)S(1)}, bf16[12,4,4,256]{3,2,0,1:T(4,128)(2,1)S(1)}, u32[]{:S(2)}, u32[]{:S(2)}) %collective-permute-start.13) | collective-permute-done | bytes 98336 | tf_op jit(solution)/shard_map/ppermute | solution.py:105
  26.7 2.5 %collective-permute-start.16 = (bf16[2,3,256,128]{3,2,1,0:T(8,128)(2,1)S(1)}, bf16[2,3,256,128]{3,2,1,0:T(8,128)(2,1)S(1)}, u32[]{:S(2)}, u32[]{:S(2)}) collective-permute-start(bf16[2,3,256,128]{3,2,1,0:T(8,128)(2,1)S(1)} %pad_maximum_fusion.2.refs_0_), channel_id=1, source_target_pairs={{0,8},{2,10},{4,12},{6,14},{8,0},{10,2},{12,4},{14,6},{16,24},{18,... | collective-permute-start | bytes 1179656 | tf_op jit(solution)/shard_map/ppermute | solution.py:105
  30.3 11.6 %collective-permute-done.35.far_q_ref = bf16[3,256,128]{2,1,0:T(8,128)(2,1)} collective-permute-done((bf16[3,256,128]{2,1,0:T(8,128)(2,1)}, bf16[3,256,128]{2,1,0:T(8,128)(2,1)}, u32[]{:S(2)}, u32[]{:S(2)}) %collective-permute-start.35) | collective-permute-done | bytes 196640 | tf_op jit(solution)/shard_map/ppermute | solution.py:105
  42.0 3.5 %collective-permute-start.14 = (bf16[12,8,4,256]{3,2,0,1:T(4,128)(2,1)S(1)}, bf16[12,8,4,256]{3,2,0,1:T(4,128)(2,1)S(1)}, u32[]{:S(2)}, u32[]{:S(2)}) collective-permute-start(bf16[12,8,4,256]{3,2,0,1:T(4,128)(2,1)S(1)} %pad_maximum_fusion.5), channel_id=1, source_target_pairs={{0,16},{2,18},{4,20},{6,22},{8,24},{10,26},{12,28},{14,30},{16,0},... | collective-permute-start | bytes 589832 | tf_op jit(solution)/shard_map/ppermute | solution.py:105
  46.2 7.4 %collective-permute-done.14 = bf16[12,8,4,256]{3,2,0,1:T(4,128)(2,1)S(1)} collective-permute-done((bf16[12,8,4,256]{3,2,0,1:T(4,128)(2,1)S(1)}, bf16[12,8,4,256]{3,2,0,1:T(4,128)(2,1)S(1)}, u32[]{:S(2)}, u32[]{:S(2)}) %collective-permute-start.14) | collective-permute-done | bytes 196640 | tf_op jit(solution)/shard_map/ppermute | solution.py:105
  55.8 1.9 %collective-permute-start.36 = (bf16[2,3,256,128]{3,2,1,0:T(8,128)(2,1)S(1)}, bf16[2,3,256,128]{3,2,1,0:T(8,128)(2,1)}, u32[]{:S(2)}, u32[]{:S(2)}) collective-permute-start(bf16[2,3,256,128]{3,2,1,0:T(8,128)(2,1)S(1)} %pad_maximum_fusion.4.refs_0_), channel_id=1, source_target_pairs={{0,8},{2,10},{4,12},{6,14},{8,0},{10,2},{12,4},{14,6},{16,24},{18,... | collective-permute-start | bytes 1179656 | tf_op jit(solution)/shard_map/ppermute | solution.py:105
  60.8 4.9 %collective-permute-done.17.refs_2_ = bf16[2,3,256,128]{3,2,1,0:T(8,128)(2,1)} collective-permute-done((bf16[2,3,256,128]{3,2,1,0:T(8,128)(2,1)S(1)}, bf16[2,3,256,128]{3,2,1,0:T(8,128)(2,1)}, u32[]{:S(2)}, u32[]{:S(2)}) %collective-permute-start.17) | collective-permute-done | bytes 393248 | tf_op jit(solution)/shard_map/ppermute | solution.py:105
  68.5 5.5 %collective-permute-done.27.refs_2_ = bf16[2,3,256,128]{3,2,1,0:T(8,128)(2,1)S(1)} collective-permute-done((bf16[2,3,256,128]{3,2,1,0:T(8,128)(2,1)S(1)}, bf16[2,3,256,128]{3,2,1,0:T(8,128)(2,1)S(1)}, u32[]{:S(2)}, u32[]{:S(2)}) %collective-permute-start.27) | collective-permute-done | bytes 393248 | tf_op jit(solution)/shard_map/ppermute | solution.py:105
  76.1 6.3 %collective-permute-done.37.refs_2_ = bf16[2,3,256,128]{3,2,1,0:T(8,128)(2,1)S(1)} collective-permute-done((bf16[2,3,256,128]{3,2,1,0:T(8,128)(2,1)S(1)}, bf16[2,3,256,128]{3,2,1,0:T(8,128)(2,1)S(1)}, u32[]{:S(2)}, u32[]{:S(2)}) %collective-permute-start.37) | collective-permute-done | bytes 393248 | tf_op jit(solution)/shard_map/ppermute | solution.py:105
  84.7 6.1 %collective-permute-done.4.refs_3_ = bf16[2,3,256,128]{3,2,1,0:T(8,128)(2,1)S(1)} collective-permute-done((bf16[2,3,256,128]{3,2,1,0:T(8,128)(2,1)S(1)}, bf16[2,3,256,128]{3,2,1,0:T(8,128)(2,1)S(1)}, u32[]{:S(2)}, u32[]{:S(2)}) %collective-permute-start.4) | collective-permute-done | bytes 393248 | tf_op jit(solution)/shard_map/ppermute | solution.py:105
  95.6 1.9 reshape.252
  100.0 7.8 %collective-permute-done.28.refs_3_ = bf16[2,3,256,128]{3,2,1,0:T(8,128)(2,1)} collective-permute-done((bf16[2,3,256,128]{3,2,1,0:T(8,128)(2,1)S(1)}, bf16[2,3,256,128]{3,2,1,0:T(8,128)(2,1)}, u32[]{:S(2)}, u32[]{:S(2)}) %collective-permute-start.28) | collective-permute-done | bytes 393248 | tf_op jit(solution)/shard_map/ppermute | solution.py:105
  107.8 7.5 %collective-permute-done.38.refs_3_ = bf16[2,3,256,128]{3,2,1,0:T(8,128)(2,1)} collective-permute-done((bf16[2,3,256,128]{3,2,1,0:T(8,128)(2,1)}, bf16[2,3,256,128]{3,2,1,0:T(8,128)(2,1)}, u32[]{:S(2)}, u32[]{:S(2)}) %collective-permute-start.38) | collective-permute-done | bytes 393248 | tf_op jit(solution)/shard_map/ppermute | solution.py:105
  120.6 7.3 %shard_map.55 = (f32[3,256,128]{2,1,0:T(8,128)S(1)}, s16[3,256,128]{2,1,0:T(8,128)(2,1)S(1)}, f32[3,8,256]{2,1,0:T(8,128)S(1)}, f32[3,8,256]{2,1,0:T(8,128)S(1)}) custom-call(f32[8,2048]{1,0:T(8,128)S(1)} %broadcast_select_fusion.bias_ref, bf16[12,256,128]{2,1,0:T(8,128)(2,1)S(1)} %copy-done, bf16[3,256,128]{2,1,0:T(8,128)(2,1)S(1)} %copy-done.20, ...), custom_call_target="tpu_custom_call" | custom-call | flops 1610612736 | bytes 4128768 | tf_op jit(solution)/shard_map/pallas_call | solution.py:71
  128.1 7.5 %shard_map.56 = (f32[3,256,128]{2,1,0:T(8,128)S(1)}, s16[3,256,128]{2,1,0:T(8,128)(2,1)S(1)}, f32[3,8,256]{2,1,0:T(8,128)S(1)}, f32[3,8,256]{2,1,0:T(8,128)S(1)}) custom-call(f32[8,2048]{1,0:T(8,128)S(1)} %broadcast_select_fusion.bias_ref, bf16[12,256,128]{2,1,0:T(8,128)(2,1)S(1)} %copy-done, bf16[3,256,128]{2,1,0:T(8,128)(2,1)S(1)} %copy-done.18, ...), custom_call_target="tpu_custom_call" | custom-call | flops 1610612736 | bytes 4128768 | tf_op jit(solution)/shard_map/pallas_call | solution.py:71
  135.8 7.4 %shard_map.58 = (f32[3,256,128]{2,1,0:T(8,128)S(1)}, s16[3,256,128]{2,1,0:T(8,128)(2,1)S(1)}, f32[3,8,256]{2,1,0:T(8,128)S(1)}, f32[3,8,256]{2,1,0:T(8,128)S(1)}) custom-call(f32[8,2048]{1,0:T(8,128)S(1)} %broadcast_select_fusion.bias_ref, bf16[12,256,128]{2,1,0:T(8,128)(2,1)S(1)} %copy-done, bf16[3,256,128]{2,1,0:T(8,128)(2,1)} %collective-permute-done.35.far_q_ref, ...), custom_call_target="tpu_custom_call" | custom-call | flops 1610612736 | bytes 4128768 | tf_op jit(solution)/shard_map/pallas_call | solution.py:71
  143.2 2.9 %collective-permute-start.9 = (f32[3,8,256]{2,0,1:T(4,128)S(1)}, f32[3,8,256]{2,0,1:T(4,128)S(1)}, u32[]{:S(2)}, u32[]{:S(2)}) collective-permute-start(f32[3,8,256]{2,0,1:T(4,128)S(1)} %copy.21), channel_id=1, source_target_pairs={{0,16},{2,18},{4,20},{6,22},{8,24},{10,26},{12,28},{14,30},{16,0},... | collective-permute-start | bytes 73736 | tf_op jit(solution)/shard_map/ppermute | solution.py:105
  146.2 2.8 %collective-permute-start.23 = (f32[3,8,256]{2,0,1:T(4,128)S(1)}, f32[3,8,256]{2,0,1:T(4,128)S(1)}, u32[]{:S(2)}, u32[]{:S(2)}) collective-permute-start(f32[3,8,256]{2,0,1:T(4,128)S(1)} %copy.25), channel_id=1, source_target_pairs={{0,16},{2,18},{4,20},{6,22},{8,24},{10,26},{12,28},{14,30},{16,0},... | collective-permute-start | bytes 73736 | tf_op jit(solution)/shard_map/ppermute | solution.py:105
  149.1 2.8 %collective-permute-start.43 = (f32[3,8,256]{2,1,0:T(8,128)S(1)}, f32[3,8,256]{2,1,0:T(8,128)S(1)}, u32[]{:S(2)}, u32[]{:S(2)}) collective-permute-start(f32[3,8,256]{2,1,0:T(8,128)S(1)} %get-tuple-element.35), channel_id=1, source_target_pairs={{0,16},{2,18},{4,20},{6,22},{8,24},{10,26},{12,28},{14,30},{16,0},... | collective-permute-start | bytes 73736 | tf_op jit(solution)/shard_map/ppermute | solution.py:105
  152.0 7.3 %shard_map.57 = (f32[3,256,128]{2,1,0:T(8,128)S(1)}, s16[3,256,128]{2,1,0:T(8,128)(2,1)S(1)}, f32[3,8,256]{2,1,0:T(8,128)S(1)}, f32[3,8,256]{2,1,0:T(8,128)S(1)}) custom-call(f32[8,2048]{1,0:T(8,128)S(1)} %broadcast_select_fusion.bias_ref, bf16[12,256,128]{2,1,0:T(8,128)(2,1)S(1)} %copy-done, bf16[3,256,128]{2,1,0:T(8,128)(2,1)S(1)} %collective-permute-done.25.far_q_ref, ...), custom_call_target="tpu_custom_call" | custom-call | flops 1610612736 | bytes 4128768 | tf_op jit(solution)/shard_map/pallas_call | solution.py:71
  159.3 8.3 %collective-permute-done.43 = f32[3,8,256]{2,1,0:T(8,128)S(1)} collective-permute-done((f32[3,8,256]{2,1,0:T(8,128)S(1)}, f32[3,8,256]{2,1,0:T(8,128)S(1)}, u32[]{:S(2)}, u32[]{:S(2)}) %collective-permute-start.43) | collective-permute-done | bytes 24608 | tf_op jit(solution)/shard_map/ppermute | solution.py:105
  167.6 3.0 %collective-permute-start.34 = (s16[3,256,128]{2,1,0:T(8,128)(2,1)S(1)}, s16[3,256,128]{2,1,0:T(8,128)(2,1)S(1)}, u32[]{:S(2)}, u32[]{:S(2)}) collective-permute-start(s16[3,256,128]{2,1,0:T(8,128)(2,1)S(1)} %get-tuple-element.32), channel_id=1, source_target_pairs={{0,16},{2,18},{4,20},{6,22},{8,24},{10,26},{12,28},{14,30},{16,0},... | collective-permute-start | bytes 589832 | tf_op jit(solution)/shard_map/ppermute | solution.py:105
  170.8 10.2 %collective-permute-done.33 = f32[3,8,256]{2,0,1:T(4,128)S(1)} collective-permute-done((f32[3,8,256]{2,0,1:T(4,128)S(1)}, f32[3,8,256]{2,0,1:T(4,128)S(1)}, u32[]{:S(2)}, u32[]{:S(2)}) %collective-permute-start.33) | collective-permute-done | bytes 24608 | tf_op jit(solution)/shard_map/ppermute | solution.py:105
  181.8 3.4 %collective-permute-done.34 = s16[3,256,128]{2,1,0:T(8,128)(2,1)S(1)} collective-permute-done((s16[3,256,128]{2,1,0:T(8,128)(2,1)S(1)}, s16[3,256,128]{2,1,0:T(8,128)(2,1)S(1)}, u32[]{:S(2)}, u32[]{:S(2)}) %collective-permute-start.34) | collective-permute-done | bytes 196640 | tf_op jit(solution)/shard_map/ppermute | solution.py:105
  185.6 3.4 %collective-permute-done.44 = s16[3,256,128]{2,1,0:T(8,128)(2,1)S(1)} collective-permute-done((s16[3,256,128]{2,1,0:T(8,128)(2,1)S(1)}, s16[3,256,128]{2,1,0:T(8,128)(2,1)S(1)}, u32[]{:S(2)}, u32[]{:S(2)}) %collective-permute-start.44) | collective-permute-done | bytes 196640 | tf_op jit(solution)/shard_map/ppermute | solution.py:105
  (184 shorter events, 37.0 us)
Async XLA Ops:
  0.0 19.9 %collective-permute-start = (s32[4,16]{1,0:T(4,128)}, s32[4,16]{1,0:T(4,128)S(1)}, u32[]{:S(2)}, u32[]{:S(2)}) collective-permute-start(s32[4,16]{1,0:T(4,128)} %param.8), channel_id=1, source_target_pairs={{0,16},{2,18},{4,20},{6,22},{8,24},{10,26},{12,28},{14,30},{16,0},... | collective-permute-start | bytes 776 | tf_op jit(solution)/shard_map/ppermute | solution.py:105
  5.7 49.5 %collective-permute-start.2 = (bf16[2,3,256,128]{3,2,1,0:T(8,128)(2,1)S(1)}, bf16[2,3,256,128]{3,2,1,0:T(8,128)(2,1)S(1)}, u32[]{:S(2)}, u32[]{:S(2)}) collective-permute-start(bf16[2,3,256,128]{3,2,1,0:T(8,128)(2,1)S(1)} %pad_maximum_fusion.1.refs_0_), channel_id=1, source_target_pairs={{0,8},{2,10},{4,12},{6,14},{8,0},{10,2},{12,4},{14,6},{16,24},{18,... | collective-permute-start | bytes 1179656 | tf_op jit(solution)/shard_map/ppermute | solution.py:105
  8.3 18.4 %collective-permute-start.1 = (bf16[3,256,128]{2,1,0:T(8,128)(2,1)}, bf16[3,256,128]{2,1,0:T(8,128)(2,1)S(1)}, u32[]{:S(2)}, u32[]{:S(2)}) collective-permute-start(bf16[3,256,128]{2,1,0:T(8,128)(2,1)} %get-tuple-element.45), channel_id=1, source_target_pairs={{0,16},{2,18},{4,20},{6,22},{8,24},{10,26},{12,28},{14,30},{16,0},... | collective-permute-start | bytes 589832 | tf_op jit(solution)/shard_map/ppermute | solution.py:105
  10.2 18.9 %collective-permute-start.15 = (bf16[3,256,128]{2,1,0:T(8,128)(2,1)}, bf16[3,256,128]{2,1,0:T(8,128)(2,1)S(1)}, u32[]{:S(2)}, u32[]{:S(2)}) collective-permute-start(bf16[3,256,128]{2,1,0:T(8,128)(2,1)} %get-tuple-element.47), channel_id=1, source_target_pairs={{0,16},{2,18},{4,20},{6,22},{8,24},{10,26},{12,28},{14,30},{16,0},... | collective-permute-start | bytes 589832 | tf_op jit(solution)/shard_map/ppermute | solution.py:105
  19.9 35.3 %collective-permute-start.3 = (bf16[2,3,256,128]{3,2,1,0:T(8,128)(2,1)S(1)}, bf16[2,3,256,128]{3,2,1,0:T(8,128)(2,1)}, u32[]{:S(2)}, u32[]{:S(2)}) collective-permute-start(bf16[2,3,256,128]{3,2,1,0:T(8,128)(2,1)S(1)} %pad_maximum_fusion.1.refs_0_), channel_id=1, source_target_pairs={{0,4},{2,6},{4,0},{6,2},{8,12},{10,14},{12,8},{14,10},{16,20},{18,... | collective-permute-start | bytes 1179656 | tf_op jit(solution)/shard_map/ppermute | solution.py:105
  26.0 29.3 %collective-permute-start.5 = (bf16[2,3,256,128]{3,2,1,0:T(8,128)(2,1)S(1)}, bf16[2,3,256,128]{3,2,1,0:T(8,128)(2,1)}, u32[]{:S(2)}, u32[]{:S(2)}) collective-permute-start(bf16[2,3,256,128]{3,2,1,0:T(8,128)(2,1)S(1)} %pad_maximum_fusion.1.refs_0_), channel_id=1, source_target_pairs={{0,2},{2,0},{4,6},{6,4},{8,10},{10,8},{12,14},{14,12},{16,18},{18,... | collective-permute-start | bytes 1179656 | tf_op jit(solution)/shard_map/ppermute | solution.py:105
  26.7 29.2 %collective-permute-start.16 = (bf16[2,3,256,128]{3,2,1,0:T(8,128)(2,1)S(1)}, bf16[2,3,256,128]{3,2,1,0:T(8,128)(2,1)S(1)}, u32[]{:S(2)}, u32[]{:S(2)}) collective-permute-start(bf16[2,3,256,128]{3,2,1,0:T(8,128)(2,1)S(1)} %pad_maximum_fusion.2.refs_0_), channel_id=1, source_target_pairs={{0,8},{2,10},{4,12},{6,14},{8,0},{10,2},{12,4},{14,6},{16,24},{18,... | collective-permute-start | bytes 1179656 | tf_op jit(solution)/shard_map/ppermute | solution.py:105
  55.3 18.7 %collective-permute-start.27 = (bf16[2,3,256,128]{3,2,1,0:T(8,128)(2,1)S(1)}, bf16[2,3,256,128]{3,2,1,0:T(8,128)(2,1)S(1)}, u32[]{:S(2)}, u32[]{:S(2)}) collective-permute-start(bf16[2,3,256,128]{3,2,1,0:T(8,128)(2,1)S(1)} %pad_maximum_fusion.3.refs_0_), channel_id=1, source_target_pairs={{0,4},{2,6},{4,0},{6,2},{8,12},{10,14},{12,8},{14,10},{16,20},{18,... | collective-permute-start | bytes 1179656 | tf_op jit(solution)/shard_map/ppermute | solution.py:105
  55.8 19.5 %collective-permute-start.36 = (bf16[2,3,256,128]{3,2,1,0:T(8,128)(2,1)S(1)}, bf16[2,3,256,128]{3,2,1,0:T(8,128)(2,1)}, u32[]{:S(2)}, u32[]{:S(2)}) collective-permute-start(bf16[2,3,256,128]{3,2,1,0:T(8,128)(2,1)S(1)} %pad_maximum_fusion.4.refs_0_), channel_id=1, source_target_pairs={{0,8},{2,10},{4,12},{6,14},{8,0},{10,2},{12,4},{14,6},{16,24},{18,... | collective-permute-start | bytes 1179656 | tf_op jit(solution)/shard_map/ppermute | solution.py:105
  65.7 16.7 %collective-permute-start.37 = (bf16[2,3,256,128]{3,2,1,0:T(8,128)(2,1)S(1)}, bf16[2,3,256,128]{3,2,1,0:T(8,128)(2,1)S(1)}, u32[]{:S(2)}, u32[]{:S(2)}) collective-permute-start(bf16[2,3,256,128]{3,2,1,0:T(8,128)(2,1)S(1)} %pad_maximum_fusion.4.refs_0_), channel_id=1, source_target_pairs={{0,4},{2,6},{4,0},{6,2},{8,12},{10,14},{12,8},{14,10},{16,20},{18,... | collective-permute-start | bytes 1179656 | tf_op jit(solution)/shard_map/ppermute | solution.py:105
  68.0 16.0 %collective-permute-start.39 = (bf16[2,3,256,128]{3,2,1,0:T(8,128)(2,1)S(1)}, bf16[2,3,256,128]{3,2,1,0:T(8,128)(2,1)S(1)}, u32[]{:S(2)}, u32[]{:S(2)}) collective-permute-start(bf16[2,3,256,128]{3,2,1,0:T(8,128)(2,1)S(1)} %pad_maximum_fusion.4.refs_0_), channel_id=1, source_target_pairs={{0,2},{2,0},{4,6},{6,4},{8,10},{10,8},{12,14},{14,12},{16,18},{18,... | collective-permute-start | bytes 1179656 | tf_op jit(solution)/shard_map/ppermute | solution.py:105
  68.0 22.8 %collective-permute-start.4 = (bf16[2,3,256,128]{3,2,1,0:T(8,128)(2,1)S(1)}, bf16[2,3,256,128]{3,2,1,0:T(8,128)(2,1)S(1)}, u32[]{:S(2)}, u32[]{:S(2)}) collective-permute-start(bf16[2,3,256,128]{3,2,1,0:T(8,128)(2,1)S(1)} %collective-permute-done.2.refs_1_), channel_id=1, source_target_pairs={{0,4},{2,6},{4,0},{6,2},{8,12},{10,14},{12,8},{14,10},{16,20},{18,... | collective-permute-start | bytes 1179656 | tf_op jit(solution)/shard_map/ppermute | solution.py:105
  74.0 16.9 %collective-permute-start.6 = (bf16[2,3,256,128]{3,2,1,0:T(8,128)(2,1)S(1)}, bf16[2,3,256,128]{3,2,1,0:T(8,128)(2,1)S(1)}, u32[]{:S(2)}, u32[]{:S(2)}) collective-permute-start(bf16[2,3,256,128]{3,2,1,0:T(8,128)(2,1)S(1)} %collective-permute-done.2.refs_1_), channel_id=1, source_target_pairs={{0,2},{2,0},{4,6},{6,4},{8,10},{10,8},{12,14},{14,12},{16,18},{18,... | collective-permute-start | bytes 1179656 | tf_op jit(solution)/shard_map/ppermute | solution.py:105
  75.3 17.9 %collective-permute-start.7 = (bf16[2,3,256,128]{3,2,1,0:T(8,128)(2,1)}, bf16[2,3,256,128]{3,2,1,0:T(8,128)(2,1)S(1)}, u32[]{:S(2)}, u32[]{:S(2)}) collective-permute-start(bf16[2,3,256,128]{3,2,1,0:T(8,128)(2,1)} %collective-permute-done.3.refs_2_), channel_id=1, source_target_pairs={{0,2},{2,0},{4,6},{6,4},{8,10},{10,8},{12,14},{14,12},{16,18},{18,... | collective-permute-start | bytes 1179656 | tf_op jit(solution)/shard_map/ppermute | solution.py:105
  82.4 17.0 %collective-permute-start.18 = (bf16[2,3,256,128]{3,2,1,0:T(8,128)(2,1)}, bf16[2,3,256,128]{3,2,1,0:T(8,128)(2,1)}, u32[]{:S(2)}, u32[]{:S(2)}) collective-permute-start(bf16[2,3,256,128]{3,2,1,0:T(8,128)(2,1)} %copy-done.3), channel_id=1, source_target_pairs={{0,4},{2,6},{4,0},{6,2},{8,12},{10,14},{12,8},{14,10},{16,20},{18,... | collective-permute-start | bytes 1179656 | tf_op jit(solution)/shard_map/ppermute | solution.py:105
  91.7 16.1 %collective-permute-start.28 = (bf16[2,3,256,128]{3,2,1,0:T(8,128)(2,1)S(1)}, bf16[2,3,256,128]{3,2,1,0:T(8,128)(2,1)}, u32[]{:S(2)}, u32[]{:S(2)}) collective-permute-start(bf16[2,3,256,128]{3,2,1,0:T(8,128)(2,1)S(1)} %collective-permute-done.26.refs_1_), channel_id=1, source_target_pairs={{0,4},{2,6},{4,0},{6,2},{8,12},{10,14},{12,8},{14,10},{16,20},{18,... | collective-permute-start | bytes 1179656 | tf_op jit(solution)/shard_map/ppermute | solution.py:105
  94.0 21.3 %collective-permute-start.38 = (bf16[2,3,256,128]{3,2,1,0:T(8,128)(2,1)}, bf16[2,3,256,128]{3,2,1,0:T(8,128)(2,1)}, u32[]{:S(2)}, u32[]{:S(2)}) collective-permute-start(bf16[2,3,256,128]{3,2,1,0:T(8,128)(2,1)} %collective-permute-done.36.refs_1_), channel_id=1, source_target_pairs={{0,4},{2,6},{4,0},{6,2},{8,12},{10,14},{12,8},{14,10},{16,20},{18,... | collective-permute-start | bytes 1179656 | tf_op jit(solution)/shard_map/ppermute | solution.py:105
  99.4 17.1 %collective-permute-start.40 = (bf16[2,3,256,128]{3,2,1,0:T(8,128)(2,1)}, bf16[2,3,256,128]{3,2,1,0:T(8,128)(2,1)S(1)}, u32[]{:S(2)}, u32[]{:S(2)}) collective-permute-start(bf16[2,3,256,128]{3,2,1,0:T(8,128)(2,1)} %collective-permute-done.36.refs_1_), channel_id=1, source_target_pairs={{0,2},{2,0},{4,6},{6,4},{8,10},{10,8},{12,14},{14,12},{16,18},{18,... | collective-permute-start | bytes 1179656 | tf_op jit(solution)/shard_map/ppermute | solution.py:105
  99.4 17.7 %collective-permute-start.41 = (bf16[2,3,256,128]{3,2,1,0:T(8,128)(2,1)}, bf16[2,3,256,128]{3,2,1,0:T(8,128)(2,1)S(1)}, u32[]{:S(2)}, u32[]{:S(2)}) collective-permute-start(bf16[2,3,256,128]{3,2,1,0:T(8,128)(2,1)} %copy-done.7), channel_id=1, source_target_pairs={{0,2},{2,0},{4,6},{6,4},{8,10},{10,8},{12,14},{14,12},{16,18},{18,... | collective-permute-start | bytes 1179656 | tf_op jit(solution)/shard_map/ppermute | solution.py:105
  99.9 17.2 %collective-permute-start.8 = (bf16[2,3,256,128]{3,2,1,0:T(8,128)(2,1)}, bf16[2,3,256,128]{3,2,1,0:T(8,128)(2,1)S(1)}, u32[]{:S(2)}, u32[]{:S(2)}) collective-permute-start(bf16[2,3,256,128]{3,2,1,0:T(8,128)(2,1)} %copy-done.11), channel_id=1, source_target_pairs={{0,2},{2,0},{4,6},{6,4},{8,10},{10,8},{12,14},{14,12},{16,18},{18,... | collective-permute-start | bytes 1179656 | tf_op jit(solution)/shard_map/ppermute | solution.py:105
  116.5 29.6 %collective-permute-start.29 = (bf16[2,3,256,128]{3,2,1,0:T(8,128)(2,1)S(1)}, bf16[2,3,256,128]{3,2,1,0:T(8,128)(2,1)S(1)}, u32[]{:S(2)}, u32[]{:S(2)}) collective-permute-start(bf16[2,3,256,128]{3,2,1,0:T(8,128)(2,1)S(1)} %pad_maximum_fusion.3.refs_0_), channel_id=1, source_target_pairs={{0,2},{2,0},{4,6},{6,4},{8,10},{10,8},{12,14},{14,12},{16,18},{18,... | collective-permute-start | bytes 1179656 | tf_op jit(solution)/shard_map/ppermute | solution.py:105
  117.0 29.2 %collective-permute-start.30 = (bf16[2,3,256,128]{3,2,1,0:T(8,128)(2,1)S(1)}, bf16[2,3,256,128]{3,2,1,0:T(8,128)(2,1)S(1)}, u32[]{:S(2)}, u32[]{:S(2)}) collective-permute-start(bf16[2,3,256,128]{3,2,1,0:T(8,128)(2,1)S(1)} %collective-permute-done.26.refs_1_), channel_id=1, source_target_pairs={{0,2},{2,0},{4,6},{6,4},{8,10},{10,8},{12,14},{14,12},{16,18},{18,... | collective-permute-start | bytes 1179656 | tf_op jit(solution)/shard_map/ppermute | solution.py:105
  117.1 31.9 %collective-permute-start.31 = (bf16[2,3,256,128]{3,2,1,0:T(8,128)(2,1)}, bf16[2,3,256,128]{3,2,1,0:T(8,128)(2,1)S(1)}, u32[]{:S(2)}, u32[]{:S(2)}) collective-permute-start(bf16[2,3,256,128]{3,2,1,0:T(8,128)(2,1)} %copy-done.1), channel_id=1, source_target_pairs={{0,2},{2,0},{4,6},{6,4},{8,10},{10,8},{12,14},{14,12},{16,18},{18,... | collective-permute-start | bytes 1179656 | tf_op jit(solution)/shard_map/ppermute | solution.py:105
  117.6 31.6 %collective-permute-start.32 = (bf16[2,3,256,128]{3,2,1,0:T(8,128)(2,1)}, bf16[2,3,256,128]{3,2,1,0:T(8,128)(2,1)S(1)}, u32[]{:S(2)}, u32[]{:S(2)}) collective-permute-start(bf16[2,3,256,128]{3,2,1,0:T(8,128)(2,1)} %collective-permute-done.28.refs_3_), channel_id=1, source_target_pairs={{0,2},{2,0},{4,6},{6,4},{8,10},{10,8},{12,14},{14,12},{16,18},{18,... | collective-permute-start | bytes 1179656 | tf_op jit(solution)/shard_map/ppermute | solution.py:105
  128.0 15.2 %collective-permute-start.25 = (bf16[3,256,128]{2,1,0:T(8,128)(2,1)S(1)}, bf16[3,256,128]{2,1,0:T(8,128)(2,1)S(1)}, u32[]{:S(2)}, u32[]{:S(2)}) collective-permute-start(bf16[3,256,128]{2,1,0:T(8,128)(2,1)S(1)} %copy-done.28), channel_id=1, source_target_pairs={{0,16},{2,18},{4,20},{6,22},{8,24},{10,26},{12,28},{14,30},{16,0},... | collective-permute-start | bytes 589832 | tf_op jit(solution)/shard_map/ppermute | solution.py:105
  143.2 24.4 %collective-permute-start.9 = (f32[3,8,256]{2,0,1:T(4,128)S(1)}, f32[3,8,256]{2,0,1:T(4,128)S(1)}, u32[]{:S(2)}, u32[]{:S(2)}) collective-permute-start(f32[3,8,256]{2,0,1:T(4,128)S(1)} %copy.21), channel_id=1, source_target_pairs={{0,16},{2,18},{4,20},{6,22},{8,24},{10,26},{12,28},{14,30},{16,0},... | collective-permute-start | bytes 73736 | tf_op jit(solution)/shard_map/ppermute | solution.py:105
  146.1 34.9 %collective-permute-start.10 = (s16[3,256,128]{2,1,0:T(8,128)(2,1)S(1)}, s16[3,256,128]{2,1,0:T(8,128)(2,1)S(1)}, u32[]{:S(2)}, u32[]{:S(2)}) collective-permute-start(s16[3,256,128]{2,1,0:T(8,128)(2,1)S(1)} %get-tuple-element.24), channel_id=1, source_target_pairs={{0,16},{2,18},{4,20},{6,22},{8,24},{10,26},{12,28},{14,30},{16,0},... | collective-permute-start | bytes 589832 | tf_op jit(solution)/shard_map/ppermute | solution.py:105
  146.2 24.5 %collective-permute-start.23 = (f32[3,8,256]{2,0,1:T(4,128)S(1)}, f32[3,8,256]{2,0,1:T(4,128)S(1)}, u32[]{:S(2)}, u32[]{:S(2)}) collective-permute-start(f32[3,8,256]{2,0,1:T(4,128)S(1)} %copy.25), channel_id=1, source_target_pairs={{0,16},{2,18},{4,20},{6,22},{8,24},{10,26},{12,28},{14,30},{16,0},... | collective-permute-start | bytes 73736 | tf_op jit(solution)/shard_map/ppermute | solution.py:105
  149.0 32.4 %collective-permute-start.24 = (s16[3,256,128]{2,1,0:T(8,128)(2,1)S(1)}, s16[3,256,128]{2,1,0:T(8,128)(2,1)S(1)}, u32[]{:S(2)}, u32[]{:S(2)}) collective-permute-start(s16[3,256,128]{2,1,0:T(8,128)(2,1)S(1)} %get-tuple-element.28), channel_id=1, source_target_pairs={{0,16},{2,18},{4,20},{6,22},{8,24},{10,26},{12,28},{14,30},{16,0},... | collective-permute-start | bytes 589832 | tf_op jit(solution)/shard_map/ppermute | solution.py:105
  149.1 18.5 %collective-permute-start.43 = (f32[3,8,256]{2,1,0:T(8,128)S(1)}, f32[3,8,256]{2,1,0:T(8,128)S(1)}, u32[]{:S(2)}, u32[]{:S(2)}) collective-permute-start(f32[3,8,256]{2,1,0:T(8,128)S(1)} %get-tuple-element.35), channel_id=1, source_target_pairs={{0,16},{2,18},{4,20},{6,22},{8,24},{10,26},{12,28},{14,30},{16,0},... | collective-permute-start | bytes 73736 | tf_op jit(solution)/shard_map/ppermute | solution.py:105
  167.6 17.5 %collective-permute-start.34 = (s16[3,256,128]{2,1,0:T(8,128)(2,1)S(1)}, s16[3,256,128]{2,1,0:T(8,128)(2,1)S(1)}, u32[]{:S(2)}, u32[]{:S(2)}) collective-permute-start(s16[3,256,128]{2,1,0:T(8,128)(2,1)S(1)} %get-tuple-element.32), channel_id=1, source_target_pairs={{0,16},{2,18},{4,20},{6,22},{8,24},{10,26},{12,28},{14,30},{16,0},... | collective-permute-start | bytes 589832 | tf_op jit(solution)/shard_map/ppermute | solution.py:105
  170.7 18.3 %collective-permute-start.44 = (s16[3,256,128]{2,1,0:T(8,128)(2,1)S(1)}, s16[3,256,128]{2,1,0:T(8,128)(2,1)S(1)}, u32[]{:S(2)}, u32[]{:S(2)}) collective-permute-start(s16[3,256,128]{2,1,0:T(8,128)(2,1)S(1)} %get-tuple-element.36), channel_id=1, source_target_pairs={{0,16},{2,18},{4,20},{6,22},{8,24},{10,26},{12,28},{14,30},{16,0},... | collective-permute-start | bytes 589832 | tf_op jit(solution)/shard_map/ppermute | solution.py:105
  (47 other events, 574.3 us)

commit v2 on v0

v2 whole, which is shorter than its diff:
```python
import functools
import math

import jax
import jax.numpy as jnp
from jax import lax
from jax.experimental import pallas as pl
from jax.experimental.pallas import tpu as pltpu
from jax.sharding import PartitionSpec as P

CUBE = 64
NEG = -1e30
LEVELS = 32766.0
FRACTION = 32767.0


def pool_cubes(field):
    heads, tokens, width = field.shape
    summed = jnp.sum(field.reshape(heads, tokens // CUBE, CUBE, width), axis=2, dtype=jnp.float32)
    return (summed / CUBE).astype(jnp.bfloat16)


def pack_kernel(spans, core_ref, keys_ref, values_ref, got_ref, *pack_refs):
    tokens = keys_ref.shape[1]
    share = got_ref.shape[1]
    for (first, size), pack_ref in zip(spans, pack_refs):
        heads = pl.ds(core_ref[0] * share + first, size)
        pack_ref[0, :, :tokens] = keys_ref[heads]
        pack_ref[1, :, :tokens] = values_ref[heads]
        pack_ref[:, :, tokens:] = got_ref[:, first : first + size]


def pack_groups(spans, core, keys, values, got):
    tokens, width = keys.shape[1:]

    def whole(shape):
        return pl.BlockSpec(tuple(shape), lambda h, core: (0,) * len(shape))

    outs = [jax.ShapeDtypeStruct((2, size, 2 * tokens, width), keys.dtype) for _, size in spans]
    return pl.pallas_call(
        functools.partial(pack_kernel, spans),
        grid_spec=pltpu.PrefetchScalarGridSpec(
            num_scalar_prefetch=1,
            grid=(1,),
            in_specs=[whole(a.shape) for a in (keys, values, got)],
            out_specs=[whole(out.shape) for out in outs],
        ),
        out_shape=outs,
        compiler_params=pltpu.CompilerParams(vmem_limit_bytes=24 * 1024 * 1024),
    )(core[None], keys, values, got)


def attend_kernel(blocks, factor, bias_ref, own_q_ref, far_q_ref, *refs):
    kv_refs = refs[:blocks]
    own_acc_ref, own_stat_ref, code_ref = refs[blocks : blocks + 3]
    scratch = refs[blocks + 3 :]
    heads, rows, width = own_q_ref.shape
    span = kv_refs[0].shape[2]
    cubes = rows // CUBE
    lane = lax.broadcasted_iota(jnp.int32, (rows, width), 1)
    ones = jnp.ones((span, width), jnp.bfloat16)
    for head in range(heads):
        for half, q_ref in enumerate((own_q_ref, far_q_ref)):
            score_ref = scratch[(2 * head + half) % len(scratch)]
            cube = lax.broadcasted_iota(jnp.int32, (rows, width), 0) // CUBE + half * cubes
            query = jnp.concatenate([q_ref[head], (lane == cube).astype(jnp.bfloat16)], axis=1)
            top = jnp.full((rows, width), NEG, jnp.float32)
            for b, ref in enumerate(kv_refs):
                key = jnp.concatenate([ref[0, head], bias_ref[b * span : (b + 1) * span]], axis=1)
                scores = lax.dot_general(
                    query, key, (((1,), (1,)), ((), ())), preferred_element_type=jnp.float32
                )
                for i in range(0, span, width):
                    top = jnp.maximum(top, scores[:, i : i + width])
                score_ref[:, b * span : (b + 1) * span] = scores
            top = jnp.max(top, axis=1, keepdims=True)
            both = jnp.zeros((rows, 2 * width), jnp.float32)
            for b, ref in enumerate(kv_refs):
                listed = jnp.concatenate([ref[1, head], ones], axis=1)
                weights = jnp.exp2((score_ref[:, b * span : (b + 1) * span] - top) * factor)
                both += jnp.dot(
                    weights.astype(jnp.bfloat16), listed, preferred_element_type=jnp.float32
                )
            acc, total = both[:, :width], both[:, width:]
            level = jnp.maximum(top * factor, -30000.0) + jnp.log2(total)
            result = acc / total
            if half == 0:
                own_acc_ref[head] = result
                own_stat_ref[head] = jnp.transpose(level)[:8]
            else:
                peak = jnp.max(jnp.abs(result), axis=1, keepdims=True)
                power = jnp.ceil(jnp.log2(jnp.maximum(peak, 1e-30)) + 1e-3)
                code = jnp.floor(result * (jnp.exp2(-power) * LEVELS) + 0.5)
                code_ref[head, :rows] = code.astype(jnp.int32).astype(jnp.int16)
                units = jnp.floor(level)
                fraction = jnp.floor((level - units) * FRACTION + 0.5)
                stats = jnp.where(lane == 0, units, jnp.where(lane == 1, fraction, power))
                stats = jnp.transpose(stats)[:8]
                stats = jnp.concatenate(
                    [stats[:, i * width : (i + 1) * width] for i in range(rows // width)], axis=0
                )
                code_ref[head, rows:] = stats.astype(jnp.int32).astype(jnp.int16)


def attend(heads, bias, own_q, far_q, blocks):
    span, width = blocks[0][1].shape[2:]
    rows = own_q[1].shape[1]
    factor = math.log2(math.e) / math.sqrt(width)
    extra = 8 * (rows // width)

    def whole(array):
        return pl.BlockSpec(array.shape, lambda h: (0,) * len(array.shape))

    def queries_from(start):
        shape = tuple(pl.Element(n) for n in (heads, rows, width))
        return pl.BlockSpec(shape, lambda h: (start, 0, 0))

    def block_from(start):
        shape = tuple(pl.Element(n) for n in (2, heads, span, width))
        return pl.BlockSpec(shape, lambda h: (0, start, 0, 0))

    outs = [
        jax.ShapeDtypeStruct((heads, rows, width), jnp.float32),
        jax.ShapeDtypeStruct((heads, 8, rows), jnp.float32),
        jax.ShapeDtypeStruct((heads, rows + extra, width), jnp.int16),
    ]
    work = heads * 2 * rows * len(blocks) * span
    return pl.pallas_call(
        functools.partial(attend_kernel, len(blocks), factor),
        grid=(1,),
        in_specs=[whole(bias), queries_from(own_q[0]), queries_from(far_q[0])]
        + [block_from(start) for start, _ in blocks],
        out_specs=[whole(out) for out in outs],
        out_shape=outs,
        scratch_shapes=[pltpu.VMEM((rows, len(blocks) * span), jnp.float32)] * 4,
        compiler_params=pltpu.CompilerParams(vmem_limit_bytes=60 * 1024 * 1024),
        cost_estimate=pl.CostEstimate(
            flops=work * width * 8,
            bytes_accessed=heads * rows * width * 2 * (2 * len(blocks) + 5),
            transcendentals=work,
        ),
    )(bias, own_q[1], far_q[1], *[array for _, array in blocks])


def merge_kernel(own_acc_ref, own_stat_ref, code_ref, gate_ref, coarse_ref, *out_refs):
    tokens = out_refs[0].shape[1]
    heads, rows, width = own_acc_ref.shape
    for head in range(heads):
        stats = code_ref[head, rows:].astype(jnp.int32).astype(jnp.float32)
        for i in range(rows // width):
            part = slice(i * width, (i + 1) * width)
            sent = stats[8 * i : 8 * i + 8]
            own = own_stat_ref[head, :, part]
            far = sent[0:1] + sent[1:2] * (1.0 / FRACTION)
            far = jnp.broadcast_to(far, own.shape)
            best = jnp.maximum(own, far)
            own = jnp.exp2(own - best)
            far = jnp.exp2(far - best)
            total = own + far
            step = jnp.exp2(jnp.broadcast_to(sent[2:3], own.shape)) * (1.0 / LEVELS)
            gate = jnp.broadcast_to(gate_ref[head, :, part].astype(jnp.float32), own.shape)
            row = lax.broadcasted_iota(jnp.int32, own.shape, 0)
            shares = jnp.where(row == 0, own / total, jnp.where(row == 1, far / total * step, gate))
            shares = jnp.transpose(shares)
            code = code_ref[head, part].astype(jnp.int32).astype(jnp.float32)
            fine = own_acc_ref[head, part] * shares[:, 0:1] + code * shares[:, 1:2]
            per = width // CUBE
            coarse = jnp.concatenate(
                [
                    jnp.broadcast_to(coarse_ref[head, c : c + 1], (CUBE, width))
                    for c in range(i * per, (i + 1) * per)
                ],
                axis=0,
            )
            at = i * width % tokens
            out_refs[i * width // tokens][head, at : at + width] = (fine + shares[:, 2:3] * coarse).astype(jnp.bfloat16)


def merge(first, tokens, own_acc, own_stat, code, gate, coarse):
    heads, rows, width = own_acc.shape

    def block(array, start):
        shape = (heads,) + array.shape[1:]
        return pl.BlockSpec(tuple(pl.Element(n) for n in shape), lambda h: (start, 0, 0))

    arrays = [own_acc, own_stat, code, gate, coarse]
    outs = [jax.ShapeDtypeStruct((heads, tokens, width), jnp.bfloat16)] * (rows // tokens)
    return pl.pallas_call(
        merge_kernel,
        grid=(1,),
        in_specs=[block(a, s) for a, s in zip(arrays, (0, 0, 0, first, first))],
        out_specs=[block(out, 0) for out in outs],
        out_shape=outs,
        compiler_params=pltpu.CompilerParams(vmem_limit_bytes=16 * 1024 * 1024),
        cost_estimate=pl.CostEstimate(
            flops=heads * rows * width * 4, bytes_accessed=heads * rows * width * 8, transcendentals=0
        ),
    )(*arrays)


def after(array, *others):
    return lax.optimization_barrier((array,) + others)[0] if others else array


def plan_of(heads):
    if heads == 6:
        return [2, 2, 1, 1], [(0, 2), (2, 4)], [(0, 1), (1, 2), (2, 4)], [(0, 1), (1, 4)]
    return [heads], [(0, 1)], [(0, 1)], [(0, 1)]


def body(ring, queries, keys, values, block_lists, coarse_gate):
    tokens, width = queries.shape[1:]
    scale = 1.0 / math.sqrt(width)
    half = ring // 2
    me = lax.axis_index("ctx")

    def swap(array, bit):
        return lax.ppermute(array, "ctx", [(i, i ^ bit) for i in range(ring)])

    split = queries.shape[0] % 2 == 0
    offsets = [0, 1] if split else [0]
    heads = queries.shape[0] // len(offsets)
    own_cubes = tokens // CUBE
    sizes, to_side, to_next, to_far = plan_of(heads)
    starts = [sum(sizes[:i]) for i in range(len(sizes) + 1)]
    parts = range(len(sizes))
    spans = [(starts[low], starts[high] - starts[low]) for low, high in to_side + to_next]

    def cut(array, start):
        return lax.dynamic_slice_in_dim(array, start, heads, 0)

    pooled = jnp.concatenate([pool_cubes(keys), pool_cubes(values)], axis=2)
    lists = jnp.zeros((1, own_cubes + 1, 2 * width), jnp.bfloat16)
    lists = lists.at[0, :own_cubes, : block_lists.shape[1]].set(block_lists.astype(jnp.bfloat16))
    gate = coarse_gate.reshape(-1, 1, 2 * width)
    small = jnp.concatenate([jnp.concatenate([pooled, gate], axis=1), lists], axis=0)
    far_small = swap(small, half)
    small = [small, far_small]
    if split:
        core = me & 1
        mine, theirs = core * heads, (1 - core) * heads
        got = swap(jnp.stack([cut(keys, theirs), cut(values, theirs)]), 1)
        packs = pack_groups(spans, core, keys, values, got)
        queries = after(queries, packs[0])
        queries = jnp.concatenate([cut(queries, mine), swap(cut(queries, theirs), 1)], axis=1)
        both = jnp.concatenate(small, axis=1)
        got = swap(jnp.concatenate([cut(both, theirs), both[-1:]], axis=0), 1)
        both = jnp.concatenate([cut(both, mine), both[-1:]], axis=0)
        step = own_cubes + 1
        small = [both[:, :step], got[:, :step], both[:, step:], got[:, step:]]
    else:
        packs = [jnp.stack([keys[f : f + n], values[f : f + n]]) for f, n in spans]
    pooled = jnp.concatenate([part[:heads, :own_cubes] for part in small], axis=1)
    lists = jnp.concatenate([part[heads, :own_cubes] for part in small], axis=0)
    lists = lists[:, : block_lists.shape[1]].astype(jnp.int32)
    gate = jnp.concatenate([part[:heads, own_cubes:] for part in small[: len(offsets)]], axis=2)
    heads, rows, width = queries.shape
    cubes = rows // CUBE
    side = len(offsets)
    masks = list(range(0, half, side))
    hops = [m for m in masks[1:] if m & -m == m]
    pooled_q = pool_cubes(queries)

    lanes = jnp.concatenate(
        [
            (me ^ m ^ o) * own_cubes + jnp.arange(tokens, dtype=jnp.int32) // CUBE
            for m in masks
            for o in offsets
        ]
    )
    hit = jnp.any(lists[:, :, None] == lanes[None, None, :], axis=1)
    bias = jnp.where(hit, 0.0, NEG).astype(jnp.bfloat16)
    bias = jnp.pad(bias.T, ((0, 0), (0, width - 2 * cubes)))

    side_packs, next_packs = packs[: len(to_side)], packs[len(to_side) :]
    held = [{} for _ in parts]
    wait = [far_small]
    for (low, high), pack in zip(to_side, side_packs):
        got = swap(after(pack, *wait), side)
        for part in range(low, high):
            held[part][0] = (starts[part] - starts[low], pack)
            held[part][side] = (starts[part] - starts[low], got)
        wait = [got]
    others = [far_small]
    pooled_wait = [far_small]
    wait = [far_small]
    for (low, high), pack in zip(to_next, next_packs):
        for mask in hops[1:]:
            got = swap(after(pack, *wait), mask)
            for part in range(low, high):
                held[part][mask] = (starts[part] - starts[low], got)
        if low == 0:
            others = [got]
        wait = [got]
    far_q = []
    wait = others
    for low, high in to_far:
        got = swap(after(queries[starts[low] : starts[high]], *wait), half)
        far_q += [(starts[part] - starts[low], got) for part in range(low, high)]
        wait = [got]
    for bit in hops:
        other = swap(after(pooled, *pooled_wait), bit)
        pooled = jnp.concatenate([pooled, other], axis=1)
        pooled_wait = others
    done = []
    for part in parts:
        wait = []
        if part == 1:
            bias = after(bias, held[parts[-1]][side][1])
        if part >= 2:
            wait = [done[part - 2][0]]
        if part == 2:
            bias = after(bias, done[0][2])
        for mask in masks[1:]:
            bit = mask & -mask
            if mask != bit:
                start, array = held[part][mask ^ bit]
                if array.shape[1] != sizes[part]:
                    array = array[:, start : start + sizes[part]]
                held[part][mask] = (0, swap(after(array, *wait), bit))
        blocks = [held[part][mask] for mask in masks]
        own_acc, own_stat, code = attend(
            sizes[part], bias, (starts[part], queries), far_q[part], blocks
        )
        done.append((own_acc, own_stat, swap(code, half)))

    coarse_scores = (
        jnp.einsum(
            "hqd,hkd->hqk", pooled_q, pooled[..., :width], preferred_element_type=jnp.float32
        )
        * scale
    )
    coarse_top = jnp.max(coarse_scores, axis=-1, keepdims=True)
    coarse_weights = jnp.exp(coarse_scores - coarse_top).astype(jnp.bfloat16)
    coarse_total = jnp.sum(coarse_weights.astype(jnp.float32), axis=-1)
    coarse_cube = (
        jnp.einsum(
            "hqk,hkd->hqd", coarse_weights, pooled[..., width:], preferred_element_type=jnp.float32
        )
        / coarse_total[..., None]
    )
    kept, received = [], []
    for part in parts:
        own_acc, own_stat, code = done[part]
        if part != parts[-1]:
            code = after(code, done[parts[-1]][0])
        outs = merge(starts[part], tokens, own_acc, own_stat, code, gate, coarse_cube)
        kept.append(outs[0])
        if split:
            received.append(swap(outs[1], 1))
    kept = jnp.concatenate(kept, axis=0)
    if not split:
        return kept
    received = jnp.concatenate(received, axis=0)
    first = jnp.where(core == 0, kept, received)
    second = jnp.where(core == 0, received, kept)
    return jnp.concatenate([first, second], axis=0)


def solution(mesh):
    in_specs = (
        P("head", "ctx", None),
        P("head", "ctx", None),
        P("head", "ctx", None),
        P("ctx", None),
        P("head", "ctx"),
    )
    out_specs = P("head", "ctx", None)
    return jax.shard_map(
        functools.partial(body, mesh.shape["ctx"]),
        mesh=mesh,
        in_specs=in_specs,
        out_specs=out_specs,
        check_vma=False,
    )
```

time: 349 us -> 124 us (0.36)
  waiting for transfers between devices: 159 us -> 51.5 us
  matrix products: 83.1 us -> 0.45 us
  blocking collectives: 44.1 us -> 0 us
  other arithmetic: 44.3 us -> 7.16 us
  Pallas kernels: 0 us -> 32.4 us
  starting transfers between devices: 0.04 us -> 24.6 us
  between operations: 13.5 us -> 0.57 us
  local copies, waits for them, and re-layouts: 3.75 us -> 7.27 us
    all_gather x2 -> x0, waiting for transfers between devices: 158 us -> none  [the longest x1 101 us: body(): tile_v = lax.all_gather(values, 'ctx', axis=1, tiled=True)]
    dot_general x18 -> x1, matrix products: 83.1 us -> 0.14 us  [body(): jnp.einsum('hqk,hkd->hqd', coarse_weights, pooled[..., width:], preferred...]
    ppermute x0 -> x25, waiting for transfers between devices: none -> 51.5 us  [swap(): return lax.ppermute(array, 'ctx', [(i, i ^ bit) for i in range(ring)])]
    all_gather x2 -> x0, blocking collectives: 44.1 us -> none  [the longest x1 24.8 us: body(): lax.all_gather(pooled_v, 'ctx', axis=1, tiled=True)]
    reduce_sum x9 -> x0, other arithmetic: 35.6 us -> none  [soft_update(): jnp.sum(weights.astype(jnp.float32), axis=-1)]
    pallas_call x0 -> x7, Pallas kernels: none -> 32.4 us  [the longest x4 29.9 us: attend(): pl.pallas_call(functools.partial(attend_kernel, len(blocks), factor), gri...]
    ppermute x0 -> x25, starting transfers between devices: none -> 24.6 us  [swap(): return lax.ppermute(array, 'ctx', [(i, i ^ bit) for i in range(ring)])]
    convert_element_type x2, other arithmetic: 3.56 us -> 0.03 us  [the longest x1 0.02 us: body(): bias = jnp.where(hit, 0.0, NEG).astype(jnp.bfloat16)]
  transfers between devices with their start and end apart: 2 -> 25, of which waited for: 2 -> 8; matrix products, arithmetic and copies ran while one was open for 2% -> 6% of each run, Pallas kernels for 0% -> 26%
where the time goes in v2:
time: 124 us
  waiting for transfers between devices  51.5 us (42%)
  Pallas kernels  32.4 us (26%)
  starting transfers between devices  24.6 us (20%)
  local copies, waits for them, and re-layouts  7.27 us (6%)
  other arithmetic  7.16 us (6%)
    ppermute x25, waiting for transfers between devices, swap(): return lax.ppermute(array, 'ctx', [(i, i ^ bit) for i in range(ring)])  51.5 us
    pallas_call x4, Pallas kernels, attend(): pl.pallas_call(functools.partial(attend_kernel, len(blocks), factor), gri...  29.9 us
    ppermute x25, starting transfers between devices, swap(): return lax.ppermute(array, 'ctx', [(i, i ^ bit) for i in range(ring)])  24.6 us
    unnamed x47, local copies, waits for them, and re-layouts  3.16 us
  transfers between devices with their start and end apart: 25, of which 8 were waited for; matrix products, arithmetic and copies ran while one was open for 6% of the time, Pallas kernels for 26%

profile of v2, /device:TPU:0, one launch (start us, length us, event | category | flops | bytes accessed | tf_op | source)
XLA Modules:
  0.0 123.9 jit_solution(3036883729778548901)
XLA Ops:
  0.0 0.8 convert_bitcast_fusion
  1.5 1.3 %convert_reduce_fusion.2 = f32[12,4,128]{2,1,0:T(4,128)S(1)} fusion(bf16[12,256,128]{2,1,0:T(8,128)(2,1)} %keys_ref.1), kind=kLoop, calls=%fused_computation.3 | loop fusion | flops 780288 | bytes 811008 | tf_op jit(solution)/shard_map/reduce_sum | solution.py:19
  3.1 4.1 %collective-permute-start = (bf16[13,5,256]{2,1,0:T(8,128)(2,1)S(1)}, bf16[13,5,256]{2,1,0:T(8,128)(2,1)S(1)}, u32[]{:S(2)}, u32[]{:S(2)}) collective-permute-start(bf16[13,5,256]{2,1,0:T(8,128)(2,1)S(1)} %pad_maximum_fusion.5), channel_id=1, source_target_pairs={{0,16},{2,18},{4,20},{6,22},{8,24},{10,26},{12,28},{14,30},{16,0},... | collective-permute-start | bytes 99848 | tf_op jit(solution)/shard_map/ppermute | solution.py:218
  7.6 2.3 %collective-permute-done = bf16[13,5,256]{2,1,0:T(8,128)(2,1)S(1)} collective-permute-done((bf16[13,5,256]{2,1,0:T(8,128)(2,1)S(1)}, bf16[13,5,256]{2,1,0:T(8,128)(2,1)S(1)}, u32[]{:S(2)}, u32[]{:S(2)}) %collective-permute-start) | collective-permute-done | bytes 33312 | tf_op jit(solution)/shard_map/ppermute | solution.py:218
  10.2 1.2 collective-permute-done.1
  11.4 1.8 %collective-permute-start.15 = (bf16[6,16,256]{2,1,0:T(8,128)(2,1)S(1)}, bf16[6,16,256]{2,1,0:T(8,128)(2,1)S(1)}, u32[]{:S(2)}, u32[]{:S(2)}) collective-permute-start(bf16[6,16,256]{2,1,0:T(8,128)(2,1)S(1)} %pad_maximum_fusion.6), channel_id=1, source_target_pairs={{0,4},{2,6},{4,0},{6,2},{8,12},{10,14},{12,8},{14,10},{16,20},{18,... | collective-permute-start | bytes 147464 | tf_op jit(solution)/shard_map/ppermute | solution.py:218
  13.8 1.0 shard_map.55
  14.8 0.8 copy-done.9
  15.6 1.1 collective-permute-start.4
  17.4 12.0 %collective-permute-done.4.refs_2_ = bf16[2,2,512,128]{3,2,1,0:T(8,128)(2,1)} collective-permute-done((bf16[2,2,512,128]{3,2,1,0:T(8,128)(2,1)S(1)}, bf16[2,2,512,128]{3,2,1,0:T(8,128)(2,1)}, u32[]{:S(2)}, u32[]{:S(2)}) %collective-permute-start.4) | collective-permute-done | bytes 524320 | tf_op jit(solution)/shard_map/ppermute | solution.py:218
  29.4 1.1 collective-permute-start.11
  30.8 0.9 pad.9.bias_ref
  31.7 1.9 %concatenate.60 = bf16[6,32,256]{2,1,0:T(8,128)(2,1)} concatenate(bf16[6,4,256]{2,1,0:T(4,128)(2,1)S(1)} %get-tuple-element.116, bf16[6,4,256]{2,1,0:T(4,128)(2,1)S(1)} %get-tuple-element.118, bf16[6,4,256]{2,1,0:T(4,128)(2,1)S(1)} %get-tuple-element.115, bf16[6,4,256]{2,1,0:T(4,128)(2,1)S(1)} %get-tuple-element.117, bf16[6,16,256]{2,1,0:T(8,128)(2,1)S(1)} %collective-permute-done.15), dimensions={1} | concatenate | bytes 196608 | tf_op jit(solution)/shard_map/concatenate | solution.py:303
  34.1 0.8 fusion
  35.0 0.9 pad_maximum_fusion.own_q_ref
  36.6 2.7 %collective-permute-start.5 = (bf16[2,512,128]{2,1,0:T(8,128)(2,1)S(1)}, bf16[2,512,128]{2,1,0:T(8,128)(2,1)}, u32[]{:S(2)}, u32[]{:S(2)}) collective-permute-start(bf16[2,512,128]{2,1,0:T(8,128)(2,1)S(1)} %fusion.1), channel_id=1, source_target_pairs={{0,16},{2,18},{4,20},{6,22},{8,24},{10,26},{12,28},{14,30},{16,0},... | collective-permute-start | bytes 786440 | tf_op jit(solution)/shard_map/ppermute | solution.py:218
  39.5 10.7 %collective-permute-done.16 = bf16[6,32,256]{2,1,0:T(8,128)(2,1)S(1)} collective-permute-done((bf16[6,32,256]{2,1,0:T(8,128)(2,1)}, bf16[6,32,256]{2,1,0:T(8,128)(2,1)S(1)}, u32[]{:S(2)}, u32[]{:S(2)}) %collective-permute-start.16) | collective-permute-done | bytes 98336 | tf_op jit(solution)/shard_map/ppermute | solution.py:218
  50.6 4.2 %collective-permute-start.10 = (bf16[4,512,128]{2,1,0:T(8,128)(2,1)}, bf16[4,512,128]{2,1,0:T(8,128)(2,1)}, u32[]{:S(2)}, u32[]{:S(2)}) collective-permute-start(bf16[4,512,128]{2,1,0:T(8,128)(2,1)} %fusion), channel_id=1, source_target_pairs={{0,16},{2,18},{4,20},{6,22},{8,24},{10,26},{12,28},{14,30},{16,0},... | collective-permute-start | bytes 1572872 | tf_op jit(solution)/shard_map/ppermute | solution.py:218
  54.9 2.0 %collective-permute-start.13 = (bf16[2,2,512,128]{3,2,1,0:T(8,128)(2,1)}, bf16[2,2,512,128]{3,2,1,0:T(8,128)(2,1)S(1)}, u32[]{:S(2)}, u32[]{:S(2)}) collective-permute-start(bf16[2,2,512,128]{3,2,1,0:T(8,128)(2,1)} %collective-permute-done.11.refs_2_), channel_id=1, source_target_pairs={{0,4},{2,6},{4,0},{6,2},{8,12},{10,14},{12,8},{14,10},{16,20},{18,... | collective-permute-start | bytes 1572872 | tf_op jit(solution)/shard_map/ppermute | solution.py:218
  56.9 8.8 %shard_map.56 = (f32[2,512,128]{2,1,0:T(8,128)}, f32[2,8,512]{2,1,0:T(8,128)}, s16[2,544,128]{2,1,0:T(8,128)(2,1)}) custom-call(bf16[2048,128]{1,0:T(8,128)(2,1)} %pad.9.bias_ref, bf16[6,512,128]{2,1,0:T(8,128)(2,1)} %pad_maximum_fusion.own_q_ref, bf16[2,512,128]{2,1,0:T(8,128)(2,1)} %collective-permute-done.5.far_q_ref, bf16[2,4,512,128]{3,2,1,0:T(8,128)(2,1)} %copy-done.6, ...), custom_call_target="tpu_custom_call" | custom-call | flops 4294967296 | bytes 3407872 | tf_op jit(solution)/shard_map/pallas_call | solution.py:128
  66.0 6.7 %collective-permute-done.12.refs_2_ = bf16[2,2,512,128]{3,2,1,0:T(8,128)(2,1)S(1)} collective-permute-done((bf16[2,2,512,128]{3,2,1,0:T(8,128)(2,1)S(1)}, bf16[2,2,512,128]{3,2,1,0:T(8,128)(2,1)S(1)}, u32[]{:S(2)}, u32[]{:S(2)}) %collective-permute-start.12) | collective-permute-done | bytes 524320 | tf_op jit(solution)/shard_map/ppermute | solution.py:218
  72.8 0.8 collective-permute-start.18
  73.7 9.6 %collective-permute-done.10.far_q_ref = bf16[4,512,128]{2,1,0:T(8,128)(2,1)} collective-permute-done((bf16[4,512,128]{2,1,0:T(8,128)(2,1)}, bf16[4,512,128]{2,1,0:T(8,128)(2,1)}, u32[]{:S(2)}, u32[]{:S(2)}) %collective-permute-start.10) | collective-permute-done | bytes 524320 | tf_op jit(solution)/shard_map/ppermute | solution.py:218
  83.3 0.8 copy-done.18
  84.1 9.0 %shard_map.57 = (f32[2,512,128]{2,1,0:T(8,128)}, f32[2,8,512]{2,1,0:T(8,128)}, s16[2,544,128]{2,1,0:T(8,128)(2,1)}) custom-call(bf16[2048,128]{1,0:T(8,128)(2,1)} %pad.9.bias_ref, bf16[6,512,128]{2,1,0:T(8,128)(2,1)} %pad_maximum_fusion.own_q_ref, bf16[4,512,128]{2,1,0:T(8,128)(2,1)} %collective-permute-done.10.far_q_ref, ...), custom_call_target="tpu_custom_call" | custom-call | flops 4294967296 | bytes 3407872 | tf_op jit(solution)/shard_map/pallas_call | solution.py:128
  94.0 5.9 %shard_map.61 = (f32[1,512,128]{2,1,0:T(8,128)}, f32[1,8,512]{2,1,0:T(8,128)}, s16[1,544,128]{2,1,0:T(8,128)(2,1)}) custom-call(bf16[2048,128]{1,0:T(8,128)(2,1)} %pad.9.bias_ref, bf16[6,512,128]{2,1,0:T(8,128)(2,1)} %pad_maximum_fusion.own_q_ref, bf16[4,512,128]{2,1,0:T(8,128)(2,1)} %collective-permute-done.10.far_q_ref, ...), custom_call_target="tpu_custom_call" | custom-call | flops 2147483648 | bytes 1703936 | tf_op jit(solution)/shard_map/pallas_call | solution.py:128
  100.0 2.9 %collective-permute-start.19 = (s16[1,544,128]{2,1,0:T(8,128)(2,1)}, s16[1,544,128]{2,1,0:T(8,128)(2,1)S(1)}, u32[]{:S(2)}, u32[]{:S(2)}) collective-permute-start(s16[1,544,128]{2,1,0:T(8,128)(2,1)} %get-tuple-element.91), channel_id=1, source_target_pairs={{0,16},{2,18},{4,20},{6,22},{8,24},{10,26},{12,28},{14,30},{16,0},... | collective-permute-start | bytes 417800 | tf_op jit(solution)/shard_map/ppermute | solution.py:218
  103.6 6.2 %shard_map.58 = (f32[1,512,128]{2,1,0:T(8,128)}, f32[1,8,512]{2,1,0:T(8,128)}, s16[1,544,128]{2,1,0:T(8,128)(2,1)}) custom-call(bf16[2048,128]{1,0:T(8,128)(2,1)} %pad.9.bias_ref, bf16[6,512,128]{2,1,0:T(8,128)(2,1)} %pad_maximum_fusion.own_q_ref, bf16[4,512,128]{2,1,0:T(8,128)(2,1)} %collective-permute-done.10.far_q_ref, ...), custom_call_target="tpu_custom_call" | custom-call | flops 2147483648 | bytes 1703936 | tf_op jit(solution)/shard_map/pallas_call | solution.py:128
  109.8 0.8 shard_map.59
  112.7 8.2 %collective-permute-done.20 = s16[1,544,128]{2,1,0:T(8,128)(2,1)S(1)} collective-permute-done((s16[1,544,128]{2,1,0:T(8,128)(2,1)}, s16[1,544,128]{2,1,0:T(8,128)(2,1)S(1)}, u32[]{:S(2)}, u32[]{:S(2)}) %collective-permute-start.20) | collective-permute-done | bytes 139296 | tf_op jit(solution)/shard_map/ppermute | solution.py:218
  122.0 0.9 collective-permute-done.23
  123.0 0.9 pad_maximum_fusion.2
  (123 shorter events, 10.2 us)
Async XLA Ops:
  3.1 6.8 %collective-permute-start = (bf16[13,5,256]{2,1,0:T(8,128)(2,1)S(1)}, bf16[13,5,256]{2,1,0:T(8,128)(2,1)S(1)}, u32[]{:S(2)}, u32[]{:S(2)}) collective-permute-start(bf16[13,5,256]{2,1,0:T(8,128)(2,1)S(1)} %pad_maximum_fusion.5), channel_id=1, source_target_pairs={{0,16},{2,18},{4,20},{6,22},{8,24},{10,26},{12,28},{14,30},{16,0},... | collective-permute-start | bytes 99848 | tf_op jit(solution)/shard_map/ppermute | solution.py:218
  7.4 6.4 %collective-permute-start.2 = (bf16[2,6,256,128]{3,2,1,0:T(8,128)(2,1)S(1)}, bf16[2,6,256,128]{3,2,1,0:T(8,128)(2,1)S(1)}, u32[]{:S(2)}, u32[]{:S(2)}) collective-permute-start(bf16[2,6,256,128]{3,2,1,0:T(8,128)(2,1)S(1)} %pad_maximum_fusion.1), channel_id=1, source_target_pairs={{0,2},{2,0},{4,6},{6,4},{8,10},{10,8},{12,14},{14,12},{16,18},{18,... | collective-permute-start | bytes 2359304 | tf_op jit(solution)/shard_map/ppermute | solution.py:218
  10.0 1.3 %collective-permute-start.1 = (bf16[7,10,256]{2,1,0:T(8,128)(2,1)S(1)}, bf16[7,10,256]{2,1,0:T(8,128)(2,1)S(1)}, u32[]{:S(2)}, u32[]{:S(2)}) collective-permute-start(bf16[7,10,256]{2,1,0:T(8,128)(2,1)S(1)} %pad_maximum_fusion.4), channel_id=1, source_target_pairs={{0,2},{2,0},{4,6},{6,4},{8,10},{10,8},{12,14},{14,12},{16,18},{18,... | collective-permute-start | bytes 107528 | tf_op jit(solution)/shard_map/ppermute | solution.py:218
  11.4 20.3 %collective-permute-start.15 = (bf16[6,16,256]{2,1,0:T(8,128)(2,1)S(1)}, bf16[6,16,256]{2,1,0:T(8,128)(2,1)S(1)}, u32[]{:S(2)}, u32[]{:S(2)}) collective-permute-start(bf16[6,16,256]{2,1,0:T(8,128)(2,1)S(1)} %pad_maximum_fusion.6), channel_id=1, source_target_pairs={{0,4},{2,6},{4,0},{6,2},{8,12},{10,14},{12,8},{14,10},{16,20},{18,... | collective-permute-start | bytes 147464 | tf_op jit(solution)/shard_map/ppermute | solution.py:218
  15.6 13.8 %copy-start.7 = (bf16[2,2,512,128]{3,2,1,0:T(8,128)(2,1)}, bf16[2,2,512,128]{3,2,1,0:T(8,128)(2,1)S(1)}, u32[]{:S(2)}) copy-start(bf16[2,2,512,128]{3,2,1,0:T(8,128)(2,1)S(1)} %get-tuple-element.69.refs_0_) | copy-start | bytes 1572868
  15.6 15.2 %copy-start.6 = (bf16[2,4,512,128]{3,2,1,0:T(8,128)(2,1)}, bf16[2,4,512,128]{3,2,1,0:T(8,128)(2,1)S(1)}, u32[]{:S(2)}) copy-start(bf16[2,4,512,128]{3,2,1,0:T(8,128)(2,1)S(1)} %get-tuple-element.64.refs_0_) | copy-start | bytes 3145732
  15.6 13.8 %collective-permute-start.4 = (bf16[2,2,512,128]{3,2,1,0:T(8,128)(2,1)S(1)}, bf16[2,2,512,128]{3,2,1,0:T(8,128)(2,1)}, u32[]{:S(2)}, u32[]{:S(2)}) collective-permute-start(bf16[2,2,512,128]{3,2,1,0:T(8,128)(2,1)S(1)} %get-tuple-element.62), channel_id=1, source_target_pairs={{0,8},{2,10},{4,12},{6,14},{8,0},{10,2},{12,4},{14,6},{16,24},{18,... | collective-permute-start | bytes 1572872 | tf_op jit(solution)/shard_map/ppermute | solution.py:218
  16.8 17.4 %collective-permute-start.3 = (bf16[6,256,128]{2,1,0:T(8,128)(2,1)S(1)}, bf16[6,256,128]{2,1,0:T(8,128)(2,1)S(1)}, u32[]{:S(2)}, u32[]{:S(2)}) collective-permute-start(bf16[6,256,128]{2,1,0:T(8,128)(2,1)S(1)} %get-tuple-element.112), channel_id=1, source_target_pairs={{0,2},{2,0},{4,6},{6,4},{8,10},{10,8},{12,14},{14,12},{16,18},{18,... | collective-permute-start | bytes 1179656 | tf_op jit(solution)/shard_map/ppermute | solution.py:218
  16.8 38.0 %collective-permute-start.6 = (bf16[2,4,512,128]{3,2,1,0:T(8,128)(2,1)S(1)}, bf16[2,4,512,128]{3,2,1,0:T(8,128)(2,1)}, u32[]{:S(2)}, u32[]{:S(2)}) collective-permute-start(bf16[2,4,512,128]{3,2,1,0:T(8,128)(2,1)S(1)} %get-tuple-element.64.refs_0_), channel_id=1, source_target_pairs={{0,4},{2,6},{4,0},{6,2},{8,12},{10,14},{12,8},{14,10},{16,20},{18,... | collective-permute-start | bytes 3145736 | tf_op jit(solution)/shard_map/ppermute | solution.py:218
  29.4 20.8 %collective-permute-start.11 = (bf16[2,2,512,128]{3,2,1,0:T(8,128)(2,1)}, bf16[2,2,512,128]{3,2,1,0:T(8,128)(2,1)}, u32[]{:S(2)}, u32[]{:S(2)}) collective-permute-start(bf16[2,2,512,128]{3,2,1,0:T(8,128)(2,1)} %get-tuple-element.75), channel_id=1, source_target_pairs={{0,8},{2,10},{4,12},{6,14},{8,0},{10,2},{12,4},{14,6},{16,24},{18,... | collective-permute-start | bytes 1572872 | tf_op jit(solution)/shard_map/ppermute | solution.py:218
  33.6 23.3 %collective-permute-start.7 = (bf16[2,2,512,128]{3,2,1,0:T(8,128)(2,1)}, bf16[2,2,512,128]{3,2,1,0:T(8,128)(2,1)}, u32[]{:S(2)}, u32[]{:S(2)}) collective-permute-start(bf16[2,2,512,128]{3,2,1,0:T(8,128)(2,1)} %collective-permute-done.4.refs_2_), channel_id=1, source_target_pairs={{0,4},{2,6},{4,0},{6,2},{8,12},{10,14},{12,8},{14,10},{16,20},{18,... | collective-permute-start | bytes 1572872 | tf_op jit(solution)/shard_map/ppermute | solution.py:218
  35.9 14.4 %copy-start.10 = (bf16[2,2,512,128]{3,2,1,0:T(8,128)(2,1)S(1)}, bf16[2,2,512,128]{3,2,1,0:T(8,128)(2,1)}, u32[]{:S(2)}) copy-start(bf16[2,2,512,128]{3,2,1,0:T(8,128)(2,1)} %copy-done.9) | copy-start | bytes 1572868
  35.9 19.0 %copy-start.8 = (bf16[2,2,512,128]{3,2,1,0:T(8,128)(2,1)S(1)}, bf16[2,2,512,128]{3,2,1,0:T(8,128)(2,1)}, u32[]{:S(2)}) copy-start(bf16[2,2,512,128]{3,2,1,0:T(8,128)(2,1)} %copy-done.7) | copy-start | bytes 1572868
  35.9 14.3 %collective-permute-start.16 = (bf16[6,32,256]{2,1,0:T(8,128)(2,1)}, bf16[6,32,256]{2,1,0:T(8,128)(2,1)S(1)}, u32[]{:S(2)}, u32[]{:S(2)}) collective-permute-start(bf16[6,32,256]{2,1,0:T(8,128)(2,1)} %concatenate.60), channel_id=1, source_target_pairs={{0,8},{2,10},{4,12},{6,14},{8,0},{10,2},{12,4},{14,6},{16,24},{18,... | collective-permute-start | bytes 294920 | tf_op jit(solution)/shard_map/ppermute | solution.py:218
  36.6 14.0 %collective-permute-start.5 = (bf16[2,512,128]{2,1,0:T(8,128)(2,1)S(1)}, bf16[2,512,128]{2,1,0:T(8,128)(2,1)}, u32[]{:S(2)}, u32[]{:S(2)}) collective-permute-start(bf16[2,512,128]{2,1,0:T(8,128)(2,1)S(1)} %fusion.1), channel_id=1, source_target_pairs={{0,16},{2,18},{4,20},{6,22},{8,24},{10,26},{12,28},{14,30},{16,0},... | collective-permute-start | bytes 786440 | tf_op jit(solution)/shard_map/ppermute | solution.py:218
  50.3 22.5 %collective-permute-start.12 = (bf16[2,2,512,128]{3,2,1,0:T(8,128)(2,1)S(1)}, bf16[2,2,512,128]{3,2,1,0:T(8,128)(2,1)S(1)}, u32[]{:S(2)}, u32[]{:S(2)}) collective-permute-start(bf16[2,2,512,128]{3,2,1,0:T(8,128)(2,1)S(1)} %copy-done.10), channel_id=1, source_target_pairs={{0,8},{2,10},{4,12},{6,14},{8,0},{10,2},{12,4},{14,6},{16,24},{18,... | collective-permute-start | bytes 1572872 | tf_op jit(solution)/shard_map/ppermute | solution.py:218
  50.6 32.6 %collective-permute-start.10 = (bf16[4,512,128]{2,1,0:T(8,128)(2,1)}, bf16[4,512,128]{2,1,0:T(8,128)(2,1)}, u32[]{:S(2)}, u32[]{:S(2)}) collective-permute-start(bf16[4,512,128]{2,1,0:T(8,128)(2,1)} %fusion), channel_id=1, source_target_pairs={{0,16},{2,18},{4,20},{6,22},{8,24},{10,26},{12,28},{14,30},{16,0},... | collective-permute-start | bytes 1572872 | tf_op jit(solution)/shard_map/ppermute | solution.py:218
  54.9 18.8 %collective-permute-start.9 = (bf16[2,2,512,128]{3,2,1,0:T(8,128)(2,1)S(1)}, bf16[2,2,512,128]{3,2,1,0:T(8,128)(2,1)S(1)}, u32[]{:S(2)}, u32[]{:S(2)}) collective-permute-start(bf16[2,2,512,128]{3,2,1,0:T(8,128)(2,1)S(1)} %copy-done.8), channel_id=1, source_target_pairs={{0,4},{2,6},{4,0},{6,2},{8,12},{10,14},{12,8},{14,10},{16,20},{18,... | collective-permute-start | bytes 1572872 | tf_op jit(solution)/shard_map/ppermute | solution.py:218
  54.9 28.4 %collective-permute-start.13 = (bf16[2,2,512,128]{3,2,1,0:T(8,128)(2,1)}, bf16[2,2,512,128]{3,2,1,0:T(8,128)(2,1)S(1)}, u32[]{:S(2)}, u32[]{:S(2)}) collective-permute-start(bf16[2,2,512,128]{3,2,1,0:T(8,128)(2,1)} %collective-permute-done.11.refs_2_), channel_id=1, source_target_pairs={{0,4},{2,6},{4,0},{6,2},{8,12},{10,14},{12,8},{14,10},{16,20},{18,... | collective-permute-start | bytes 1572872 | tf_op jit(solution)/shard_map/ppermute | solution.py:218
  65.7 27.6 %collective-permute-start.8 = (s16[2,544,128]{2,1,0:T(8,128)(2,1)}, s16[2,544,128]{2,1,0:T(8,128)(2,1)S(1)}, u32[]{:S(2)}, u32[]{:S(2)}) collective-permute-start(s16[2,544,128]{2,1,0:T(8,128)(2,1)} %get-tuple-element.67), channel_id=1, source_target_pairs={{0,16},{2,18},{4,20},{6,22},{8,24},{10,26},{12,28},{14,30},{16,0},... | collective-permute-start | bytes 835592 | tf_op jit(solution)/shard_map/ppermute | solution.py:218
  72.8 20.3 %copy-start.12 = (bf16[2,2,512,128]{3,2,1,0:T(8,128)(2,1)}, bf16[2,2,512,128]{3,2,1,0:T(8,128)(2,1)S(1)}, u32[]{:S(2)}) copy-start(bf16[2,2,512,128]{3,2,1,0:T(8,128)(2,1)S(1)} %collective-permute-done.12.refs_2_) | copy-start | bytes 1572868
  72.8 20.5 %collective-permute-start.18 = (bf16[2,1,512,128]{3,2,1,0:T(8,128)(2,1)S(1)}, bf16[2,1,512,128]{3,2,1,0:T(8,128)(2,1)S(1)}, u32[]{:S(2)}, u32[]{:S(2)}) collective-permute-start(bf16[2,1,512,128]{3,2,1,0:T(8,128)(2,1)S(1)} %get-tuple-element.88), channel_id=1, source_target_pairs={{0,4},{2,6},{4,0},{6,2},{8,12},{10,14},{12,8},{14,10},{16,20},{18,... | collective-permute-start | bytes 786440 | tf_op jit(solution)/shard_map/ppermute | solution.py:218
  73.7 19.4 %copy-start.17 = (bf16[2,2,512,128]{3,2,1,0:T(8,128)(2,1)}, bf16[2,2,512,128]{3,2,1,0:T(8,128)(2,1)S(1)}, u32[]{:S(2)}) copy-start(bf16[2,2,512,128]{3,2,1,0:T(8,128)(2,1)S(1)} %collective-permute-done.9.refs_1_) | copy-start | bytes 1572868
  93.0 9.9 %collective-permute-start.14 = (bf16[2,1,512,128]{3,2,1,0:T(8,128)(2,1)S(1)}, bf16[2,1,512,128]{3,2,1,0:T(8,128)(2,1)S(1)}, u32[]{:S(2)}, u32[]{:S(2)}) collective-permute-start(bf16[2,1,512,128]{3,2,1,0:T(8,128)(2,1)S(1)} %get-tuple-element.78), channel_id=1, source_target_pairs={{0,4},{2,6},{4,0},{6,2},{8,12},{10,14},{12,8},{14,10},{16,20},{18,... | collective-permute-start | bytes 786440 | tf_op jit(solution)/shard_map/ppermute | solution.py:218
  93.2 17.6 %collective-permute-start.17 = (s16[2,544,128]{2,1,0:T(8,128)(2,1)}, s16[2,544,128]{2,1,0:T(8,128)(2,1)S(1)}, u32[]{:S(2)}, u32[]{:S(2)}) collective-permute-start(s16[2,544,128]{2,1,0:T(8,128)(2,1)} %get-tuple-element.85), channel_id=1, source_target_pairs={{0,16},{2,18},{4,20},{6,22},{8,24},{10,26},{12,28},{14,30},{16,0},... | collective-permute-start | bytes 835592 | tf_op jit(solution)/shard_map/ppermute | solution.py:218
  100.0 12.2 %collective-permute-start.19 = (s16[1,544,128]{2,1,0:T(8,128)(2,1)}, s16[1,544,128]{2,1,0:T(8,128)(2,1)S(1)}, u32[]{:S(2)}, u32[]{:S(2)}) collective-permute-start(s16[1,544,128]{2,1,0:T(8,128)(2,1)} %get-tuple-element.91), channel_id=1, source_target_pairs={{0,16},{2,18},{4,20},{6,22},{8,24},{10,26},{12,28},{14,30},{16,0},... | collective-permute-start | bytes 417800 | tf_op jit(solution)/shard_map/ppermute | solution.py:218
  110.6 1.5 %collective-permute-start.21 = (bf16[2,256,128]{2,1,0:T(8,128)(2,1)S(1)}, bf16[2,256,128]{2,1,0:T(8,128)(2,1)S(1)}, u32[]{:S(2)}, u32[]{:S(2)}) collective-permute-start(bf16[2,256,128]{2,1,0:T(8,128)(2,1)S(1)} %get-tuple-element.97), channel_id=1, source_target_pairs={{0,2},{2,0},{4,6},{6,4},{8,10},{10,8},{12,14},{14,12},{16,18},{18,... | collective-permute-start | bytes 393224 | tf_op jit(solution)/shard_map/ppermute | solution.py:218
  110.7 10.2 %collective-permute-start.20 = (s16[1,544,128]{2,1,0:T(8,128)(2,1)}, s16[1,544,128]{2,1,0:T(8,128)(2,1)S(1)}, u32[]{:S(2)}, u32[]{:S(2)}) collective-permute-start(s16[1,544,128]{2,1,0:T(8,128)(2,1)} %get-tuple-element.95), channel_id=1, source_target_pairs={{0,16},{2,18},{4,20},{6,22},{8,24},{10,26},{12,28},{14,30},{16,0},... | collective-permute-start | bytes 417800 | tf_op jit(solution)/shard_map/ppermute | solution.py:218
  110.8 10.1 %copy-start.13 = (f32[1,512,128]{2,1,0:T(8,128)S(1)}, f32[1,512,128]{2,1,0:T(8,128)}, u32[]{:S(2)}) copy-start(f32[1,512,128]{2,1,0:T(8,128)} %get-tuple-element.79) | copy-start | bytes 786436
  111.6 10.4 %collective-permute-start.22 = (bf16[2,256,128]{2,1,0:T(8,128)(2,1)S(1)}, bf16[2,256,128]{2,1,0:T(8,128)(2,1)S(1)}, u32[]{:S(2)}, u32[]{:S(2)}) collective-permute-start(bf16[2,256,128]{2,1,0:T(8,128)(2,1)S(1)} %get-tuple-element.98), channel_id=1, source_target_pairs={{0,2},{2,0},{4,6},{6,4},{8,10},{10,8},{12,14},{14,12},{16,18},{18,... | collective-permute-start | bytes 393224 | tf_op jit(solution)/shard_map/ppermute | solution.py:218
  121.4 1.5 %collective-permute-start.24 = (bf16[1,256,128]{2,1,0:T(8,128)(2,1)S(1)}, bf16[1,256,128]{2,1,0:T(8,128)(2,1)S(1)}, u32[]{:S(2)}, u32[]{:S(2)}) collective-permute-start(bf16[1,256,128]{2,1,0:T(8,128)(2,1)S(1)} %get-tuple-element.108), channel_id=1, source_target_pairs={{0,2},{2,0},{4,6},{6,4},{8,10},{10,8},{12,14},{14,12},{16,18},{18,... | collective-permute-start | bytes 196616 | tf_op jit(solution)/shard_map/ppermute | solution.py:218
  121.5 1.4 %collective-permute-start.23 = (bf16[1,256,128]{2,1,0:T(8,128)(2,1)S(1)}, bf16[1,256,128]{2,1,0:T(8,128)(2,1)S(1)}, u32[]{:S(2)}, u32[]{:S(2)}) collective-permute-start(bf16[1,256,128]{2,1,0:T(8,128)(2,1)S(1)} %get-tuple-element.104), channel_id=1, source_target_pairs={{0,2},{2,0},{4,6},{6,4},{8,10},{10,8},{12,14},{14,12},{16,18},{18,... | collective-permute-start | bytes 196616 | tf_op jit(solution)/shard_map/ppermute | solution.py:218
  (14 other events, 51.0 us)

commit v3 on v2

--- a/solution.py
+++ b/solution.py
@@ -133,7 +133,7 @@
         out_specs=[whole(out) for out in outs],
         out_shape=outs,
         scratch_shapes=[pltpu.VMEM((rows, len(blocks) * span), jnp.float32)] * 4,
-        compiler_params=pltpu.CompilerParams(vmem_limit_bytes=60 * 1024 * 1024),
+        compiler_params=pltpu.CompilerParams(vmem_limit_bytes=(38 if len(blocks) < 8 else 60) * 1024 * 1024),
         cost_estimate=pl.CostEstimate(
             flops=work * width * 8,
             bytes_accessed=heads * rows * width * 2 * (2 * len(blocks) + 5),
@@ -297,7 +297,6 @@
     for low, high in to_far:
         got = swap(after(queries[starts[low] : starts[high]], *wait), half)
         far_q += [(starts[part] - starts[low], got) for part in range(low, high)]
-        wait = [got]
     for bit in hops:
         other = swap(after(pooled, *pooled_wait), bit)
         pooled = jnp.concatenate([pooled, other], axis=1)

time: 124 us -> 117 us (0.944)
  Pallas kernels: 32.4 us -> 27.9 us
  waiting for transfers between devices: 51.5 us -> 49.2 us
  other arithmetic: 7.16 us -> 9.06 us
  starting transfers between devices: 24.6 us -> 22.8 us
    pallas_call x4, Pallas kernels: 29.9 us -> 25.3 us  [attend(): pl.pallas_call(functools.partial(attend_kernel, len(blocks), factor), gri...]
    ppermute x25, waiting for transfers between devices: 51.5 us -> 49.2 us  [swap(): return lax.ppermute(array, 'ctx', [(i, i ^ bit) for i in range(ring)])]
    ppermute x25, starting transfers between devices: 24.6 us -> 22.8 us  [swap(): return lax.ppermute(array, 'ctx', [(i, i ^ bit) for i in range(ring)])]
    unnamed x47 -> x33, local copies, waits for them, and re-layouts: 3.16 us -> 2.36 us
  transfers between devices with their start and end apart: 25 -> 25, of which waited for: 8 -> 11; matrix products, arithmetic and copies ran while one was open for 6% -> 8% of each run, Pallas kernels for 26% -> 24%
where the time goes in v3:
time: 117 us; the launch traced here: 116 us
  waiting for transfers between devices  49.2 us (42%)
  Pallas kernels  27.9 us (24%)
  starting transfers between devices  22.8 us (19%)
  other arithmetic  9.06 us (8%)
  local copies, waits for them, and re-layouts  6.49 us (6%)
    ppermute x25, waiting for transfers between devices, swap(): return lax.ppermute(array, 'ctx', [(i, i ^ bit) for i in range(ring)])  49.2 us
    pallas_call x4, Pallas kernels, attend(): pl.pallas_call(functools.partial(attend_kernel, len(blocks), factor), gri...  25.3 us
    ppermute x25, starting transfers between devices, swap(): return lax.ppermute(array, 'ctx', [(i, i ^ bit) for i in range(ring)])  22.8 us
    reduce_sum x3, other arithmetic, pool_cubes(): jnp.sum(field.reshape(heads, tokens // CUBE, CUBE, width), axis=2, dtype=...  2.69 us
    concatenate x3, other arithmetic, body(): jnp.concatenate([cut(queries, mine), swap(cut(queries, theirs), 1)], axis=1)  2.69 us
    unnamed x33, local copies, waits for them, and re-layouts  2.36 us
  transfers between devices with their start and end apart: 25, of which 11 were waited for; matrix products, arithmetic and copies ran while one was open for 8% of the time, Pallas kernels for 24%

profile of v3, /device:TPU:0, one launch (start us, length us, event | category | flops | bytes accessed | tf_op | source)
XLA Modules:
  0.0 116.4 jit_solution(14911857105922755960)
XLA Ops:
  1.5 1.3 %convert_reduce_fusion.2 = f32[12,4,128]{2,1,0:T(4,128)S(1)} fusion(bf16[12,256,128]{2,1,0:T(8,128)(2,1)} %keys_ref.1), kind=kLoop, calls=%fused_computation.3 | loop fusion | flops 780288 | bytes 811008 | tf_op jit(solution)/shard_map/reduce_sum | solution.py:19
  3.1 4.1 %collective-permute-start = (bf16[13,5,256]{2,1,0:T(8,128)(2,1)S(1)}, bf16[13,5,256]{2,1,0:T(8,128)(2,1)S(1)}, u32[]{:S(2)}, u32[]{:S(2)}) collective-permute-start(bf16[13,5,256]{2,1,0:T(8,128)(2,1)S(1)} %pad_maximum_fusion.5), channel_id=1, source_target_pairs={{0,16},{2,18},{4,20},{6,22},{8,24},{10,26},{12,28},{14,30},{16,0},... | collective-permute-start | bytes 99848 | tf_op jit(solution)/shard_map/ppermute | solution.py:218
  7.6 2.3 %collective-permute-done = bf16[13,5,256]{2,1,0:T(8,128)(2,1)S(1)} collective-permute-done((bf16[13,5,256]{2,1,0:T(8,128)(2,1)S(1)}, bf16[13,5,256]{2,1,0:T(8,128)(2,1)S(1)}, u32[]{:S(2)}, u32[]{:S(2)}) %collective-permute-start) | collective-permute-done | bytes 33312 | tf_op jit(solution)/shard_map/ppermute | solution.py:218
  10.2 1.2 collective-permute-done.1
  11.4 1.8 %collective-permute-start.15 = (bf16[6,16,256]{2,1,0:T(8,128)(2,1)S(1)}, bf16[6,16,256]{2,1,0:T(8,128)(2,1)S(1)}, u32[]{:S(2)}, u32[]{:S(2)}) collective-permute-start(bf16[6,16,256]{2,1,0:T(8,128)(2,1)S(1)} %pad_maximum_fusion.6), channel_id=1, source_target_pairs={{0,4},{2,6},{4,0},{6,2},{8,12},{10,14},{12,8},{14,10},{16,20},{18,... | collective-permute-start | bytes 147464 | tf_op jit(solution)/shard_map/ppermute | solution.py:218
  13.8 1.0 shard_map.55
  14.8 1.1 collective-permute-start.4
  16.6 12.0 %collective-permute-done.4.refs_2_ = bf16[2,2,512,128]{3,2,1,0:T(8,128)(2,1)} collective-permute-done((bf16[2,2,512,128]{3,2,1,0:T(8,128)(2,1)S(1)}, bf16[2,2,512,128]{3,2,1,0:T(8,128)(2,1)}, u32[]{:S(2)}, u32[]{:S(2)}) %collective-permute-start.4) | collective-permute-done | bytes 524320 | tf_op jit(solution)/shard_map/ppermute | solution.py:218
  28.6 1.1 collective-permute-start.11
  29.8 1.0 copy.12
  30.8 1.1 pad.9.bias_ref
  34.1 1.1 pad_maximum_fusion.own_q_ref
  36.8 2.6 %collective-permute-start.5 = (bf16[2,512,128]{2,1,0:T(8,128)(2,1)}, bf16[2,512,128]{2,1,0:T(8,128)(2,1)S(1)}, u32[]{:S(2)}, u32[]{:S(2)}) collective-permute-start(bf16[2,512,128]{2,1,0:T(8,128)(2,1)} %fusion.1), channel_id=1, source_target_pairs={{0,16},{2,18},{4,20},{6,22},{8,24},{10,26},{12,28},{14,30},{16,0},... | collective-permute-start | bytes 786440 | tf_op jit(solution)/shard_map/ppermute | solution.py:218
  39.4 1.2 %convert_reduce_fusion = f32[6,8,128]{2,1,0:T(8,128)S(1)} fusion(bf16[6,256,128]{2,1,0:T(8,128)(2,1)S(1)} %copy-done.9, bf16[6,256,128]{2,1,0:T(8,128)(2,1)} %copy-done.7), kind=kLoop, calls=%fused_computation.1 | loop fusion | flops 2353152 | bytes 811008 | tf_op jit(solution)/shard_map/reduce_sum | solution.py:19
  40.6 8.8 %collective-permute-done.16 = bf16[6,32,256]{2,1,0:T(8,128)(2,1)S(1)} collective-permute-done((bf16[6,32,256]{2,1,0:T(8,128)(2,1)S(1)}, bf16[6,32,256]{2,1,0:T(8,128)(2,1)S(1)}, u32[]{:S(2)}, u32[]{:S(2)}) %collective-permute-start.16) | collective-permute-done | bytes 98336 | tf_op jit(solution)/shard_map/ppermute | solution.py:218
  50.4 1.0 concatenate.61
  51.3 0.8 copy-done.5
  52.2 2.5 %collective-permute-start.12 = (bf16[2,2,512,128]{3,2,1,0:T(8,128)(2,1)}, bf16[2,2,512,128]{3,2,1,0:T(8,128)(2,1)S(1)}, u32[]{:S(2)}, u32[]{:S(2)}) collective-permute-start(bf16[2,2,512,128]{3,2,1,0:T(8,128)(2,1)} %copy-done.4), channel_id=1, source_target_pairs={{0,8},{2,10},{4,12},{6,14},{8,0},{10,2},{12,4},{14,6},{16,24},{18,... | collective-permute-start | bytes 1572872 | tf_op jit(solution)/shard_map/ppermute | solution.py:218
  55.1 2.0 %collective-permute-start.13 = (bf16[2,2,512,128]{3,2,1,0:T(8,128)(2,1)}, bf16[2,2,512,128]{3,2,1,0:T(8,128)(2,1)S(1)}, u32[]{:S(2)}, u32[]{:S(2)}) collective-permute-start(bf16[2,2,512,128]{3,2,1,0:T(8,128)(2,1)} %copy-done.5), channel_id=1, source_target_pairs={{0,4},{2,6},{4,0},{6,2},{8,12},{10,14},{12,8},{14,10},{16,20},{18,... | collective-permute-start | bytes 1572872 | tf_op jit(solution)/shard_map/ppermute | solution.py:218
  57.1 7.8 %shard_map.56 = (f32[2,512,128]{2,1,0:T(8,128)S(1)}, f32[2,8,512]{2,1,0:T(8,128)S(1)}, s16[2,544,128]{2,1,0:T(8,128)(2,1)S(1)}) custom-call(bf16[2048,128]{1,0:T(8,128)(2,1)S(1)} %pad.9.bias_ref, bf16[6,512,128]{2,1,0:T(8,128)(2,1)S(1)} %pad_maximum_fusion.own_q_ref, bf16[2,512,128]{2,1,0:T(8,128)(2,1)S(1)} %collective-permute-done.5.far_q_ref, ...), custom_call_target="tpu_custom_call" | custom-call | flops 4294967296 | bytes 3407872 | tf_op jit(solution)/shard_map/pallas_call | solution.py:128
  65.0 10.4 %collective-permute-done.12.refs_2_ = bf16[2,2,512,128]{3,2,1,0:T(8,128)(2,1)S(1)} collective-permute-done((bf16[2,2,512,128]{3,2,1,0:T(8,128)(2,1)}, bf16[2,2,512,128]{3,2,1,0:T(8,128)(2,1)S(1)}, u32[]{:S(2)}, u32[]{:S(2)}) %collective-permute-start.12) | collective-permute-done | bytes 524320 | tf_op jit(solution)/shard_map/ppermute | solution.py:218
  75.6 1.2 collective-permute-done.10.far_q_ref
  76.8 4.0 %collective-permute-done.13.refs_3_ = bf16[2,2,512,128]{3,2,1,0:T(8,128)(2,1)S(1)} collective-permute-done((bf16[2,2,512,128]{3,2,1,0:T(8,128)(2,1)}, bf16[2,2,512,128]{3,2,1,0:T(8,128)(2,1)S(1)}, u32[]{:S(2)}, u32[]{:S(2)}) %collective-permute-start.13) | collective-permute-done | bytes 524320 | tf_op jit(solution)/shard_map/ppermute | solution.py:218
  80.8 7.7 %shard_map.57 = (f32[2,512,128]{2,1,0:T(8,128)S(1)}, f32[2,8,512]{2,1,0:T(8,128)S(1)}, s16[2,544,128]{2,1,0:T(8,128)(2,1)S(1)}) custom-call(bf16[2048,128]{1,0:T(8,128)(2,1)S(1)} %pad.9.bias_ref, bf16[6,512,128]{2,1,0:T(8,128)(2,1)S(1)} %pad_maximum_fusion.own_q_ref, bf16[4,512,128]{2,1,0:T(8,128)(2,1)} %collective-permute-done.10.far_q_ref, ...), custom_call_target="tpu_custom_call" | custom-call | flops 4294967296 | bytes 3407872 | tf_op jit(solution)/shard_map/pallas_call | solution.py:128
  89.7 4.8 %shard_map.61 = (f32[1,512,128]{2,1,0:T(8,128)S(1)}, f32[1,8,512]{2,1,0:T(8,128)S(1)}, s16[1,544,128]{2,1,0:T(8,128)(2,1)S(1)}) custom-call(bf16[2048,128]{1,0:T(8,128)(2,1)S(1)} %pad.9.bias_ref, bf16[6,512,128]{2,1,0:T(8,128)(2,1)S(1)} %pad_maximum_fusion.own_q_ref, bf16[4,512,128]{2,1,0:T(8,128)(2,1)} %collective-permute-done.10.far_q_ref, ...), custom_call_target="tpu_custom_call" | custom-call | flops 2147483648 | bytes 1703936 | tf_op jit(solution)/shard_map/pallas_call | solution.py:128
  94.5 2.3 %collective-permute-start.19 = (s16[1,544,128]{2,1,0:T(8,128)(2,1)S(1)}, s16[1,544,128]{2,1,0:T(8,128)(2,1)S(1)}, u32[]{:S(2)}, u32[]{:S(2)}) collective-permute-start(s16[1,544,128]{2,1,0:T(8,128)(2,1)S(1)} %get-tuple-element.91), channel_id=1, source_target_pairs={{0,16},{2,18},{4,20},{6,22},{8,24},{10,26},{12,28},{14,30},{16,0},... | collective-permute-start | bytes 417800 | tf_op jit(solution)/shard_map/ppermute | solution.py:218
  96.8 5.0 %shard_map.58 = (f32[1,512,128]{2,1,0:T(8,128)S(1)}, f32[1,8,512]{2,1,0:T(8,128)S(1)}, s16[1,544,128]{2,1,0:T(8,128)(2,1)S(1)}) custom-call(bf16[2048,128]{1,0:T(8,128)(2,1)S(1)} %pad.9.bias_ref, bf16[6,512,128]{2,1,0:T(8,128)(2,1)S(1)} %pad_maximum_fusion.own_q_ref, bf16[4,512,128]{2,1,0:T(8,128)(2,1)} %collective-permute-done.10.far_q_ref, ...), custom_call_target="tpu_custom_call" | custom-call | flops 2147483648 | bytes 1703936 | tf_op jit(solution)/shard_map/pallas_call | solution.py:128
  103.4 2.5 %collective-permute-done.17.code_ref = s16[2,544,128]{2,1,0:T(8,128)(2,1)S(1)} collective-permute-done((s16[2,544,128]{2,1,0:T(8,128)(2,1)S(1)}, s16[2,544,128]{2,1,0:T(8,128)(2,1)S(1)}, u32[]{:S(2)}, u32[]{:S(2)}) %collective-permute-start.17) | collective-permute-done | bytes 278560 | tf_op jit(solution)/shard_map/ppermute | solution.py:218
  106.8 1.3 %collective-permute-done.19 = s16[1,544,128]{2,1,0:T(8,128)(2,1)S(1)} collective-permute-done((s16[1,544,128]{2,1,0:T(8,128)(2,1)S(1)}, s16[1,544,128]{2,1,0:T(8,128)(2,1)S(1)}, u32[]{:S(2)}, u32[]{:S(2)}) %collective-permute-start.19) | collective-permute-done | bytes 139296 | tf_op jit(solution)/shard_map/ppermute | solution.py:218
  108.6 4.8 %collective-permute-done.20 = s16[1,544,128]{2,1,0:T(8,128)(2,1)S(1)} collective-permute-done((s16[1,544,128]{2,1,0:T(8,128)(2,1)S(1)}, s16[1,544,128]{2,1,0:T(8,128)(2,1)S(1)}, u32[]{:S(2)}, u32[]{:S(2)}) %collective-permute-start.20) | collective-permute-done | bytes 139296 | tf_op jit(solution)/shard_map/ppermute | solution.py:218
  114.5 0.9 collective-permute-done.23
  115.5 0.9 pad_maximum_fusion.2
  (109 shorter events, 14.3 us)
Async XLA Ops:
  3.1 6.8 %collective-permute-start = (bf16[13,5,256]{2,1,0:T(8,128)(2,1)S(1)}, bf16[13,5,256]{2,1,0:T(8,128)(2,1)S(1)}, u32[]{:S(2)}, u32[]{:S(2)}) collective-permute-start(bf16[13,5,256]{2,1,0:T(8,128)(2,1)S(1)} %pad_maximum_fusion.5), channel_id=1, source_target_pairs={{0,16},{2,18},{4,20},{6,22},{8,24},{10,26},{12,28},{14,30},{16,0},... | collective-permute-start | bytes 99848 | tf_op jit(solution)/shard_map/ppermute | solution.py:218
  7.4 6.4 %collective-permute-start.2 = (bf16[2,6,256,128]{3,2,1,0:T(8,128)(2,1)S(1)}, bf16[2,6,256,128]{3,2,1,0:T(8,128)(2,1)S(1)}, u32[]{:S(2)}, u32[]{:S(2)}) collective-permute-start(bf16[2,6,256,128]{3,2,1,0:T(8,128)(2,1)S(1)} %pad_maximum_fusion.1), channel_id=1, source_target_pairs={{0,2},{2,0},{4,6},{6,4},{8,10},{10,8},{12,14},{14,12},{16,18},{18,... | collective-permute-start | bytes 2359304 | tf_op jit(solution)/shard_map/ppermute | solution.py:218
  10.0 1.3 %collective-permute-start.1 = (bf16[7,10,256]{2,1,0:T(8,128)(2,1)S(1)}, bf16[7,10,256]{2,1,0:T(8,128)(2,1)S(1)}, u32[]{:S(2)}, u32[]{:S(2)}) collective-permute-start(bf16[7,10,256]{2,1,0:T(8,128)(2,1)S(1)} %pad_maximum_fusion.4), channel_id=1, source_target_pairs={{0,2},{2,0},{4,6},{6,4},{8,10},{10,8},{12,14},{14,12},{16,18},{18,... | collective-permute-start | bytes 107528 | tf_op jit(solution)/shard_map/ppermute | solution.py:218
  11.4 20.5 %collective-permute-start.15 = (bf16[6,16,256]{2,1,0:T(8,128)(2,1)S(1)}, bf16[6,16,256]{2,1,0:T(8,128)(2,1)S(1)}, u32[]{:S(2)}, u32[]{:S(2)}) collective-permute-start(bf16[6,16,256]{2,1,0:T(8,128)(2,1)S(1)} %pad_maximum_fusion.6), channel_id=1, source_target_pairs={{0,4},{2,6},{4,0},{6,2},{8,12},{10,14},{12,8},{14,10},{16,20},{18,... | collective-permute-start | bytes 147464 | tf_op jit(solution)/shard_map/ppermute | solution.py:218
  14.8 13.8 %copy-start.2 = (bf16[2,2,512,128]{3,2,1,0:T(8,128)(2,1)}, bf16[2,2,512,128]{3,2,1,0:T(8,128)(2,1)S(1)}, u32[]{:S(2)}) copy-start(bf16[2,2,512,128]{3,2,1,0:T(8,128)(2,1)S(1)} %get-tuple-element.69.refs_0_) | copy-start | bytes 1572868
  14.8 14.9 %copy-start.4 = (bf16[2,2,512,128]{3,2,1,0:T(8,128)(2,1)}, bf16[2,2,512,128]{3,2,1,0:T(8,128)(2,1)S(1)}, u32[]{:S(2)}) copy-start(bf16[2,2,512,128]{3,2,1,0:T(8,128)(2,1)S(1)} %get-tuple-element.76) | copy-start | bytes 1572868
  14.8 13.8 %collective-permute-start.4 = (bf16[2,2,512,128]{3,2,1,0:T(8,128)(2,1)S(1)}, bf16[2,2,512,128]{3,2,1,0:T(8,128)(2,1)}, u32[]{:S(2)}, u32[]{:S(2)}) collective-permute-start(bf16[2,2,512,128]{3,2,1,0:T(8,128)(2,1)S(1)} %get-tuple-element.62), channel_id=1, source_target_pairs={{0,8},{2,10},{4,12},{6,14},{8,0},{10,2},{12,4},{14,6},{16,24},{18,... | collective-permute-start | bytes 1572872 | tf_op jit(solution)/shard_map/ppermute | solution.py:218
  16.0 20.1 %copy-start.7 = (bf16[6,256,128]{2,1,0:T(8,128)(2,1)}, bf16[6,256,128]{2,1,0:T(8,128)(2,1)S(1)}, u32[]{:S(2)}) copy-start(bf16[6,256,128]{2,1,0:T(8,128)(2,1)S(1)} %get-tuple-element.111) | copy-start | bytes 1179652
  16.0 16.6 %collective-permute-start.3 = (bf16[6,256,128]{2,1,0:T(8,128)(2,1)S(1)}, bf16[6,256,128]{2,1,0:T(8,128)(2,1)S(1)}, u32[]{:S(2)}, u32[]{:S(2)}) collective-permute-start(bf16[6,256,128]{2,1,0:T(8,128)(2,1)S(1)} %get-tuple-element.112), channel_id=1, source_target_pairs={{0,2},{2,0},{4,6},{6,4},{8,10},{10,8},{12,14},{14,12},{16,18},{18,... | collective-permute-start | bytes 1179656 | tf_op jit(solution)/shard_map/ppermute | solution.py:218
  16.1 38.9 %collective-permute-start.6 = (bf16[2,4,512,128]{3,2,1,0:T(8,128)(2,1)S(1)}, bf16[2,4,512,128]{3,2,1,0:T(8,128)(2,1)}, u32[]{:S(2)}, u32[]{:S(2)}) collective-permute-start(bf16[2,4,512,128]{3,2,1,0:T(8,128)(2,1)S(1)} %get-tuple-element.64.refs_0_), channel_id=1, source_target_pairs={{0,4},{2,6},{4,0},{6,2},{8,12},{10,14},{12,8},{14,10},{16,20},{18,... | collective-permute-start | bytes 3145736 | tf_op jit(solution)/shard_map/ppermute | solution.py:218
  28.6 22.7 %collective-permute-start.11 = (bf16[2,2,512,128]{3,2,1,0:T(8,128)(2,1)}, bf16[2,2,512,128]{3,2,1,0:T(8,128)(2,1)S(1)}, u32[]{:S(2)}, u32[]{:S(2)}) collective-permute-start(bf16[2,2,512,128]{3,2,1,0:T(8,128)(2,1)} %get-tuple-element.75), channel_id=1, source_target_pairs={{0,8},{2,10},{4,12},{6,14},{8,0},{10,2},{12,4},{14,6},{16,24},{18,... | collective-permute-start | bytes 1572872 | tf_op jit(solution)/shard_map/ppermute | solution.py:218
  32.0 25.1 %collective-permute-start.7 = (bf16[2,2,512,128]{3,2,1,0:T(8,128)(2,1)}, bf16[2,2,512,128]{3,2,1,0:T(8,128)(2,1)}, u32[]{:S(2)}, u32[]{:S(2)}) collective-permute-start(bf16[2,2,512,128]{3,2,1,0:T(8,128)(2,1)} %collective-permute-done.4.refs_2_), channel_id=1, source_target_pairs={{0,4},{2,6},{4,0},{6,2},{8,12},{10,14},{12,8},{14,10},{16,20},{18,... | collective-permute-start | bytes 1572872 | tf_op jit(solution)/shard_map/ppermute | solution.py:218
  35.3 14.1 %collective-permute-start.16 = (bf16[6,32,256]{2,1,0:T(8,128)(2,1)S(1)}, bf16[6,32,256]{2,1,0:T(8,128)(2,1)S(1)}, u32[]{:S(2)}, u32[]{:S(2)}) collective-permute-start(bf16[6,32,256]{2,1,0:T(8,128)(2,1)S(1)} %concatenate.60), channel_id=1, source_target_pairs={{0,8},{2,10},{4,12},{6,14},{8,0},{10,2},{12,4},{14,6},{16,24},{18,... | collective-permute-start | bytes 294920 | tf_op jit(solution)/shard_map/ppermute | solution.py:218
  36.8 18.3 %collective-permute-start.5 = (bf16[2,512,128]{2,1,0:T(8,128)(2,1)}, bf16[2,512,128]{2,1,0:T(8,128)(2,1)S(1)}, u32[]{:S(2)}, u32[]{:S(2)}) collective-permute-start(bf16[2,512,128]{2,1,0:T(8,128)(2,1)} %fusion.1), channel_id=1, source_target_pairs={{0,16},{2,18},{4,20},{6,22},{8,24},{10,26},{12,28},{14,30},{16,0},... | collective-permute-start | bytes 786440 | tf_op jit(solution)/shard_map/ppermute | solution.py:218
  50.0 26.8 %collective-permute-start.10 = (bf16[4,512,128]{2,1,0:T(8,128)(2,1)}, bf16[4,512,128]{2,1,0:T(8,128)(2,1)}, u32[]{:S(2)}, u32[]{:S(2)}) collective-permute-start(bf16[4,512,128]{2,1,0:T(8,128)(2,1)} %fusion), channel_id=1, source_target_pairs={{0,16},{2,18},{4,20},{6,22},{8,24},{10,26},{12,28},{14,30},{16,0},... | collective-permute-start | bytes 1572872 | tf_op jit(solution)/shard_map/ppermute | solution.py:218
  51.3 13.5 %copy-start.11 = (bf16[6,64,256]{2,1,0:T(8,128)(2,1)}, bf16[6,64,256]{2,1,0:T(8,128)(2,1)S(1)}, u32[]{:S(2)}) copy-start(bf16[6,64,256]{2,1,0:T(8,128)(2,1)S(1)} %concatenate.61) | copy-start | bytes 589828
  52.2 23.3 %collective-permute-start.12 = (bf16[2,2,512,128]{3,2,1,0:T(8,128)(2,1)}, bf16[2,2,512,128]{3,2,1,0:T(8,128)(2,1)S(1)}, u32[]{:S(2)}, u32[]{:S(2)}) collective-permute-start(bf16[2,2,512,128]{3,2,1,0:T(8,128)(2,1)} %copy-done.4), channel_id=1, source_target_pairs={{0,8},{2,10},{4,12},{6,14},{8,0},{10,2},{12,4},{14,6},{16,24},{18,... | collective-permute-start | bytes 1572872 | tf_op jit(solution)/shard_map/ppermute | solution.py:218
  55.0 20.6 %collective-permute-start.9 = (bf16[2,2,512,128]{3,2,1,0:T(8,128)(2,1)}, bf16[2,2,512,128]{3,2,1,0:T(8,128)(2,1)S(1)}, u32[]{:S(2)}, u32[]{:S(2)}) collective-permute-start(bf16[2,2,512,128]{3,2,1,0:T(8,128)(2,1)} %copy-done.2), channel_id=1, source_target_pairs={{0,4},{2,6},{4,0},{6,2},{8,12},{10,14},{12,8},{14,10},{16,20},{18,... | collective-permute-start | bytes 1572872 | tf_op jit(solution)/shard_map/ppermute | solution.py:218
  55.1 25.7 %collective-permute-start.13 = (bf16[2,2,512,128]{3,2,1,0:T(8,128)(2,1)}, bf16[2,2,512,128]{3,2,1,0:T(8,128)(2,1)S(1)}, u32[]{:S(2)}, u32[]{:S(2)}) collective-permute-start(bf16[2,2,512,128]{3,2,1,0:T(8,128)(2,1)} %copy-done.5), channel_id=1, source_target_pairs={{0,4},{2,6},{4,0},{6,2},{8,12},{10,14},{12,8},{14,10},{16,20},{18,... | collective-permute-start | bytes 1572872 | tf_op jit(solution)/shard_map/ppermute | solution.py:218
  64.9 15.9 %copy-start.6 = (bf16[2,2,512,128]{3,2,1,0:T(8,128)(2,1)S(1)}, bf16[2,2,512,128]{3,2,1,0:T(8,128)(2,1)}, u32[]{:S(2)}) copy-start(bf16[2,2,512,128]{3,2,1,0:T(8,128)(2,1)} %copy-done.5) | copy-start | bytes 1572868
  64.9 24.1 %collective-permute-start.8 = (s16[2,544,128]{2,1,0:T(8,128)(2,1)S(1)}, s16[2,544,128]{2,1,0:T(8,128)(2,1)S(1)}, u32[]{:S(2)}, u32[]{:S(2)}) collective-permute-start(s16[2,544,128]{2,1,0:T(8,128)(2,1)S(1)} %get-tuple-element.67), channel_id=1, source_target_pairs={{0,16},{2,18},{4,20},{6,22},{8,24},{10,26},{12,28},{14,30},{16,0},... | collective-permute-start | bytes 835592 | tf_op jit(solution)/shard_map/ppermute | solution.py:218
  75.5 13.3 %copy-start.12 = (bf16[6,64,256]{2,1,0:T(8,128)(2,1)S(1)}, bf16[6,64,256]{2,1,0:T(8,128)(2,1)}, u32[]{:S(2)}) copy-start(bf16[6,64,256]{2,1,0:T(8,128)(2,1)} %copy-done.11) | copy-start | bytes 589828
  75.5 14.2 %copy-start.3 = (bf16[2,2,512,128]{3,2,1,0:T(8,128)(2,1)S(1)}, bf16[2,2,512,128]{3,2,1,0:T(8,128)(2,1)}, u32[]{:S(2)}) copy-start(bf16[2,2,512,128]{3,2,1,0:T(8,128)(2,1)} %copy-done.2) | copy-start | bytes 1572868
  75.5 14.2 %collective-permute-start.18 = (bf16[2,1,512,128]{3,2,1,0:T(8,128)(2,1)S(1)}, bf16[2,1,512,128]{3,2,1,0:T(8,128)(2,1)S(1)}, u32[]{:S(2)}, u32[]{:S(2)}) collective-permute-start(bf16[2,1,512,128]{3,2,1,0:T(8,128)(2,1)S(1)} %get-tuple-element.88), channel_id=1, source_target_pairs={{0,4},{2,6},{4,0},{6,2},{8,12},{10,14},{12,8},{14,10},{16,20},{18,... | collective-permute-start | bytes 786440 | tf_op jit(solution)/shard_map/ppermute | solution.py:218
  88.5 8.3 %collective-permute-start.14 = (bf16[2,1,512,128]{3,2,1,0:T(8,128)(2,1)S(1)}, bf16[2,1,512,128]{3,2,1,0:T(8,128)(2,1)S(1)}, u32[]{:S(2)}, u32[]{:S(2)}) collective-permute-start(bf16[2,1,512,128]{3,2,1,0:T(8,128)(2,1)S(1)} %get-tuple-element.78), channel_id=1, source_target_pairs={{0,4},{2,6},{4,0},{6,2},{8,12},{10,14},{12,8},{14,10},{16,20},{18,... | collective-permute-start | bytes 786440 | tf_op jit(solution)/shard_map/ppermute | solution.py:218
  88.9 16.9 %collective-permute-start.17 = (s16[2,544,128]{2,1,0:T(8,128)(2,1)S(1)}, s16[2,544,128]{2,1,0:T(8,128)(2,1)S(1)}, u32[]{:S(2)}, u32[]{:S(2)}) collective-permute-start(s16[2,544,128]{2,1,0:T(8,128)(2,1)S(1)} %get-tuple-element.85), channel_id=1, source_target_pairs={{0,16},{2,18},{4,20},{6,22},{8,24},{10,26},{12,28},{14,30},{16,0},... | collective-permute-start | bytes 835592 | tf_op jit(solution)/shard_map/ppermute | solution.py:218
  94.5 13.6 %collective-permute-start.19 = (s16[1,544,128]{2,1,0:T(8,128)(2,1)S(1)}, s16[1,544,128]{2,1,0:T(8,128)(2,1)S(1)}, u32[]{:S(2)}, u32[]{:S(2)}) collective-permute-start(s16[1,544,128]{2,1,0:T(8,128)(2,1)S(1)} %get-tuple-element.91), channel_id=1, source_target_pairs={{0,16},{2,18},{4,20},{6,22},{8,24},{10,26},{12,28},{14,30},{16,0},... | collective-permute-start | bytes 417800 | tf_op jit(solution)/shard_map/ppermute | solution.py:218
  102.6 4.2 %collective-permute-start.21 = (bf16[2,256,128]{2,1,0:T(8,128)(2,1)S(1)}, bf16[2,256,128]{2,1,0:T(8,128)(2,1)S(1)}, u32[]{:S(2)}, u32[]{:S(2)}) collective-permute-start(bf16[2,256,128]{2,1,0:T(8,128)(2,1)S(1)} %get-tuple-element.97), channel_id=1, source_target_pairs={{0,2},{2,0},{4,6},{6,4},{8,10},{10,8},{12,14},{14,12},{16,18},{18,... | collective-permute-start | bytes 393224 | tf_op jit(solution)/shard_map/ppermute | solution.py:218
  102.6 10.7 %collective-permute-start.20 = (s16[1,544,128]{2,1,0:T(8,128)(2,1)S(1)}, s16[1,544,128]{2,1,0:T(8,128)(2,1)S(1)}, u32[]{:S(2)}, u32[]{:S(2)}) collective-permute-start(s16[1,544,128]{2,1,0:T(8,128)(2,1)S(1)} %get-tuple-element.95), channel_id=1, source_target_pairs={{0,16},{2,18},{4,20},{6,22},{8,24},{10,26},{12,28},{14,30},{16,0},... | collective-permute-start | bytes 417800 | tf_op jit(solution)/shard_map/ppermute | solution.py:218
  106.7 7.8 %collective-permute-start.22 = (bf16[2,256,128]{2,1,0:T(8,128)(2,1)S(1)}, bf16[2,256,128]{2,1,0:T(8,128)(2,1)S(1)}, u32[]{:S(2)}, u32[]{:S(2)}) collective-permute-start(bf16[2,256,128]{2,1,0:T(8,128)(2,1)S(1)} %get-tuple-element.98), channel_id=1, source_target_pairs={{0,2},{2,0},{4,6},{6,4},{8,10},{10,8},{12,14},{14,12},{16,18},{18,... | collective-permute-start | bytes 393224 | tf_op jit(solution)/shard_map/ppermute | solution.py:218
  113.9 1.5 %collective-permute-start.24 = (bf16[1,256,128]{2,1,0:T(8,128)(2,1)S(1)}, bf16[1,256,128]{2,1,0:T(8,128)(2,1)S(1)}, u32[]{:S(2)}, u32[]{:S(2)}) collective-permute-start(bf16[1,256,128]{2,1,0:T(8,128)(2,1)S(1)} %get-tuple-element.108), channel_id=1, source_target_pairs={{0,2},{2,0},{4,6},{6,4},{8,10},{10,8},{12,14},{14,12},{16,18},{18,... | collective-permute-start | bytes 196616 | tf_op jit(solution)/shard_map/ppermute | solution.py:218
  114.0 1.4 %collective-permute-start.23 = (bf16[1,256,128]{2,1,0:T(8,128)(2,1)S(1)}, bf16[1,256,128]{2,1,0:T(8,128)(2,1)S(1)}, u32[]{:S(2)}, u32[]{:S(2)}) collective-permute-start(bf16[1,256,128]{2,1,0:T(8,128)(2,1)S(1)} %get-tuple-element.104), channel_id=1, source_target_pairs={{0,2},{2,0},{4,6},{6,4},{8,10},{10,8},{12,14},{14,12},{16,18},{18,... | collective-permute-start | bytes 196616 | tf_op jit(solution)/shard_map/ppermute | solution.py:218
  (7 other events, 16.4 us)

commit v4 on v3

--- a/solution.py
+++ b/solution.py
@@ -132,8 +132,8 @@
         + [block_from(start) for start, _ in blocks],
         out_specs=[whole(out) for out in outs],
         out_shape=outs,
-        scratch_shapes=[pltpu.VMEM((rows, len(blocks) * span), jnp.float32)] * 4,
-        compiler_params=pltpu.CompilerParams(vmem_limit_bytes=(38 if len(blocks) < 8 else 60) * 1024 * 1024),
+        scratch_shapes=[pltpu.VMEM((rows, len(blocks) * span), jnp.float32)] * 2,
+        compiler_params=pltpu.CompilerParams(vmem_limit_bytes=(28 if len(blocks) < 8 else 60) * 1024 * 1024),
         cost_estimate=pl.CostEstimate(
             flops=work * width * 8,
             bytes_accessed=heads * rows * width * 2 * (2 * len(blocks) + 5),
@@ -342,7 +342,7 @@
     for part in parts:
         own_acc, own_stat, code = done[part]
         if part != parts[-1]:
-            code = after(code, done[parts[-1]][0])
+            code = after(code, done[min(part + 2, parts[-1])][0])
         outs = merge(starts[part], tokens, own_acc, own_stat, code, gate, coarse_cube)
         kept.append(outs[0])
         if split:

time: 117 us -> 117 us (level)
  waiting for transfers between devices: 49.2 us -> 42.6 us
  local copies, waits for them, and re-layouts: 6.49 us -> 9.95 us
  starting transfers between devices: 22.8 us -> 26.2 us
    ppermute x25, waiting for transfers between devices: 49.2 us -> 42.6 us  [swap(): return lax.ppermute(array, 'ctx', [(i, i ^ bit) for i in range(ring)])]
    ppermute x25, starting transfers between devices: 22.8 us -> 26.2 us  [swap(): return lax.ppermute(array, 'ctx', [(i, i ^ bit) for i in range(ring)])]
    concatenate x2, local copies, waits for them, and re-layouts: 1.02 us -> 2.85 us  [body(): pooled = jnp.concatenate([pooled, other], axis=1)]
    unnamed x33 -> x37, local copies, waits for them, and re-layouts: 2.36 us -> 3.98 us
  transfers between devices with their start and end apart: 25 -> 25, of which waited for: 11 -> 9; matrix products, arithmetic and copies ran while one was open for 8% -> 10% of each run, Pallas kernels for 24% -> 24%
where the time goes in v4:
time: 117 us
  waiting for transfers between devices  42.6 us (36%)
  Pallas kernels  27.8 us (24%)
  starting transfers between devices  26.2 us (22%)
  local copies, waits for them, and re-layouts  9.95 us (9%)
  other arithmetic  9.04 us (8%)
    ppermute x25, waiting for transfers between devices, swap(): return lax.ppermute(array, 'ctx', [(i, i ^ bit) for i in range(ring)])  42.6 us
    ppermute x25, starting transfers between devices, swap(): return lax.ppermute(array, 'ctx', [(i, i ^ bit) for i in range(ring)])  26.2 us
    pallas_call x4, Pallas kernels, attend(): pl.pallas_call(functools.partial(attend_kernel, len(blocks), factor), gri...  25.2 us
    unnamed x37, local copies, waits for them, and re-layouts  3.98 us
    concatenate x2, local copies, waits for them, and re-layouts, body(): pooled = jnp.concatenate([pooled, other], axis=1)  2.85 us
    reduce_sum x3, other arithmetic, pool_cubes(): jnp.sum(field.reshape(heads, tokens // CUBE, CUBE, width), axis=2, dtype=...  2.69 us
    concatenate x3, other arithmetic, body(): jnp.concatenate([cut(queries, mine), swap(cut(queries, theirs), 1)], axis=1)  2.67 us
  transfers between devices with their start and end apart: 25, of which 9 were waited for; matrix products, arithmetic and copies ran while one was open for 10% of the time, Pallas kernels for 24%

profile of v4, /device:TPU:0, one launch (start us, length us, event | category | flops | bytes accessed | tf_op | source)
XLA Modules:
  0.0 116.6 jit_solution(8724976992219870515)
XLA Ops:
  1.5 1.3 %convert_reduce_fusion.2 = f32[12,4,128]{2,1,0:T(4,128)S(1)} fusion(bf16[12,256,128]{2,1,0:T(8,128)(2,1)} %keys_ref.1), kind=kLoop, calls=%fused_computation.3 | loop fusion | flops 780288 | bytes 811008 | tf_op jit(solution)/shard_map/reduce_sum | solution.py:19
  3.1 4.1 %collective-permute-start = (bf16[13,5,256]{2,1,0:T(8,128)(2,1)S(1)}, bf16[13,5,256]{2,1,0:T(8,128)(2,1)S(1)}, u32[]{:S(2)}, u32[]{:S(2)}) collective-permute-start(bf16[13,5,256]{2,1,0:T(8,128)(2,1)S(1)} %pad_maximum_fusion.5), channel_id=1, source_target_pairs={{0,16},{2,18},{4,20},{6,22},{8,24},{10,26},{12,28},{14,30},{16,0},... | collective-permute-start | bytes 99848 | tf_op jit(solution)/shard_map/ppermute | solution.py:218
  7.6 2.3 %collective-permute-done = bf16[13,5,256]{2,1,0:T(8,128)(2,1)S(1)} collective-permute-done((bf16[13,5,256]{2,1,0:T(8,128)(2,1)S(1)}, bf16[13,5,256]{2,1,0:T(8,128)(2,1)S(1)}, u32[]{:S(2)}, u32[]{:S(2)}) %collective-permute-start) | collective-permute-done | bytes 33312 | tf_op jit(solution)/shard_map/ppermute | solution.py:218
  10.2 1.2 collective-permute-done.1
  11.4 1.8 %collective-permute-start.14 = (bf16[6,16,256]{2,1,0:T(8,128)(2,1)S(1)}, bf16[6,16,256]{2,1,0:T(8,128)(2,1)S(1)}, u32[]{:S(2)}, u32[]{:S(2)}) collective-permute-start(bf16[6,16,256]{2,1,0:T(8,128)(2,1)S(1)} %pad_maximum_fusion.6), channel_id=1, source_target_pairs={{0,4},{2,6},{4,0},{6,2},{8,12},{10,14},{12,8},{14,10},{16,20},{18,... | collective-permute-start | bytes 147464 | tf_op jit(solution)/shard_map/ppermute | solution.py:218
  13.8 1.0 shard_map.55
  14.8 1.1 collective-permute-start.4
  16.6 12.0 %collective-permute-done.4.refs_2_ = bf16[2,2,512,128]{3,2,1,0:T(8,128)(2,1)} collective-permute-done((bf16[2,2,512,128]{3,2,1,0:T(8,128)(2,1)S(1)}, bf16[2,2,512,128]{3,2,1,0:T(8,128)(2,1)}, u32[]{:S(2)}, u32[]{:S(2)}) %collective-permute-start.4) | collective-permute-done | bytes 524320 | tf_op jit(solution)/shard_map/ppermute | solution.py:218
  28.6 1.1 collective-permute-start.11
  29.7 1.0 copy.12
  30.7 1.1 pad.9.bias_ref
  31.9 1.9 %concatenate.60 = bf16[6,32,256]{2,1,0:T(8,128)(2,1)} concatenate(bf16[6,4,256]{2,1,0:T(4,128)(2,1)S(1)} %get-tuple-element.116, bf16[6,4,256]{2,1,0:T(4,128)(2,1)S(1)} %get-tuple-element.118, bf16[6,4,256]{2,1,0:T(4,128)(2,1)S(1)} %get-tuple-element.115, bf16[6,4,256]{2,1,0:T(4,128)(2,1)S(1)} %get-tuple-element.117, bf16[6,16,256]{2,1,0:T(8,128)(2,1)S(1)} %collective-permute-done.14), dimensions={1} | concatenate | bytes 196608 | tf_op jit(solution)/shard_map/concatenate | solution.py:302
  35.0 0.8 fusion
  35.9 1.1 pad_maximum_fusion.own_q_ref
  38.5 2.6 %collective-permute-start.5 = (bf16[2,512,128]{2,1,0:T(8,128)(2,1)}, bf16[2,512,128]{2,1,0:T(8,128)(2,1)S(1)}, u32[]{:S(2)}, u32[]{:S(2)}) collective-permute-start(bf16[2,512,128]{2,1,0:T(8,128)(2,1)} %fusion.1), channel_id=1, source_target_pairs={{0,16},{2,18},{4,20},{6,22},{8,24},{10,26},{12,28},{14,30},{16,0},... | collective-permute-start | bytes 786440 | tf_op jit(solution)/shard_map/ppermute | solution.py:218
  41.1 1.2 %convert_reduce_fusion = f32[6,8,128]{2,1,0:T(8,128)S(1)} fusion(bf16[6,256,128]{2,1,0:T(8,128)(2,1)S(1)} %copy-done.11, bf16[6,256,128]{2,1,0:T(8,128)(2,1)} %copy-done.9), kind=kLoop, calls=%fused_computation.1 | loop fusion | flops 2353152 | bytes 811008 | tf_op jit(solution)/shard_map/reduce_sum | solution.py:19
  42.3 6.7 %collective-permute-done.15 = bf16[6,32,256]{2,1,0:T(8,128)(2,1)S(1)} collective-permute-done((bf16[6,32,256]{2,1,0:T(8,128)(2,1)}, bf16[6,32,256]{2,1,0:T(8,128)(2,1)S(1)}, u32[]{:S(2)}, u32[]{:S(2)}) %collective-permute-start.15) | collective-permute-done | bytes 98336 | tf_op jit(solution)/shard_map/ppermute | solution.py:218
  49.7 1.0 concatenate.61
  51.5 1.5 %collective-permute-start.12 = (bf16[2,2,512,128]{3,2,1,0:T(8,128)(2,1)}, bf16[2,2,512,128]{3,2,1,0:T(8,128)(2,1)S(1)}, u32[]{:S(2)}, u32[]{:S(2)}) collective-permute-start(bf16[2,2,512,128]{3,2,1,0:T(8,128)(2,1)} %copy-done.4), channel_id=1, source_target_pairs={{0,8},{2,10},{4,12},{6,14},{8,0},{10,2},{12,4},{14,6},{16,24},{18,... | collective-permute-start | bytes 1572872 | tf_op jit(solution)/shard_map/ppermute | solution.py:218
  53.3 8.7 %collective-permute-done.5.far_q_ref = bf16[2,512,128]{2,1,0:T(8,128)(2,1)S(1)} collective-permute-done((bf16[2,512,128]{2,1,0:T(8,128)(2,1)}, bf16[2,512,128]{2,1,0:T(8,128)(2,1)S(1)}, u32[]{:S(2)}, u32[]{:S(2)}) %collective-permute-start.5) | collective-permute-done | bytes 262176 | tf_op jit(solution)/shard_map/ppermute | solution.py:218
  62.8 4.5 %collective-permute-start.16 = (bf16[2,2,512,128]{3,2,1,0:T(8,128)(2,1)}, bf16[2,2,512,128]{3,2,1,0:T(8,128)(2,1)S(1)}, u32[]{:S(2)}, u32[]{:S(2)}) collective-permute-start(bf16[2,2,512,128]{3,2,1,0:T(8,128)(2,1)} %copy-done.5), channel_id=1, source_target_pairs={{0,4},{2,6},{4,0},{6,2},{8,12},{10,14},{12,8},{14,10},{16,20},{18,... | collective-permute-start | bytes 1572872 | tf_op jit(solution)/shard_map/ppermute | solution.py:218
  67.3 0.9 copy-done.8
  68.2 7.8 %shard_map.56 = (f32[2,512,128]{2,1,0:T(8,128)S(1)}, f32[2,8,512]{2,1,0:T(8,128)S(1)}, s16[2,544,128]{2,1,0:T(8,128)(2,1)S(1)}) custom-call(bf16[2048,128]{1,0:T(8,128)(2,1)S(1)} %pad.9.bias_ref, bf16[6,512,128]{2,1,0:T(8,128)(2,1)S(1)} %pad_maximum_fusion.own_q_ref, bf16[2,512,128]{2,1,0:T(8,128)(2,1)S(1)} %copy-done.8, ...), custom_call_target="tpu_custom_call" | custom-call | flops 4294967296 | bytes 3407872 | tf_op jit(solution)/shard_map/pallas_call | solution.py:128
  76.2 1.9 %collective-permute-done.16.refs_3_ = bf16[2,2,512,128]{3,2,1,0:T(8,128)(2,1)S(1)} collective-permute-done((bf16[2,2,512,128]{3,2,1,0:T(8,128)(2,1)}, bf16[2,2,512,128]{3,2,1,0:T(8,128)(2,1)S(1)}, u32[]{:S(2)}, u32[]{:S(2)}) %collective-permute-start.16) | collective-permute-done | bytes 524320 | tf_op jit(solution)/shard_map/ppermute | solution.py:218
  78.1 7.7 %shard_map.59 = (f32[2,512,128]{2,1,0:T(8,128)S(1)}, f32[2,8,512]{2,1,0:T(8,128)S(1)}, s16[2,544,128]{2,1,0:T(8,128)(2,1)S(1)}) custom-call(bf16[2048,128]{1,0:T(8,128)(2,1)S(1)} %pad.9.bias_ref, bf16[6,512,128]{2,1,0:T(8,128)(2,1)S(1)} %pad_maximum_fusion.own_q_ref, bf16[4,512,128]{2,1,0:T(8,128)(2,1)} %collective-permute-done.10.far_q_ref, ...), custom_call_target="tpu_custom_call" | custom-call | flops 4294967296 | bytes 3407872 | tf_op jit(solution)/shard_map/pallas_call | solution.py:128
  85.8 2.8 %collective-permute-start.18 = (bf16[2,1,512,128]{3,2,1,0:T(8,128)(2,1)S(1)}, bf16[2,1,512,128]{3,2,1,0:T(8,128)(2,1)S(1)}, u32[]{:S(2)}, u32[]{:S(2)}) collective-permute-start(bf16[2,1,512,128]{3,2,1,0:T(8,128)(2,1)S(1)} %get-tuple-element.86), channel_id=1, source_target_pairs={{0,4},{2,6},{4,0},{6,2},{8,12},{10,14},{12,8},{14,10},{16,20},{18,... | collective-permute-start | bytes 786440 | tf_op jit(solution)/shard_map/ppermute | solution.py:218
  89.4 4.8 %shard_map.57 = (f32[1,512,128]{2,1,0:T(8,128)S(1)}, f32[1,8,512]{2,1,0:T(8,128)S(1)}, s16[1,544,128]{2,1,0:T(8,128)(2,1)S(1)}) custom-call(bf16[2048,128]{1,0:T(8,128)(2,1)S(1)} %pad.9.bias_ref, bf16[6,512,128]{2,1,0:T(8,128)(2,1)S(1)} %pad_maximum_fusion.own_q_ref, bf16[4,512,128]{2,1,0:T(8,128)(2,1)} %collective-permute-done.10.far_q_ref, ...), custom_call_target="tpu_custom_call" | custom-call | flops 2147483648 | bytes 1703936 | tf_op jit(solution)/shard_map/pallas_call | solution.py:128
  95.1 2.3 %collective-permute-start.19 = (s16[1,544,128]{2,1,0:T(8,128)(2,1)S(1)}, s16[1,544,128]{2,1,0:T(8,128)(2,1)S(1)}, u32[]{:S(2)}, u32[]{:S(2)}) collective-permute-start(s16[1,544,128]{2,1,0:T(8,128)(2,1)S(1)} %get-tuple-element.91), channel_id=1, source_target_pairs={{0,16},{2,18},{4,20},{6,22},{8,24},{10,26},{12,28},{14,30},{16,0},... | collective-permute-start | bytes 417800 | tf_op jit(solution)/shard_map/ppermute | solution.py:218
  97.4 5.0 %shard_map.60 = (f32[1,512,128]{2,1,0:T(8,128)S(1)}, f32[1,8,512]{2,1,0:T(8,128)S(1)}, s16[1,544,128]{2,1,0:T(8,128)(2,1)S(1)}) custom-call(bf16[2048,128]{1,0:T(8,128)(2,1)S(1)} %pad.9.bias_ref, bf16[6,512,128]{2,1,0:T(8,128)(2,1)S(1)} %pad_maximum_fusion.own_q_ref, bf16[4,512,128]{2,1,0:T(8,128)(2,1)} %collective-permute-done.10.far_q_ref, ...), custom_call_target="tpu_custom_call" | custom-call | flops 2147483648 | bytes 1703936 | tf_op jit(solution)/shard_map/pallas_call | solution.py:128
  104.9 8.6 %collective-permute-done.20 = s16[1,544,128]{2,1,0:T(8,128)(2,1)S(1)} collective-permute-done((s16[1,544,128]{2,1,0:T(8,128)(2,1)S(1)}, s16[1,544,128]{2,1,0:T(8,128)(2,1)S(1)}, u32[]{:S(2)}, u32[]{:S(2)}) %collective-permute-start.20) | collective-permute-done | bytes 139296 | tf_op jit(solution)/shard_map/ppermute | solution.py:218
  114.6 0.9 collective-permute-done.23
  115.6 0.9 pad_maximum_fusion.2
  (113 shorter events, 14.4 us)
Async XLA Ops:
  0.0 7.2 %copy-start.1 = (bf16[12,256,128]{2,1,0:T(8,128)(2,1)S(1)}, bf16[12,256,128]{2,1,0:T(8,128)(2,1)}, u32[]{:S(2)}) copy-start(bf16[12,256,128]{2,1,0:T(8,128)(2,1)} %keys_ref.1) | copy-start | bytes 2359300
  3.1 6.8 %collective-permute-start = (bf16[13,5,256]{2,1,0:T(8,128)(2,1)S(1)}, bf16[13,5,256]{2,1,0:T(8,128)(2,1)S(1)}, u32[]{:S(2)}, u32[]{:S(2)}) collective-permute-start(bf16[13,5,256]{2,1,0:T(8,128)(2,1)S(1)} %pad_maximum_fusion.5), channel_id=1, source_target_pairs={{0,16},{2,18},{4,20},{6,22},{8,24},{10,26},{12,28},{14,30},{16,0},... | collective-permute-start | bytes 99848 | tf_op jit(solution)/shard_map/ppermute | solution.py:218
  7.4 6.4 %collective-permute-start.2 = (bf16[2,6,256,128]{3,2,1,0:T(8,128)(2,1)S(1)}, bf16[2,6,256,128]{3,2,1,0:T(8,128)(2,1)S(1)}, u32[]{:S(2)}, u32[]{:S(2)}) collective-permute-start(bf16[2,6,256,128]{3,2,1,0:T(8,128)(2,1)S(1)} %pad_maximum_fusion.1), channel_id=1, source_target_pairs={{0,2},{2,0},{4,6},{6,4},{8,10},{10,8},{12,14},{14,12},{16,18},{18,... | collective-permute-start | bytes 2359304 | tf_op jit(solution)/shard_map/ppermute | solution.py:218
  10.0 1.3 %collective-permute-start.1 = (bf16[7,10,256]{2,1,0:T(8,128)(2,1)S(1)}, bf16[7,10,256]{2,1,0:T(8,128)(2,1)S(1)}, u32[]{:S(2)}, u32[]{:S(2)}) collective-permute-start(bf16[7,10,256]{2,1,0:T(8,128)(2,1)S(1)} %pad_maximum_fusion.4), channel_id=1, source_target_pairs={{0,2},{2,0},{4,6},{6,4},{8,10},{10,8},{12,14},{14,12},{16,18},{18,... | collective-permute-start | bytes 107528 | tf_op jit(solution)/shard_map/ppermute | solution.py:218
  11.4 20.5 %collective-permute-start.14 = (bf16[6,16,256]{2,1,0:T(8,128)(2,1)S(1)}, bf16[6,16,256]{2,1,0:T(8,128)(2,1)S(1)}, u32[]{:S(2)}, u32[]{:S(2)}) collective-permute-start(bf16[6,16,256]{2,1,0:T(8,128)(2,1)S(1)} %pad_maximum_fusion.6), channel_id=1, source_target_pairs={{0,4},{2,6},{4,0},{6,2},{8,12},{10,14},{12,8},{14,10},{16,20},{18,... | collective-permute-start | bytes 147464 | tf_op jit(solution)/shard_map/ppermute | solution.py:218
  14.8 13.8 %copy-start.2 = (bf16[2,2,512,128]{3,2,1,0:T(8,128)(2,1)}, bf16[2,2,512,128]{3,2,1,0:T(8,128)(2,1)S(1)}, u32[]{:S(2)}) copy-start(bf16[2,2,512,128]{3,2,1,0:T(8,128)(2,1)S(1)} %get-tuple-element.69.refs_0_) | copy-start | bytes 1572868
  14.8 14.9 %copy-start.4 = (bf16[2,2,512,128]{3,2,1,0:T(8,128)(2,1)}, bf16[2,2,512,128]{3,2,1,0:T(8,128)(2,1)S(1)}, u32[]{:S(2)}) copy-start(bf16[2,2,512,128]{3,2,1,0:T(8,128)(2,1)S(1)} %get-tuple-element.76) | copy-start | bytes 1572868
  14.8 13.8 %collective-permute-start.4 = (bf16[2,2,512,128]{3,2,1,0:T(8,128)(2,1)S(1)}, bf16[2,2,512,128]{3,2,1,0:T(8,128)(2,1)}, u32[]{:S(2)}, u32[]{:S(2)}) collective-permute-start(bf16[2,2,512,128]{3,2,1,0:T(8,128)(2,1)S(1)} %get-tuple-element.62), channel_id=1, source_target_pairs={{0,8},{2,10},{4,12},{6,14},{8,0},{10,2},{12,4},{14,6},{16,24},{18,... | collective-permute-start | bytes 1572872 | tf_op jit(solution)/shard_map/ppermute | solution.py:218
  16.0 21.8 %copy-start.9 = (bf16[6,256,128]{2,1,0:T(8,128)(2,1)}, bf16[6,256,128]{2,1,0:T(8,128)(2,1)S(1)}, u32[]{:S(2)}) copy-start(bf16[6,256,128]{2,1,0:T(8,128)(2,1)S(1)} %get-tuple-element.111) | copy-start | bytes 1179652
  16.0 18.3 %collective-permute-start.3 = (bf16[6,256,128]{2,1,0:T(8,128)(2,1)S(1)}, bf16[6,256,128]{2,1,0:T(8,128)(2,1)S(1)}, u32[]{:S(2)}, u32[]{:S(2)}) collective-permute-start(bf16[6,256,128]{2,1,0:T(8,128)(2,1)S(1)} %get-tuple-element.112), channel_id=1, source_target_pairs={{0,2},{2,0},{4,6},{6,4},{8,10},{10,8},{12,14},{14,12},{16,18},{18,... | collective-permute-start | bytes 1179656 | tf_op jit(solution)/shard_map/ppermute | solution.py:218
  16.0 37.2 %collective-permute-start.6 = (bf16[2,4,512,128]{3,2,1,0:T(8,128)(2,1)S(1)}, bf16[2,4,512,128]{3,2,1,0:T(8,128)(2,1)}, u32[]{:S(2)}, u32[]{:S(2)}) collective-permute-start(bf16[2,4,512,128]{3,2,1,0:T(8,128)(2,1)S(1)} %get-tuple-element.64.refs_0_), channel_id=1, source_target_pairs={{0,4},{2,6},{4,0},{6,2},{8,12},{10,14},{12,8},{14,10},{16,20},{18,... | collective-permute-start | bytes 3145736 | tf_op jit(solution)/shard_map/ppermute | solution.py:218
  28.6 22.1 %collective-permute-start.11 = (bf16[2,2,512,128]{3,2,1,0:T(8,128)(2,1)}, bf16[2,2,512,128]{3,2,1,0:T(8,128)(2,1)S(1)}, u32[]{:S(2)}, u32[]{:S(2)}) collective-permute-start(bf16[2,2,512,128]{3,2,1,0:T(8,128)(2,1)} %get-tuple-element.75), channel_id=1, source_target_pairs={{0,8},{2,10},{4,12},{6,14},{8,0},{10,2},{12,4},{14,6},{16,24},{18,... | collective-permute-start | bytes 1572872 | tf_op jit(solution)/shard_map/ppermute | solution.py:218
  33.8 33.5 %collective-permute-start.7 = (bf16[2,2,512,128]{3,2,1,0:T(8,128)(2,1)}, bf16[2,2,512,128]{3,2,1,0:T(8,128)(2,1)}, u32[]{:S(2)}, u32[]{:S(2)}) collective-permute-start(bf16[2,2,512,128]{3,2,1,0:T(8,128)(2,1)} %collective-permute-done.4.refs_2_), channel_id=1, source_target_pairs={{0,4},{2,6},{4,0},{6,2},{8,12},{10,14},{12,8},{14,10},{16,20},{18,... | collective-permute-start | bytes 1572872 | tf_op jit(solution)/shard_map/ppermute | solution.py:218
  37.0 12.1 %collective-permute-start.15 = (bf16[6,32,256]{2,1,0:T(8,128)(2,1)}, bf16[6,32,256]{2,1,0:T(8,128)(2,1)S(1)}, u32[]{:S(2)}, u32[]{:S(2)}) collective-permute-start(bf16[6,32,256]{2,1,0:T(8,128)(2,1)} %concatenate.60), channel_id=1, source_target_pairs={{0,8},{2,10},{4,12},{6,14},{8,0},{10,2},{12,4},{14,6},{16,24},{18,... | collective-permute-start | bytes 294920 | tf_op jit(solution)/shard_map/ppermute | solution.py:218
  38.5 23.6 %collective-permute-start.5 = (bf16[2,512,128]{2,1,0:T(8,128)(2,1)}, bf16[2,512,128]{2,1,0:T(8,128)(2,1)S(1)}, u32[]{:S(2)}, u32[]{:S(2)}) collective-permute-start(bf16[2,512,128]{2,1,0:T(8,128)(2,1)} %fusion.1), channel_id=1, source_target_pairs={{0,16},{2,18},{4,20},{6,22},{8,24},{10,26},{12,28},{14,30},{16,0},... | collective-permute-start | bytes 786440 | tf_op jit(solution)/shard_map/ppermute | solution.py:218
  49.7 26.5 %collective-permute-start.10 = (bf16[4,512,128]{2,1,0:T(8,128)(2,1)}, bf16[4,512,128]{2,1,0:T(8,128)(2,1)}, u32[]{:S(2)}, u32[]{:S(2)}) collective-permute-start(bf16[4,512,128]{2,1,0:T(8,128)(2,1)} %fusion), channel_id=1, source_target_pairs={{0,16},{2,18},{4,20},{6,22},{8,24},{10,26},{12,28},{14,30},{16,0},... | collective-permute-start | bytes 1572872 | tf_op jit(solution)/shard_map/ppermute | solution.py:218
  50.7 16.6 %copy-start.13 = (bf16[6,64,256]{2,1,0:T(8,128)(2,1)}, bf16[6,64,256]{2,1,0:T(8,128)(2,1)S(1)}, u32[]{:S(2)}) copy-start(bf16[6,64,256]{2,1,0:T(8,128)(2,1)S(1)} %concatenate.61) | copy-start | bytes 589828
  51.5 24.6 %collective-permute-start.12 = (bf16[2,2,512,128]{3,2,1,0:T(8,128)(2,1)}, bf16[2,2,512,128]{3,2,1,0:T(8,128)(2,1)S(1)}, u32[]{:S(2)}, u32[]{:S(2)}) collective-permute-start(bf16[2,2,512,128]{3,2,1,0:T(8,128)(2,1)} %copy-done.4), channel_id=1, source_target_pairs={{0,8},{2,10},{4,12},{6,14},{8,0},{10,2},{12,4},{14,6},{16,24},{18,... | collective-permute-start | bytes 1572872 | tf_op jit(solution)/shard_map/ppermute | solution.py:218
  53.3 23.0 %collective-permute-start.9 = (bf16[2,2,512,128]{3,2,1,0:T(8,128)(2,1)}, bf16[2,2,512,128]{3,2,1,0:T(8,128)(2,1)S(1)}, u32[]{:S(2)}, u32[]{:S(2)}) collective-permute-start(bf16[2,2,512,128]{3,2,1,0:T(8,128)(2,1)} %copy-done.2), channel_id=1, source_target_pairs={{0,4},{2,6},{4,0},{6,2},{8,12},{10,14},{12,8},{14,10},{16,20},{18,... | collective-permute-start | bytes 1572872 | tf_op jit(solution)/shard_map/ppermute | solution.py:218
  62.8 15.4 %collective-permute-start.16 = (bf16[2,2,512,128]{3,2,1,0:T(8,128)(2,1)}, bf16[2,2,512,128]{3,2,1,0:T(8,128)(2,1)S(1)}, u32[]{:S(2)}, u32[]{:S(2)}) collective-permute-start(bf16[2,2,512,128]{3,2,1,0:T(8,128)(2,1)} %copy-done.5), channel_id=1, source_target_pairs={{0,4},{2,6},{4,0},{6,2},{8,12},{10,14},{12,8},{14,10},{16,20},{18,... | collective-permute-start | bytes 1572872 | tf_op jit(solution)/shard_map/ppermute | solution.py:218
  76.0 12.7 %collective-permute-start.8 = (s16[2,544,128]{2,1,0:T(8,128)(2,1)S(1)}, s16[2,544,128]{2,1,0:T(8,128)(2,1)S(1)}, u32[]{:S(2)}, u32[]{:S(2)}) collective-permute-start(s16[2,544,128]{2,1,0:T(8,128)(2,1)S(1)} %get-tuple-element.67), channel_id=1, source_target_pairs={{0,16},{2,18},{4,20},{6,22},{8,24},{10,26},{12,28},{14,30},{16,0},... | collective-permute-start | bytes 835592 | tf_op jit(solution)/shard_map/ppermute | solution.py:218
  76.1 12.5 %copy-start.14 = (bf16[6,64,256]{2,1,0:T(8,128)(2,1)S(1)}, bf16[6,64,256]{2,1,0:T(8,128)(2,1)}, u32[]{:S(2)}) copy-start(bf16[6,64,256]{2,1,0:T(8,128)(2,1)} %copy-done.13) | copy-start | bytes 589828
  76.1 13.3 %copy-start.3 = (bf16[2,2,512,128]{3,2,1,0:T(8,128)(2,1)S(1)}, bf16[2,2,512,128]{3,2,1,0:T(8,128)(2,1)}, u32[]{:S(2)}) copy-start(bf16[2,2,512,128]{3,2,1,0:T(8,128)(2,1)} %copy-done.2) | copy-start | bytes 1572868
  76.1 13.3 %collective-permute-start.13 = (bf16[2,1,512,128]{3,2,1,0:T(8,128)(2,1)S(1)}, bf16[2,1,512,128]{3,2,1,0:T(8,128)(2,1)S(1)}, u32[]{:S(2)}, u32[]{:S(2)}) collective-permute-start(bf16[2,1,512,128]{3,2,1,0:T(8,128)(2,1)S(1)} %get-tuple-element.77), channel_id=1, source_target_pairs={{0,4},{2,6},{4,0},{6,2},{8,12},{10,14},{12,8},{14,10},{16,20},{18,... | collective-permute-start | bytes 786440 | tf_op jit(solution)/shard_map/ppermute | solution.py:218
  85.8 11.6 %collective-permute-start.18 = (bf16[2,1,512,128]{3,2,1,0:T(8,128)(2,1)S(1)}, bf16[2,1,512,128]{3,2,1,0:T(8,128)(2,1)S(1)}, u32[]{:S(2)}, u32[]{:S(2)}) collective-permute-start(bf16[2,1,512,128]{3,2,1,0:T(8,128)(2,1)S(1)} %get-tuple-element.86), channel_id=1, source_target_pairs={{0,4},{2,6},{4,0},{6,2},{8,12},{10,14},{12,8},{14,10},{16,20},{18,... | collective-permute-start | bytes 786440 | tf_op jit(solution)/shard_map/ppermute | solution.py:218
  88.7 14.4 %collective-permute-start.17 = (s16[2,544,128]{2,1,0:T(8,128)(2,1)S(1)}, s16[2,544,128]{2,1,0:T(8,128)(2,1)S(1)}, u32[]{:S(2)}, u32[]{:S(2)}) collective-permute-start(s16[2,544,128]{2,1,0:T(8,128)(2,1)S(1)} %get-tuple-element.85), channel_id=1, source_target_pairs={{0,16},{2,18},{4,20},{6,22},{8,24},{10,26},{12,28},{14,30},{16,0},... | collective-permute-start | bytes 835592 | tf_op jit(solution)/shard_map/ppermute | solution.py:218
  95.0 9.0 %collective-permute-start.21 = (bf16[2,256,128]{2,1,0:T(8,128)(2,1)S(1)}, bf16[2,256,128]{2,1,0:T(8,128)(2,1)S(1)}, u32[]{:S(2)}, u32[]{:S(2)}) collective-permute-start(bf16[2,256,128]{2,1,0:T(8,128)(2,1)S(1)} %get-tuple-element.97), channel_id=1, source_target_pairs={{0,2},{2,0},{4,6},{6,4},{8,10},{10,8},{12,14},{14,12},{16,18},{18,... | collective-permute-start | bytes 393224 | tf_op jit(solution)/shard_map/ppermute | solution.py:218
  95.1 9.3 %collective-permute-start.19 = (s16[1,544,128]{2,1,0:T(8,128)(2,1)S(1)}, s16[1,544,128]{2,1,0:T(8,128)(2,1)S(1)}, u32[]{:S(2)}, u32[]{:S(2)}) collective-permute-start(s16[1,544,128]{2,1,0:T(8,128)(2,1)S(1)} %get-tuple-element.91), channel_id=1, source_target_pairs={{0,16},{2,18},{4,20},{6,22},{8,24},{10,26},{12,28},{14,30},{16,0},... | collective-permute-start | bytes 417800 | tf_op jit(solution)/shard_map/ppermute | solution.py:218
  102.5 11.1 %collective-permute-start.20 = (s16[1,544,128]{2,1,0:T(8,128)(2,1)S(1)}, s16[1,544,128]{2,1,0:T(8,128)(2,1)S(1)}, u32[]{:S(2)}, u32[]{:S(2)}) collective-permute-start(s16[1,544,128]{2,1,0:T(8,128)(2,1)S(1)} %get-tuple-element.95), channel_id=1, source_target_pairs={{0,16},{2,18},{4,20},{6,22},{8,24},{10,26},{12,28},{14,30},{16,0},... | collective-permute-start | bytes 417800 | tf_op jit(solution)/shard_map/ppermute | solution.py:218
  104.0 10.7 %collective-permute-start.22 = (bf16[2,256,128]{2,1,0:T(8,128)(2,1)S(1)}, bf16[2,256,128]{2,1,0:T(8,128)(2,1)S(1)}, u32[]{:S(2)}, u32[]{:S(2)}) collective-permute-start(bf16[2,256,128]{2,1,0:T(8,128)(2,1)S(1)} %get-tuple-element.98), channel_id=1, source_target_pairs={{0,2},{2,0},{4,6},{6,4},{8,10},{10,8},{12,14},{14,12},{16,18},{18,... | collective-permute-start | bytes 393224 | tf_op jit(solution)/shard_map/ppermute | solution.py:218
  114.0 1.5 %collective-permute-start.24 = (bf16[1,256,128]{2,1,0:T(8,128)(2,1)S(1)}, bf16[1,256,128]{2,1,0:T(8,128)(2,1)S(1)}, u32[]{:S(2)}, u32[]{:S(2)}) collective-permute-start(bf16[1,256,128]{2,1,0:T(8,128)(2,1)S(1)} %get-tuple-element.104), channel_id=1, source_target_pairs={{0,2},{2,0},{4,6},{6,4},{8,10},{10,8},{12,14},{14,12},{16,18},{18,... | collective-permute-start | bytes 196616 | tf_op jit(solution)/shard_map/ppermute | solution.py:218
  114.1 1.4 %collective-permute-start.23 = (bf16[1,256,128]{2,1,0:T(8,128)(2,1)S(1)}, bf16[1,256,128]{2,1,0:T(8,128)(2,1)S(1)}, u32[]{:S(2)}, u32[]{:S(2)}) collective-permute-start(bf16[1,256,128]{2,1,0:T(8,128)(2,1)S(1)} %get-tuple-element.108), channel_id=1, source_target_pairs={{0,2},{2,0},{4,6},{6,4},{8,10},{10,8},{12,14},{14,12},{16,18},{18,... | collective-permute-start | bytes 196616 | tf_op jit(solution)/shard_map/ppermute | solution.py:218
  (9 other events, 12.9 us)
